TPU v7x, 32 devices: a whole 2x2x4 slice. The times are simulated.
32 devices in a mesh: group: 2 (over x), ha: 16 (over z, y, core).
Axes of the slice: x: 2, y: 2, z: 4, core: 2. Of those that a mesh axis runs over, the one named last changes fastest.
Arguments:
- volume: bfloat16 [64, 64, 16, 128], P(('group', 'ha')), parts along dimension 0, may hold values from -6 to 6
- skip_grad: bfloat16 [64, 64, 16, 128], P(('group', 'ha')), parts along dimension 0, may hold values from -6 to 6
- coarse_grad: bfloat16 [32, 8, 64, 128], P(('group', 'ha')), parts along dimension 0, may hold values from -6 to 6
- w_first: bfloat16 [3, 3, 3, 64, 64], replicated, may hold values from -0.15625 to 0.15625
- w_second: bfloat16 [3, 3, 3, 64, 64], replicated, may hold values from -0.15625 to 0.15625
- w_down: bfloat16 [2, 2, 2, 64, 128], replicated, may hold values from -0.25 to 0.25
- w_coarse: bfloat16 [3, 3, 3, 128, 128], replicated, may hold values from -0.109375 to 0.109375
Outputs:
- input_grad: float32 [64, 64, 16, 128], P(('group', 'ha')), parts along dimension 0
- first_kernel: float32 [6, 3, 3, 64, 64], P('group'), parts along dimension 0
- second_kernel: float32 [6, 3, 3, 64, 64], P('group'), parts along dimension 0
- down_kernel: float32 [4, 2, 2, 64, 128], P('group'), parts along dimension 0
- coarse_kernel: float32 [6, 3, 3, 128, 128], P('group'), parts along dimension 0
There are 2 independent parts, one for each index of `group`. A program takes and returns all parts, laid end to end along the dimension named above; an argument that names none is the same for every part. Nothing has to cross between parts.
All inputs are finite; a program needn't handle non-finite values.
Results may differ from a plain program's by a relative error of at most 0.017.
Values may be sent and summed in bfloat16 or wider, within the bound.
No kernel may reach another device: no remote copies, remote signals or barrier semaphores. Data moves between devices by JAX's collectives and lax.ppermute only.
A program may use at most 128 MiB of HBM per device.

v0:
```python
import functools

import jax
import jax.numpy as jnp
from jax import lax
from jax.experimental import pallas as pl
from jax.experimental.pallas import tpu as pltpu
from jax.sharding import PartitionSpec as P

BF = jnp.bfloat16
F32 = jnp.float32
NT = (((1,), (1,)), ((), ()))
TN = (((0,), (0,)), ((), ()))
AXIS = "ha"


def dot(a, b, dims=(((1,), (0,)), ((), ()))):
    return lax.dot_general(a, b, dims, preferred_element_type=F32)


def call(body, outs, *args, scratch=(), flops=10**9, smem=0):
    in_specs = [pl.BlockSpec(memory_space=pltpu.SMEM)] * smem
    in_specs += [pl.BlockSpec(memory_space=pltpu.VMEM)] * (len(args) - smem)
    size = sum(a.size * a.dtype.itemsize for a in args)
    return pl.pallas_call(
        body,
        out_shape=[jax.ShapeDtypeStruct(s, d) for s, d in outs],
        in_specs=in_specs,
        out_specs=[pl.BlockSpec(memory_space=pltpu.VMEM)] * len(outs),
        scratch_shapes=list(scratch),
        compiler_params=pltpu.CompilerParams(vmem_limit_bytes=48 * 2**20),
        cost_estimate=pl.CostEstimate(flops=flops, bytes_accessed=size, transcendentals=0),
    )(*args)


def neighbours(array):
    size = lax.axis_size(AXIS)
    up = [(i, i + 1) for i in range(size - 1)]
    down = [(j, i) for i, j in up]
    return up, down


def from_before(array):
    return lax.ppermute(array, AXIS, neighbours(array)[0])


def from_after(array):
    return lax.ppermute(array, AXIS, neighbours(array)[1])


def sigmoid(value):
    return 1.0 / (1.0 + jnp.exp(-value))


def fine_pair(rows, w_ref, col):
    num = rows[0].shape[0]
    chan, deep = rows[0].shape[1], rows[0].shape[2]
    none = jnp.zeros((chan, deep), BF)
    sides = []
    for at in (col, col + 1):
        tiles = []
        for row in rows:
            for k in (-1, 0, 1):
                tiles.append(row[at + k] if 0 <= at + k < num else none)
        sides.append(jnp.concatenate(tiles, 0))
    y = dot(w_ref[...], jnp.concatenate(sides, 1))
    lane = lax.broadcasted_iota(jnp.int32, (chan, deep), 1)
    outs = []
    for side in range(2):
        part = y[:, side * deep : (side + 1) * deep]
        left = jnp.where(lane == 0, 0.0, pltpu.roll(part[:chan], 1, 1))
        right = jnp.where(lane == deep - 1, 0.0, pltpu.roll(part[2 * chan :], deep - 1, 1))
        outs.append(part[chan : 2 * chan] + left + right)
    return outs


def fine_grad(sources, deltas, a_scr, b_scr, out_ref):
    num, chan, deep = deltas[0].shape
    lane = lax.broadcasted_iota(jnp.int32, (chan, deep), 1)
    for r in range(2):
        for at in range(num):
            cols = slice((r * num + at) * deep, (r * num + at + 1) * deep)
            for kh in range(3):
                for kw in range(3):
                    tap = kh * 3 + kw
                    src = at + kw - 1
                    tile = sources[r + kh][src] if 0 <= src < num else jnp.zeros((chan, deep), BF)
                    a_scr[tap * chan : (tap + 1) * chan, cols] = tile
            value = deltas[r][at]
            wide = value.astype(F32)
            b_scr[:chan, cols] = jnp.where(
                lane == deep - 1, 0.0, pltpu.roll(wide, deep - 1, 1)
            ).astype(BF)
            b_scr[chan : 2 * chan, cols] = value
            b_scr[2 * chan :, cols] = jnp.where(lane == 0, 0.0, pltpu.roll(wide, 1, 1)).astype(BF)
    acc = dot(a_scr[...], b_scr[...], NT).astype(BF)
    for tap in range(9):
        rows = slice(tap * chan, (tap + 1) * chan)
        out_ref[rows, :] = acc[rows, : 2 * chan]
    for tap in range(0, 10, 2):
        first = acc[tap * chan : (tap + 1) * chan, 2 * chan :]
        if tap + 1 < 9:
            other = acc[(tap + 1) * chan : (tap + 2) * chan, 2 * chan :]
        else:
            other = jnp.zeros_like(first)
        at = (9 + tap // 2) * chan
        out_ref[at : at + chan, :] = jnp.concatenate([first, other], 1)


def fine_grad_scratch(num, chan, deep):
    return (
        pltpu.VMEM((9 * chan, 2 * num * deep), BF),
        pltpu.VMEM((3 * chan, 2 * num * deep), BF),
    )


def coarse_stack(rows, deep):
    size, chan = rows[0].shape
    none = jnp.zeros((deep, chan), BF)
    tiles = []
    for row in rows:
        value = row[...]
        tiles.append(jnp.concatenate([none, value[: size - deep]], 0))
        tiles.append(value)
        tiles.append(jnp.concatenate([value[deep:], none], 0))
    return jnp.concatenate(tiles, 1)


def coarse_conv(rows, w_ref, deep):
    size, chan = rows[0].shape
    y = dot(coarse_stack(rows, deep), w_ref[...])
    at = lax.rem(lax.broadcasted_iota(jnp.int32, (size, chan), 0), deep)
    left = jnp.where(at == 0, 0.0, pltpu.roll(y[:, :chan], 1, 0))
    right = jnp.where(at == deep - 1, 0.0, pltpu.roll(y[:, 2 * chan :], size - 1, 0))
    return y[:, chan : 2 * chan] + left + right


def forward_kernel(
    flags, before, own, after, w_first, w_second, w_down, perm,
    v0, v1, v2, v3, f0, f1, f2, f3, slope1, slope2, act_t, pooled,
    first_scr, rows_scr,
):
    num = f0.shape[0]
    deep = f0.shape[2]
    volumes = [v0, v1, v2, v3]
    firsts = [f0, f1, f2, f3]
    sources = [(before, 0), (before, 1), (own, 0), (own, 1), (after, 0), (after, 1)]
    for i, (ref, r) in enumerate(sources):
        turned = pltpu.einshape("cwd->wcd", ref[r])
        rows_scr[i] = turned
        if 1 <= i <= 4:
            volumes[i - 1][...] = turned
    for r in range(4):
        rows = [rows_scr.at[r + k] for k in range(3)]
        for col in range(0, num, 2):
            for side, pre in enumerate(fine_pair(rows, w_first, col)):
                sigma = sigmoid(pre)
                act = pre * sigma
                if r == 0:
                    act = jnp.where(flags[0] > 0, act, 0.0)
                if r == 3:
                    act = jnp.where(flags[1] > 0, act, 0.0)
                firsts[r][col + side] = act.astype(BF)
                if 1 <= r <= 2:
                    slope1[r - 1, col + side] = sigma * (1.0 + pre * (1.0 - sigma))
    half = deep // 2
    for r in range(2):
        rows = firsts[r : r + 3]
        for col in range(0, num, 2):
            acts = []
            for side, pre in enumerate(fine_pair(rows, w_second, col)):
                sigma = sigmoid(pre)
                acts.append((pre * sigma).astype(BF))
                slope2[r, col + side] = sigma * (1.0 + pre * (1.0 - sigma))
            both = jnp.concatenate(acts, 0)
            wide = both.shape[0]
            turned = dot(perm[...], both, NT).astype(BF)
            at = slice(col // 2 * half, (col // 2 + 1) * half)
            for c in range(2):
                lanes = slice((2 * r + c) * wide, (2 * r + c + 1) * wide)
                act_t[at, lanes] = turned[c * half : (c + 1) * half]
    pooled[...] = dot(act_t[...], w_down[...]).astype(BF)


def coarse_kernel_body(deep, before, own, after, grad, w, delta):
    pre = coarse_conv([before, own, after], w, deep)
    sigma = sigmoid(pre)
    slope = sigma * (1.0 + pre * (1.0 - sigma))
    delta[...] = (grad[...].astype(F32) * slope).astype(BF)


def coarse_grad_body(deep, before, own, after, delta, out):
    size, chan = own.shape
    wide = delta[...].astype(F32)
    at = lax.rem(lax.broadcasted_iota(jnp.int32, (size, chan), 0), deep)
    up = jnp.where(at == deep - 1, 0.0, pltpu.roll(wide, size - 1, 0)).astype(BF)
    down = jnp.where(at == 0, 0.0, pltpu.roll(wide, 1, 0)).astype(BF)
    shifted = jnp.concatenate([up, delta[...], down], 1)
    stack = coarse_stack([before, own, after], deep)
    acc = dot(stack, shifted, TN).astype(BF)
    rows = acc.shape[0]
    for k in range(3):
        out[k * rows : (k + 1) * rows, :] = acc[:, k * chan : (k + 1) * chan]


def second_delta_body(deep, before, own, after, w, w_up, spread, skip, slope, pg, d0, d1):
    value = coarse_conv([before, own, after], w, deep).astype(BF)
    pg[...] = value
    turned = value.T
    chan = turned.shape[0]
    half = d0.shape[1]
    fine = d0.shape[2]
    outs = [d0, d1]
    for m in range(turned.shape[1] // (2 * deep)):
        up = dot(turned[:, 2 * m * deep : 2 * (m + 1) * deep], spread[...]).astype(BF)
        parts = [
            jnp.concatenate([up[:, (2 * s + c) * fine : (2 * s + c + 1) * fine] for s in range(2)], 1)
            for c in range(2)
        ]
        back = dot(w_up[...], jnp.concatenate(parts, 0))
        for s in range(2):
            for a in range(2):
                for b in range(2):
                    rows = slice((2 * a + b) * half, (2 * a + b + 1) * half)
                    at = 4 * m + 2 * s + b
                    total = back[rows, s * fine : (s + 1) * fine] + skip[a, at].astype(F32)
                    outs[a][at] = (total * slope[a, at]).astype(BF)


def second_grad_body(s0, s1, s2, s3, d0, d1, act_t, pg, out, down, a_scr, b_scr):
    fine_grad([s0, s1, s2, s3], [d0, d1], a_scr, b_scr, out)
    down[...] = dot(act_t[...], pg[...], TN).astype(BF)


def first_delta_body(r0, r1, r2, r3, w, slope, d0, d1):
    rows = [r0, r1, r2, r3]
    outs = [d0, d1]
    for r in range(2):
        for col in range(0, d0.shape[0], 2):
            for side, value in enumerate(fine_pair(rows[r : r + 3], w, col)):
                outs[r][col + side] = (value * slope[r, col + side]).astype(BF)


def first_grad_body(s0, s1, s2, s3, d0, d1, out, a_scr, b_scr):
    fine_grad([s0, s1, s2, s3], [d0, d1], a_scr, b_scr, out)


def input_grad_body(r0, r1, r2, r3, w, out, scr):
    rows = [r0, r1, r2, r3]
    for r in range(2):
        for col in range(0, r0.shape[0], 2):
            for side, value in enumerate(fine_pair(rows[r : r + 3], w, col)):
                scr[col + side] = value
        out[r] = pltpu.einshape("wcd->cwd", scr[...])


def reduced(array):
    size = lax.axis_size(AXIS)
    me = lax.axis_index(AXIS)
    steps = []
    step = 1
    while step < size:
        steps.append(step)
        step *= 2
    for step in steps:
        half = array.shape[0] // 2
        bit = (me // step) % 2
        mine = lax.dynamic_slice_in_dim(array, bit * half, half, 0)
        other = lax.dynamic_slice_in_dim(array, (1 - bit) * half, half, 0)
        got = lax.ppermute(other, AXIS, [(i, i ^ step) for i in range(size)])
        array = (mine.astype(F32) + got.astype(F32)).astype(BF)
    for step in steps[::-1]:
        bit = (me // step) % 2
        got = lax.ppermute(array, AXIS, [(i, i ^ step) for i in range(size)])
        low = jnp.where(bit == 0, array, got)
        high = jnp.where(bit == 0, got, array)
        array = jnp.concatenate([low, high], 0)
    return array


def fine_unpack(flat, chan):
    pairs = flat[: 9 * chan].reshape(9, chan, 2, chan)
    last = flat[9 * chan :].reshape(5, chan, 2, chan).transpose(0, 2, 1, 3).reshape(10, chan, chan)[:9]
    stacked = jnp.stack([pairs[:, :, 0], pairs[:, :, 1], last], 1)
    return stacked.reshape(3, 3, 3, chan, chan).astype(F32)


def body(volume, skip_grad, coarse_grad, w_first, w_second, w_down, w_coarse):
    _, chan, num, deep = volume.shape
    wide = w_coarse.shape[-1]
    half = deep // 2
    size = num // 2 * half
    index = lax.axis_index(AXIS)
    flags = jnp.stack([index, lax.axis_size(AXIS) - 1 - index]).astype(jnp.int32)

    before, after = from_before(volume), from_after(volume)

    forward = lambda w: w.transpose(2, 4, 0, 1, 3).reshape(3 * chan, 9 * chan)
    backward = lambda w: w[::-1, ::-1, ::-1].transpose(2, 3, 0, 1, 4).reshape(3 * chan, 9 * chan)
    first_f, second_f = forward(w_first), forward(w_second)
    first_b, second_b = backward(w_first), backward(w_second)
    coarse_f = w_coarse.transpose(0, 1, 3, 2, 4).reshape(9 * wide, 3 * wide)
    coarse_b = w_coarse[::-1, ::-1, ::-1].transpose(0, 1, 4, 2, 3).reshape(9 * wide, 3 * wide)
    down_f = w_down.transpose(0, 2, 1, 3, 4).reshape(8 * chan, wide)
    down_b = w_down.transpose(0, 1, 3, 2, 4).reshape(4 * chan, 2 * wide)
    skip = skip_grad.transpose(0, 2, 1, 3)

    at = lax.broadcasted_iota(jnp.int32, (deep, deep), 1)
    q = lax.broadcasted_iota(jnp.int32, (deep, deep), 0)
    perm = (at == 2 * (q % half) + q // half).astype(BF)
    row = lax.broadcasted_iota(jnp.int32, (deep, 4 * deep), 0)
    lane = lax.broadcasted_iota(jnp.int32, (deep, 4 * deep), 1)
    spread = (
        (lane // (2 * deep) == row // half)
        & (lane % deep == 2 * (row % half) + (lane // deep) % 2)
    ).astype(BF)

    fine = ((num, chan, deep), BF)
    fine32 = ((2, num, chan, deep), F32)
    coarse = ((size, wide), BF)
    outs = call(
        forward_kernel,
        [fine] * 8 + [fine32] * 2 + [((size, 8 * chan), BF), coarse],
        flags, before, volume, after, first_f, second_f, down_f, perm,
        scratch=(pltpu.VMEM((8, 128), F32), pltpu.VMEM((6, num, chan, deep), BF)),
        smem=1,
    )
    volumes, firsts = outs[:4], outs[4:8]
    slope1, slope2, act_t, pooled = outs[8:]

    rows = [from_before(pooled), pooled, from_after(pooled)]
    (delta,) = call(
        functools.partial(coarse_kernel_body, half), [coarse],
        *rows, coarse_grad.reshape(size, wide), coarse_f,
    )
    delta_rows = [from_before(delta), delta, from_after(delta)]
    (coarse_sum,) = call(
        functools.partial(coarse_grad_body, half), [((27 * wide, wide), BF)], *rows, delta
    )
    pg, d0, d1 = call(
        functools.partial(second_delta_body, half), [coarse, fine, fine],
        *delta_rows, coarse_b, down_b, spread, skip, slope2,
    )
    packed = ((14 * chan, 2 * chan), BF)
    second_rows = [from_before(d1), d0, d1, from_after(d0)]
    second_sum, down_sum = call(
        second_grad_body, [packed, ((8 * chan, wide), BF)], *firsts, d0, d1, act_t, pg,
        scratch=fine_grad_scratch(num, chan, deep),
    )
    e0, e1 = call(first_delta_body, [fine, fine], *second_rows, second_b, slope1)
    first_rows = [from_before(e1), e0, e1, from_after(e0)]
    (first_sum,) = call(
        first_grad_body, [packed], *volumes, e0, e1, scratch=fine_grad_scratch(num, chan, deep)
    )
    (input_grad,) = call(
        input_grad_body, [((2, chan, num, deep), F32)], *first_rows, first_b,
        scratch=(pltpu.VMEM((num, chan, deep), F32),),
    )

    coarse_sum = reduced(coarse_sum)
    middle = reduced(jnp.concatenate([second_sum, down_sum], 0))
    first_sum = reduced(first_sum)
    split = second_sum.shape[0]
    return (
        input_grad,
        fine_unpack(first_sum, chan),
        fine_unpack(middle[:split], chan),
        middle[split:].reshape(2, 2, 2, chan, wide).transpose(0, 2, 1, 3, 4).astype(F32),
        coarse_sum.reshape(3, 3, 3, wide, wide).transpose(1, 2, 0, 3, 4).astype(F32),
    )


def solution(mesh):
    rows = P(("group", "ha"), None, None, None)
    kernels = P("group", None, None, None, None)
    return jax.shard_map(
        body,
        mesh=mesh,
        in_specs=(rows, rows, rows, P(), P(), P(), P()),
        out_specs=(rows, kernels, kernels, kernels, kernels),
        check_vma=False,
    )
```

profile of v0, /device:TPU:1, one launch (start us, length us, event | category | flops | bytes accessed | tf_op | source)
XLA Modules:
  0.0 150.0 jit_solution(3907095834480671450)
XLA Ops:
  0.6 4.5 %collective-permute-start = (bf16[2,64,16,128]{3,2,1,0:T(8,128)(2,1)}, bf16[2,64,16,128]{3,2,1,0:T(8,128)(2,1)S(1)}, u32[]{:S(2)}, u32[]{:S(2)}) collective-permute-start(bf16[2,64,16,128]{3,2,1,0:T(8,128)(2,1)} %own.1), channel_id=1, source_target_pairs={{0,1},{1,2},{2,3},{3,4},{4,5},{5,6},{6,7},{7,8},{8,9},{9,10},{10,1... | collective-permute-start | bytes 1572872 | tf_op jit(solution)/shard_map/ppermute | solution.py:44
  5.2 1.9 %collective-permute-start.1 = (bf16[2,64,16,128]{3,2,1,0:T(8,128)(2,1)}, bf16[2,64,16,128]{3,2,1,0:T(8,128)(2,1)}, u32[]{:S(2)}, u32[]{:S(2)}) collective-permute-start(bf16[2,64,16,128]{3,2,1,0:T(8,128)(2,1)} %own.1), channel_id=1, source_target_pairs={{1,0},{2,1},{3,2},{4,3},{5,4},{6,5},{7,6},{8,7},{9,8},{10,9},{11,1... | collective-permute-start | bytes 1572872 | tf_op jit(solution)/shard_map/ppermute | solution.py:48
  7.2 1.7 %copy.23 = bf16[3,64,3,3,64]{4,3,2,1,0:T(4,128)(2,1)S(1)} copy(bf16[3,64,3,3,64]{1,4,0,3,2:T(8,128)(2,1)} %bitcast.64) | data formatting | bytes 442368 | tf_op jit(solution)/shard_map/transpose | solution.py:298
  9.3 1.8 %reverse_bitcast_fusion.2 = bf16[3,64,3,3,64]{4,1,0,3,2:T(8,128)(2,1)} fusion(bf16[3,3,3,64,64]{4,3,2,1,0:T(8,128)(2,1)} %param.11), kind=kLoop, calls=%fused_computation.15 | loop fusion | bytes 442368 | tf_op jit(solution)/shard_map/transpose | solution.py:299
  11.1 1.6 %copy.24 = bf16[3,64,3,3,64]{4,3,2,1,0:T(4,128)(2,1)S(1)} copy(bf16[3,64,3,3,64]{1,4,0,3,2:T(8,128)(2,1)} %bitcast.63) | data formatting | bytes 442368 | tf_op jit(solution)/shard_map/transpose | solution.py:298
  13.2 0.8 copy.26
  14.6 2.7 %collective-permute-done.before = bf16[2,64,16,128]{3,2,1,0:T(8,128)(2,1)S(1)} collective-permute-done((bf16[2,64,16,128]{3,2,1,0:T(8,128)(2,1)}, bf16[2,64,16,128]{3,2,1,0:T(8,128)(2,1)S(1)}, u32[]{:S(2)}, u32[]{:S(2)}) %collective-permute-start) | collective-permute-done | bytes 524320 | tf_op jit(solution)/shard_map/ppermute | solution.py:44
  17.2 11.0 %shard_map.110 = (bf16[16,64,128]{2,1,0:T(8,128)(2,1)S(1)}, bf16[16,64,128]{2,1,0:T(8,128)(2,1)S(1)}, bf16[16,64,128]{2,1,0:T(8,128)(2,1)S(1)}, bf16[16,64,128]{...) custom-call(s32[2]{0:T(128)S(1)} %pad_add_fusion.flags, ...), custom_call_target="tpu_custom_call" | custom-call | flops 1000000000 | bytes 2179080 | tf_op jit(solution)/shard_map/pallas_call | solution.py:25
  28.3 4.4 %collective-permute-start.2 = (bf16[512,128]{1,0:T(8,128)(2,1)S(1)}, bf16[512,128]{1,0:T(8,128)(2,1)S(1)}, u32[]{:S(2)}, u32[]{:S(2)}) collective-permute-start(bf16[512,128]{1,0:T(8,128)(2,1)S(1)} %get-tuple-element.24.own), channel_id=1, source_target_pairs={{0,1},{1,2},{2,3},{3,4},{4,5},{5,6},{6,7},{7,8},{8,9},{9,10},{10,1... | collective-permute-start | bytes 393224 | tf_op jit(solution)/shard_map/ppermute | solution.py:44
  32.8 1.9 %collective-permute-start.3 = (bf16[512,128]{1,0:T(8,128)(2,1)S(1)}, bf16[512,128]{1,0:T(8,128)(2,1)S(1)}, u32[]{:S(2)}, u32[]{:S(2)}) collective-permute-start(bf16[512,128]{1,0:T(8,128)(2,1)S(1)} %get-tuple-element.24.own), channel_id=1, source_target_pairs={{1,0},{2,1},{3,2},{4,3},{5,4},{6,5},{7,6},{8,7},{9,8},{10,9},{11,1... | collective-permute-start | bytes 393224 | tf_op jit(solution)/shard_map/ppermute | solution.py:48
  34.8 4.3 %collective-permute-done.3.after = bf16[512,128]{1,0:T(8,128)(2,1)S(1)} collective-permute-done((bf16[512,128]{1,0:T(8,128)(2,1)S(1)}, bf16[512,128]{1,0:T(8,128)(2,1)S(1)}, u32[]{:S(2)}, u32[]{:S(2)}) %collective-permute-start.3) | collective-permute-done | bytes 131104 | tf_op jit(solution)/shard_map/ppermute | solution.py:48
  39.1 0.9 shard_map.111.own.delta
  40.0 1.9 %collective-permute-start.4 = (bf16[512,128]{1,0:T(8,128)(2,1)S(1)}, bf16[512,128]{1,0:T(8,128)(2,1)S(1)}, u32[]{:S(2)}, u32[]{:S(2)}) collective-permute-start(bf16[512,128]{1,0:T(8,128)(2,1)S(1)} %shard_map.111.own.delta), channel_id=1, source_target_pairs={{0,1},{1,2},{2,3},{3,4},{4,5},{5,6},{6,7},{7,8},{8,9},{9,10},{10,1... | collective-permute-start | bytes 393224 | tf_op jit(solution)/shard_map/ppermute | solution.py:44
  42.0 2.6 %collective-permute-start.5 = (bf16[512,128]{1,0:T(8,128)(2,1)S(1)}, bf16[512,128]{1,0:T(8,128)(2,1)S(1)}, u32[]{:S(2)}, u32[]{:S(2)}) collective-permute-start(bf16[512,128]{1,0:T(8,128)(2,1)S(1)} %shard_map.111.own.delta), channel_id=1, source_target_pairs={{1,0},{2,1},{3,2},{4,3},{5,4},{6,5},{7,6},{8,7},{9,8},{10,9},{11,1... | collective-permute-start | bytes 393224 | tf_op jit(solution)/shard_map/ppermute | solution.py:48
  44.6 0.8 reverse_bitcast_fusion.1
  45.4 2.0 %copy.27 = bf16[3,3,128,3,128]{4,3,2,1,0:T(4,128)(2,1)} copy(bf16[3,3,128,3,128]{2,4,3,1,0:T(8,128)(2,1)S(1)} %reverse_bitcast_fusion) | data formatting | bytes 1769472 | tf_op jit(solution)/shard_map/transpose | solution.py:303
  47.4 1.5 copy.55
  49.2 1.2 copy.30
  50.4 1.5 reshape.82.w
  51.9 2.2 %copy.31 = bf16[3,64,3,3,64]{4,3,2,1,0:T(4,128)(2,1)} copy(bf16[3,64,3,3,64]{4,1,0,3,2:T(8,128)(2,1)} %reverse_bitcast_fusion.1) | data formatting | bytes 442368 | tf_op jit(solution)/shard_map/transpose | solution.py:299
  54.1 1.5 reshape.83.w
  55.8 0.8 shard_map.117
  57.0 1.4 shard_map.112
  58.4 1.8 %shard_map.116 = (bf16[896,128]{1,0:T(8,128)(2,1)S(1)}, bf16[512,128]{1,0:T(8,128)(2,1)S(1)}) custom-call(bf16[16,64,128]{2,1,0:T(8,128)(2,1)S(1)} %copy-done.14, bf16[16,64,128]{2,1,0:T(8,128)(2,1)S(1)} %copy-done.16, bf16[16,64,128]{2,1,0:T(8,128)(2,1)S(1)} %copy-done.18, bf16[16,64,128]{2,1,0:T(8,128)(2,1)S(1)} %copy-done.20, ...), custom_call_target="tpu_custom_call" | custom-call | flops 1000000000 | bytes 2228224 | tf_op jit(solution)/shard_map/pallas_call | solution.py:25
  61.0 3.1 %collective-permute-start.6 = (bf16[16,64,128]{2,1,0:T(8,128)(2,1)S(1)}, bf16[16,64,128]{2,1,0:T(8,128)(2,1)S(1)}, u32[]{:S(2)}, u32[]{:S(2)}) collective-permute-start(bf16[16,64,128]{2,1,0:T(8,128)(2,1)S(1)} %get-tuple-element.26.r2.d1), channel_id=1, source_target_pairs={{0,1},{1,2},{2,3},{3,4},{4,5},{5,6},{6,7},{7,8},{8,9},{9,10},{10,1... | collective-permute-start | bytes 786440 | tf_op jit(solution)/shard_map/ppermute | solution.py:44
  64.1 1.9 %collective-permute-start.7 = (bf16[16,64,128]{2,1,0:T(8,128)(2,1)S(1)}, bf16[16,64,128]{2,1,0:T(8,128)(2,1)S(1)}, u32[]{:S(2)}, u32[]{:S(2)}) collective-permute-start(bf16[16,64,128]{2,1,0:T(8,128)(2,1)S(1)} %get-tuple-element.27.r1.d0), channel_id=1, source_target_pairs={{1,0},{2,1},{3,2},{4,3},{5,4},{6,5},{7,6},{8,7},{9,8},{10,9},{11,1... | collective-permute-start | bytes 786440 | tf_op jit(solution)/shard_map/ppermute | solution.py:48
  66.2 1.3 collective-permute-start.19
  67.4 5.0 %collective-permute-done.7.r3 = bf16[16,64,128]{2,1,0:T(8,128)(2,1)S(1)} collective-permute-done((bf16[16,64,128]{2,1,0:T(8,128)(2,1)S(1)}, bf16[16,64,128]{2,1,0:T(8,128)(2,1)S(1)}, u32[]{:S(2)}, u32[]{:S(2)}) %collective-permute-start.7) | collective-permute-done | bytes 262176 | tf_op jit(solution)/shard_map/ppermute | solution.py:48
  72.4 1.5 shard_map.113
  73.9 1.9 %collective-permute-start.8 = (bf16[16,64,128]{2,1,0:T(8,128)(2,1)S(1)}, bf16[16,64,128]{2,1,0:T(8,128)(2,1)S(1)}, u32[]{:S(2)}, u32[]{:S(2)}) collective-permute-start(bf16[16,64,128]{2,1,0:T(8,128)(2,1)S(1)} %get-tuple-element.29.r2.d1), channel_id=1, source_target_pairs={{0,1},{1,2},{2,3},{3,4},{4,5},{5,6},{6,7},{7,8},{8,9},{9,10},{10,1... | collective-permute-start | bytes 786440 | tf_op jit(solution)/shard_map/ppermute | solution.py:44
  75.8 2.6 %collective-permute-start.9 = (bf16[16,64,128]{2,1,0:T(8,128)(2,1)S(1)}, bf16[16,64,128]{2,1,0:T(8,128)(2,1)S(1)}, u32[]{:S(2)}, u32[]{:S(2)}) collective-permute-start(bf16[16,64,128]{2,1,0:T(8,128)(2,1)S(1)} %get-tuple-element.30.r1.d0), channel_id=1, source_target_pairs={{1,0},{2,1},{3,2},{4,3},{5,4},{6,5},{7,6},{8,7},{9,8},{10,9},{11,1... | collective-permute-start | bytes 786440 | tf_op jit(solution)/shard_map/ppermute | solution.py:48
  78.5 1.8 %shard_map.115 = bf16[896,128]{1,0:T(8,128)(2,1)S(1)} custom-call(bf16[16,64,128]{2,1,0:T(8,128)(2,1)S(1)} %get-tuple-element.31.s0, bf16[16,64,128]{2,1,0:T(8,128)(2,1)S(1)} %copy-done.8, bf16[16,64,128]{2,1,0:T(8,128)(2,1)S(1)} %copy-done.10, bf16[16,64,128]{2,1,0:T(8,128)(2,1)S(1)} %copy-done.12, bf16[16,64,128]{2,1,0:T(8,128)(2,1)S(1)} %get-tuple-element.30.r1.d0, ...), custom_call_target="tpu_custom_call" | custom-call | flops 1000000000 | bytes 1572864 | tf_op jit(solution)/shard_map/pallas_call | solution.py:25
  80.4 2.7 %collective-permute-start.20 = (bf16[176,128]{1,0:T(8,128)(2,1)S(1)}, bf16[176,128]{1,0:T(8,128)(2,1)S(1)}, u32[]{:S(2)}, u32[]{:S(2)}) collective-permute-start(bf16[176,128]{1,0:T(8,128)(2,1)S(1)} %constant_dynamic-slice_fusion.5), channel_id=1, source_target_pairs={{0,4},{1,5},{2,6},{3,7},{4,0},{5,1},{6,2},{7,3},{8,12},{9,13},{10,... | collective-permute-start | bytes 135176 | tf_op jit(solution)/shard_map/ppermute | solution.py:270
  83.3 1.9 %collective-permute-done.20 = bf16[176,128]{1,0:T(8,128)(2,1)S(1)} collective-permute-done((bf16[176,128]{1,0:T(8,128)(2,1)S(1)}, bf16[176,128]{1,0:T(8,128)(2,1)S(1)}, u32[]{:S(2)}, u32[]{:S(2)}) %collective-permute-start.20) | collective-permute-done | bytes 45088 | tf_op jit(solution)/shard_map/ppermute | solution.py:270
  85.2 2.5 %collective-permute-start.21 = (bf16[88,128]{1,0:T(8,128)(2,1)S(1)}, bf16[88,128]{1,0:T(8,128)(2,1)S(1)}, u32[]{:S(2)}, u32[]{:S(2)}) collective-permute-start(bf16[88,128]{1,0:T(8,128)(2,1)S(1)} %constant_dynamic-slice_fusion.4), channel_id=1, source_target_pairs={{0,8},{1,9},{2,10},{3,11},{4,12},{5,13},{6,14},{7,15},{8,0},{9,1},... | collective-permute-start | bytes 67592 | tf_op jit(solution)/shard_map/ppermute | solution.py:270
  87.8 1.1 collective-permute-done.21
  88.9 2.4 %collective-permute-start.22 = (bf16[88,128]{1,0:T(8,128)(2,1)S(1)}, bf16[88,128]{1,0:T(8,128)(2,1)S(1)}, u32[]{:S(2)}, u32[]{:S(2)}) collective-permute-start(bf16[88,128]{1,0:T(8,128)(2,1)S(1)} %add_convert_fusion.10), channel_id=1, source_target_pairs={{0,8},{1,9},{2,10},{3,11},{4,12},{5,13},{6,14},{7,15},{8,0},{9,1},... | collective-permute-start | bytes 67592 | tf_op jit(solution)/shard_map/ppermute | solution.py:274
  91.5 1.1 collective-permute-done.22
  92.6 2.9 %collective-permute-done.11 = bf16[224,128]{1,0:T(8,128)(2,1)S(1)} collective-permute-done((bf16[224,128]{1,0:T(8,128)(2,1)S(1)}, bf16[224,128]{1,0:T(8,128)(2,1)S(1)}, u32[]{:S(2)}, u32[]{:S(2)}) %collective-permute-start.11) | collective-permute-done | bytes 57376 | tf_op jit(solution)/shard_map/ppermute | solution.py:270
  95.5 0.8 collective-permute-start.12
  96.4 0.7 collective-permute-start.23
  97.1 1.2 collective-permute-done.12
  98.4 0.8 collective-permute-done.23
  99.3 2.6 %collective-permute-done.13 = bf16[56,128]{1,0:T(8,128)(2,1)S(1)} collective-permute-done((bf16[56,128]{1,0:T(8,128)(2,1)S(1)}, bf16[56,128]{1,0:T(8,128)(2,1)S(1)}, u32[]{:S(2)}, u32[]{:S(2)}) %collective-permute-start.13) | collective-permute-done | bytes 14368 | tf_op jit(solution)/shard_map/ppermute | solution.py:270
  102.3 3.1 %collective-permute-done.14 = bf16[56,128]{1,0:T(8,128)(2,1)S(1)} collective-permute-done((bf16[56,128]{1,0:T(8,128)(2,1)S(1)}, bf16[56,128]{1,0:T(8,128)(2,1)S(1)}, u32[]{:S(2)}, u32[]{:S(2)}) %collective-permute-start.14) | collective-permute-done | bytes 14368 | tf_op jit(solution)/shard_map/ppermute | solution.py:274
  105.5 1.0 collective-permute-start.15
  106.5 6.4 %collective-permute-start.25 = (bf16[704,128]{1,0:T(8,128)(2,1)S(1)}, bf16[704,128]{1,0:T(8,128)(2,1)S(1)}, u32[]{:S(2)}, u32[]{:S(2)}) collective-permute-start(bf16[704,128]{1,0:T(8,128)(2,1)S(1)} %pad_maximum_fusion.3), channel_id=1, source_target_pairs={{0,1},{1,0},{2,3},{3,2},{4,5},{5,4},{6,7},{7,6},{8,9},{9,8},{10,11... | collective-permute-start | bytes 540680 | tf_op jit(solution)/shard_map/ppermute | solution.py:274
  113.3 2.5 %shard_map.114 = f32[2,64,16,128]{3,2,1,0:T(8,128)} custom-call(bf16[16,64,128]{2,1,0:T(8,128)(2,1)S(1)} %collective-permute-done.8.r0, bf16[16,64,128]{2,1,0:T(8,128)(2,1)S(1)} %get-tuple-element.30.r1.d0, bf16[16,64,128]{2,1,0:T(8,128)(2,1)S(1)} %get-tuple-element.29.r2.d1, bf16[16,64,128]{2,1,0:T(8,128)(2,1)S(1)} %collective-permute-done.9.r3, ...), custom_call_target="tpu_custom_call" | custom-call | flops 1000000000 | bytes 1269760 | tf_op jit(solution)/shard_map/pallas_call | solution.py:25
  115.9 0.7 collective-permute-start.28
  116.6 3.5 %collective-permute-start.17 = (bf16[448,128]{1,0:T(8,128)(2,1)S(1)}, bf16[448,128]{1,0:T(8,128)(2,1)S(1)}, u32[]{:S(2)}, u32[]{:S(2)}) collective-permute-start(bf16[448,128]{1,0:T(8,128)(2,1)S(1)} %pad_maximum_fusion.5), channel_id=1, source_target_pairs={{0,1},{1,0},{2,3},{3,2},{4,5},{5,4},{6,7},{7,6},{8,9},{9,8},{10,11... | collective-permute-start | bytes 344072 | tf_op jit(solution)/shard_map/ppermute | solution.py:274
  120.1 0.9 collective-permute-start.29
  121.3 0.6 fusion.14
  121.8 0.7 copy_bitcast_fusion.4
  122.6 2.1 %collective-permute-done.29 = bf16[216,128]{1,0:T(8,128)(2,1)S(1)} collective-permute-done((bf16[216,128]{1,0:T(8,128)(2,1)S(1)}, bf16[216,128]{1,0:T(8,128)(2,1)S(1)}, u32[]{:S(2)}, u32[]{:S(2)}) %collective-permute-start.29) | collective-permute-done | bytes 55328 | tf_op jit(solution)/shard_map/ppermute | solution.py:270
  124.7 0.6 collective-permute-start.30
  125.6 4.3 %collective-permute-done.30 = bf16[216,128]{1,0:T(8,128)(2,1)S(1)} collective-permute-done((bf16[216,128]{1,0:T(8,128)(2,1)S(1)}, bf16[216,128]{1,0:T(8,128)(2,1)S(1)}, u32[]{:S(2)}, u32[]{:S(2)}) %collective-permute-start.30) | collective-permute-done | bytes 55328 | tf_op jit(solution)/shard_map/ppermute | solution.py:274
  130.1 1.0 copy.41
  131.1 3.0 %collective-permute-done.31 = bf16[432,128]{1,0:T(8,128)(2,1)S(1)} collective-permute-done((bf16[432,128]{1,0:T(8,128)(2,1)S(1)}, bf16[432,128]{1,0:T(8,128)(2,1)S(1)}, u32[]{:S(2)}, u32[]{:S(2)}) %collective-permute-start.31) | collective-permute-done | bytes 110624 | tf_op jit(solution)/shard_map/ppermute | solution.py:274
  134.2 0.8 collective-permute-start.32
  135.3 3.8 %collective-permute-done.32 = bf16[864,128]{1,0:T(8,128)(2,1)S(1)} collective-permute-done((bf16[864,128]{1,0:T(8,128)(2,1)S(1)}, bf16[864,128]{1,0:T(8,128)(2,1)S(1)}, u32[]{:S(2)}, u32[]{:S(2)}) %collective-permute-start.32) | collective-permute-done | bytes 221216 | tf_op jit(solution)/shard_map/ppermute | solution.py:274
  139.2 7.2 %collective-permute-start.33 = (bf16[1728,128]{1,0:T(8,128)(2,1)S(1)}, bf16[1728,128]{1,0:T(8,128)(2,1)S(1)}, u32[]{:S(2)}, u32[]{:S(2)}) collective-permute-start(bf16[1728,128]{1,0:T(8,128)(2,1)S(1)} %pad_maximum_fusion.1), channel_id=1, source_target_pairs={{0,1},{1,0},{2,3},{3,2},{4,5},{5,4},{6,7},{7,6},{8,9},{9,8},{10,11... | collective-permute-start | bytes 1327112 | tf_op jit(solution)/shard_map/ppermute | solution.py:274
  146.5 0.6 fusion.15
  147.3 1.0 copy.40
  148.6 1.4 copy_bitcast_fusion
  (171 shorter events, 6.5 us)
Async XLA Ops:
  0.6 16.6 %collective-permute-start = (bf16[2,64,16,128]{3,2,1,0:T(8,128)(2,1)}, bf16[2,64,16,128]{3,2,1,0:T(8,128)(2,1)S(1)}, u32[]{:S(2)}, u32[]{:S(2)}) collective-permute-start(bf16[2,64,16,128]{3,2,1,0:T(8,128)(2,1)} %own.1), channel_id=1, source_target_pairs={{0,1},{1,2},{2,3},{3,4},{4,5},{5,6},{6,7},{7,8},{8,9},{9,10},{10,1... | collective-permute-start | bytes 1572872 | tf_op jit(solution)/shard_map/ppermute | solution.py:44
  5.2 12.0 %collective-permute-start.1 = (bf16[2,64,16,128]{3,2,1,0:T(8,128)(2,1)}, bf16[2,64,16,128]{3,2,1,0:T(8,128)(2,1)}, u32[]{:S(2)}, u32[]{:S(2)}) collective-permute-start(bf16[2,64,16,128]{3,2,1,0:T(8,128)(2,1)} %own.1), channel_id=1, source_target_pairs={{1,0},{2,1},{3,2},{4,3},{5,4},{6,5},{7,6},{8,7},{9,8},{10,9},{11,1... | collective-permute-start | bytes 1572872 | tf_op jit(solution)/shard_map/ppermute | solution.py:48
  8.9 4.3 %copy-start.26 = (bf16[2,2,2,64,128]{4,3,2,1,0:T(8,128)(2,1)S(1)}, bf16[2,2,2,64,128]{4,3,2,1,0:T(8,128)(2,1)}, u32[]{:S(2)}) copy-start(bf16[2,2,2,64,128]{4,3,2,1,0:T(8,128)(2,1)} %param.12) | copy-start | bytes 393220
  8.9 4.3 %copy-start.21 = (bf16[3,3,3,128,128]{4,3,2,1,0:T(8,128)(2,1)S(1)}, bf16[3,3,3,128,128]{4,3,2,1,0:T(8,128)(2,1)}, u32[]{:S(2)}) copy-start(bf16[3,3,3,128,128]{4,3,2,1,0:T(8,128)(2,1)} %param.13) | copy-start | bytes 2654212
  13.2 4.0 %copy-start = (bf16[2,64,16,128]{3,2,1,0:T(8,128)(2,1)S(1)}, bf16[2,64,16,128]{3,2,1,0:T(8,128)(2,1)}, u32[]{:S(2)}) copy-start(bf16[2,64,16,128]{3,2,1,0:T(8,128)(2,1)} %own.1) | copy-start | bytes 1572868
  17.2 17.5 %copy-start.22 = (bf16[3,3,3,128,128]{4,3,2,1,0:T(8,128)(2,1)S(1)}, bf16[3,3,3,128,128]{4,3,2,1,0:T(8,128)(2,1)}, u32[]{:S(2)}) copy-start(bf16[3,3,3,128,128]{4,3,2,1,0:T(8,128)(2,1)} %param.13) | copy-start | bytes 2654212
  28.3 11.7 %copy-start.3 = (f32[2,16,64,128]{3,2,1,0:T(8,128)}, f32[2,16,64,128]{3,2,1,0:T(8,128)S(1)}, u32[]{:S(2)}) copy-start(f32[2,16,64,128]{3,2,1,0:T(8,128)S(1)} %get-tuple-element.28.slope) | copy-start | bytes 3145732
  28.3 11.7 %copy-start.5 = (bf16[512,512]{1,0:T(8,128)(2,1)}, bf16[512,512]{1,0:T(8,128)(2,1)S(1)}, u32[]{:S(2)}) copy-start(bf16[512,512]{1,0:T(8,128)(2,1)S(1)} %get-tuple-element.39.act_t) | copy-start | bytes 1572868
  28.3 11.7 %copy-start.7 = (bf16[16,64,128]{2,1,0:T(8,128)(2,1)}, bf16[16,64,128]{2,1,0:T(8,128)(2,1)S(1)}, u32[]{:S(2)}) copy-start(bf16[16,64,128]{2,1,0:T(8,128)(2,1)S(1)} %get-tuple-element.32.s1) | copy-start | bytes 786436
  28.3 11.7 %copy-start.9 = (bf16[16,64,128]{2,1,0:T(8,128)(2,1)}, bf16[16,64,128]{2,1,0:T(8,128)(2,1)S(1)}, u32[]{:S(2)}) copy-start(bf16[16,64,128]{2,1,0:T(8,128)(2,1)S(1)} %get-tuple-element.33.s2) | copy-start | bytes 786436
  28.3 11.7 %copy-start.11 = (bf16[16,64,128]{2,1,0:T(8,128)(2,1)}, bf16[16,64,128]{2,1,0:T(8,128)(2,1)S(1)}, u32[]{:S(2)}) copy-start(bf16[16,64,128]{2,1,0:T(8,128)(2,1)S(1)} %get-tuple-element.34.s3) | copy-start | bytes 786436
  28.3 11.7 %copy-start.13 = (bf16[16,64,128]{2,1,0:T(8,128)(2,1)}, bf16[16,64,128]{2,1,0:T(8,128)(2,1)S(1)}, u32[]{:S(2)}) copy-start(bf16[16,64,128]{2,1,0:T(8,128)(2,1)S(1)} %get-tuple-element.35.s0) | copy-start | bytes 786436
  28.3 11.7 %copy-start.15 = (bf16[16,64,128]{2,1,0:T(8,128)(2,1)}, bf16[16,64,128]{2,1,0:T(8,128)(2,1)S(1)}, u32[]{:S(2)}) copy-start(bf16[16,64,128]{2,1,0:T(8,128)(2,1)S(1)} %get-tuple-element.36.s1) | copy-start | bytes 786436
  28.3 11.7 %copy-start.17 = (bf16[16,64,128]{2,1,0:T(8,128)(2,1)}, bf16[16,64,128]{2,1,0:T(8,128)(2,1)S(1)}, u32[]{:S(2)}) copy-start(bf16[16,64,128]{2,1,0:T(8,128)(2,1)S(1)} %get-tuple-element.37.s2) | copy-start | bytes 786436
  28.3 11.7 %copy-start.19 = (bf16[16,64,128]{2,1,0:T(8,128)(2,1)}, bf16[16,64,128]{2,1,0:T(8,128)(2,1)S(1)}, u32[]{:S(2)}) copy-start(bf16[16,64,128]{2,1,0:T(8,128)(2,1)S(1)} %get-tuple-element.38.s3) | copy-start | bytes 786436
  28.3 10.7 %copy-start.1 = (bf16[1,8,64,128]{3,2,1,0:T(8,128)(2,1)S(1)}, bf16[1,8,64,128]{3,2,1,0:T(8,128)(2,1)}, u32[]{:S(2)}) copy-start(bf16[1,8,64,128]{3,2,1,0:T(8,128)(2,1)} %param.9) | copy-start | bytes 393220
  28.3 6.4 %collective-permute-start.2 = (bf16[512,128]{1,0:T(8,128)(2,1)S(1)}, bf16[512,128]{1,0:T(8,128)(2,1)S(1)}, u32[]{:S(2)}, u32[]{:S(2)}) collective-permute-start(bf16[512,128]{1,0:T(8,128)(2,1)S(1)} %get-tuple-element.24.own), channel_id=1, source_target_pairs={{0,1},{1,2},{2,3},{3,4},{4,5},{5,6},{6,7},{7,8},{8,9},{9,10},{10,1... | collective-permute-start | bytes 393224 | tf_op jit(solution)/shard_map/ppermute | solution.py:44
  32.8 6.3 %collective-permute-start.3 = (bf16[512,128]{1,0:T(8,128)(2,1)S(1)}, bf16[512,128]{1,0:T(8,128)(2,1)S(1)}, u32[]{:S(2)}, u32[]{:S(2)}) collective-permute-start(bf16[512,128]{1,0:T(8,128)(2,1)S(1)} %get-tuple-element.24.own), channel_id=1, source_target_pairs={{1,0},{2,1},{3,2},{4,3},{5,4},{6,5},{7,6},{8,7},{9,8},{10,9},{11,1... | collective-permute-start | bytes 393224 | tf_op jit(solution)/shard_map/ppermute | solution.py:48
  39.0 5.5 %copy-start.23 = (bf16[3,3,3,64,64]{4,3,2,1,0:T(8,128)(2,1)S(1)}, bf16[3,3,3,64,64]{4,3,2,1,0:T(8,128)(2,1)}, u32[]{:S(2)}) copy-start(bf16[3,3,3,64,64]{4,3,2,1,0:T(8,128)(2,1)} %param.10) | copy-start | bytes 663556
  40.0 16.5 %collective-permute-start.4 = (bf16[512,128]{1,0:T(8,128)(2,1)S(1)}, bf16[512,128]{1,0:T(8,128)(2,1)S(1)}, u32[]{:S(2)}, u32[]{:S(2)}) collective-permute-start(bf16[512,128]{1,0:T(8,128)(2,1)S(1)} %shard_map.111.own.delta), channel_id=1, source_target_pairs={{0,1},{1,2},{2,3},{3,4},{4,5},{5,6},{6,7},{7,8},{8,9},{9,10},{10,1... | collective-permute-start | bytes 393224 | tf_op jit(solution)/shard_map/ppermute | solution.py:44
  42.0 14.6 %collective-permute-start.5 = (bf16[512,128]{1,0:T(8,128)(2,1)S(1)}, bf16[512,128]{1,0:T(8,128)(2,1)S(1)}, u32[]{:S(2)}, u32[]{:S(2)}) collective-permute-start(bf16[512,128]{1,0:T(8,128)(2,1)S(1)} %shard_map.111.own.delta), channel_id=1, source_target_pairs={{1,0},{2,1},{3,2},{4,3},{5,4},{6,5},{7,6},{8,7},{9,8},{10,9},{11,1... | collective-permute-start | bytes 393224 | tf_op jit(solution)/shard_map/ppermute | solution.py:48
  45.4 3.5 %copy-start.27 = (bf16[2,2,2,64,128]{4,3,2,1,0:T(8,128)(2,1)S(1)}, bf16[2,2,2,64,128]{4,3,2,1,0:T(8,128)(2,1)}, u32[]{:S(2)}) copy-start(bf16[2,2,2,64,128]{4,3,2,1,0:T(8,128)(2,1)} %param.12) | copy-start | bytes 393220
  47.4 1.7 %copy-start.25 = (bf16[2,64,16,128]{3,2,1,0:T(8,128)(2,1)S(1)}, bf16[2,64,16,128]{3,2,1,0:T(8,128)(2,1)}, u32[]{:S(2)}) copy-start(bf16[2,64,16,128]{3,2,1,0:T(8,128)(2,1)} %param.8) | copy-start | bytes 1572868
  47.4 1.8 %copy-start.24 = (bf16[3,64,3,3,64]{4,1,0,3,2:T(8,128)(2,1)S(1)}, bf16[3,64,3,3,64]{4,1,0,3,2:T(8,128)(2,1)}, u32[]{:S(2)}) copy-start(bf16[3,64,3,3,64]{4,1,0,3,2:T(8,128)(2,1)} %reverse_bitcast_fusion.2) | copy-start | bytes 663556
  55.7 1.2 copy-start.2
  57.0 1.4 copy-start.6
  57.0 1.4 copy-start.14
  57.0 1.4 copy-start.16
  57.0 1.4 copy-start.18
  57.0 1.4 copy-start.20
  60.2 12.2 %copy-start.4 = (f32[2,16,64,128]{3,2,1,0:T(8,128)S(1)}, f32[2,16,64,128]{3,2,1,0:T(8,128)}, u32[]{:S(2)}) copy-start(f32[2,16,64,128]{3,2,1,0:T(8,128)} %copy-done.3) | copy-start | bytes 3145732
  60.3 5.8 %collective-permute-start.18 = (bf16[704,128]{1,0:T(8,128)(2,1)S(1)}, bf16[704,128]{1,0:T(8,128)(2,1)S(1)}, u32[]{:S(2)}, u32[]{:S(2)}) collective-permute-start(bf16[704,128]{1,0:T(8,128)(2,1)S(1)} %constant_dynamic-slice_fusion.7), channel_id=1, source_target_pairs={{0,1},{1,0},{2,3},{3,2},{4,5},{5,4},{6,7},{7,6},{8,9},{9,8},{10,11... | collective-permute-start | bytes 540680 | tf_op jit(solution)/shard_map/ppermute | solution.py:270
  60.4 22.7 %collective-permute-start.26 = (bf16[1728,128]{1,0:T(8,128)(2,1)S(1)}, bf16[1728,128]{1,0:T(8,128)(2,1)S(1)}, u32[]{:S(2)}, u32[]{:S(2)}) collective-permute-start(bf16[1728,128]{1,0:T(8,128)(2,1)S(1)} %constant_dynamic-slice_fusion.3), channel_id=1, source_target_pairs={{0,1},{1,0},{2,3},{3,2},{4,5},{5,4},{6,7},{7,6},{8,9},{9,8},{10,11... | collective-permute-start | bytes 1327112 | tf_op jit(solution)/shard_map/ppermute | solution.py:270
  61.0 6.5 %collective-permute-start.6 = (bf16[16,64,128]{2,1,0:T(8,128)(2,1)S(1)}, bf16[16,64,128]{2,1,0:T(8,128)(2,1)S(1)}, u32[]{:S(2)}, u32[]{:S(2)}) collective-permute-start(bf16[16,64,128]{2,1,0:T(8,128)(2,1)S(1)} %get-tuple-element.26.r2.d1), channel_id=1, source_target_pairs={{0,1},{1,2},{2,3},{3,4},{4,5},{5,6},{6,7},{7,8},{8,9},{9,10},{10,1... | collective-permute-start | bytes 786440 | tf_op jit(solution)/shard_map/ppermute | solution.py:44
  64.1 8.3 %collective-permute-start.7 = (bf16[16,64,128]{2,1,0:T(8,128)(2,1)S(1)}, bf16[16,64,128]{2,1,0:T(8,128)(2,1)S(1)}, u32[]{:S(2)}, u32[]{:S(2)}) collective-permute-start(bf16[16,64,128]{2,1,0:T(8,128)(2,1)S(1)} %get-tuple-element.27.r1.d0), channel_id=1, source_target_pairs={{1,0},{2,1},{3,2},{4,3},{5,4},{6,5},{7,6},{8,7},{9,8},{10,9},{11,1... | collective-permute-start | bytes 786440 | tf_op jit(solution)/shard_map/ppermute | solution.py:48
  66.2 14.2 %collective-permute-start.19 = (bf16[352,128]{1,0:T(8,128)(2,1)S(1)}, bf16[352,128]{1,0:T(8,128)(2,1)S(1)}, u32[]{:S(2)}, u32[]{:S(2)}) collective-permute-start(bf16[352,128]{1,0:T(8,128)(2,1)S(1)} %constant_dynamic-slice_fusion.6), channel_id=1, source_target_pairs={{0,2},{1,3},{2,0},{3,1},{4,6},{5,7},{6,4},{7,5},{8,10},{9,11},{10,... | collective-permute-start | bytes 270344 | tf_op jit(solution)/shard_map/ppermute | solution.py:270
  72.4 6.1 %copy-start.8 = (bf16[16,64,128]{2,1,0:T(8,128)(2,1)S(1)}, bf16[16,64,128]{2,1,0:T(8,128)(2,1)}, u32[]{:S(2)}) copy-start(bf16[16,64,128]{2,1,0:T(8,128)(2,1)} %copy-done.7) | copy-start | bytes 786436
  72.4 6.1 %copy-start.10 = (bf16[16,64,128]{2,1,0:T(8,128)(2,1)S(1)}, bf16[16,64,128]{2,1,0:T(8,128)(2,1)}, u32[]{:S(2)}) copy-start(bf16[16,64,128]{2,1,0:T(8,128)(2,1)} %copy-done.9) | copy-start | bytes 786436
  72.4 6.1 %copy-start.12 = (bf16[16,64,128]{2,1,0:T(8,128)(2,1)S(1)}, bf16[16,64,128]{2,1,0:T(8,128)(2,1)}, u32[]{:S(2)}) copy-start(bf16[16,64,128]{2,1,0:T(8,128)(2,1)} %copy-done.11) | copy-start | bytes 786436
  73.9 39.4 %collective-permute-start.8 = (bf16[16,64,128]{2,1,0:T(8,128)(2,1)S(1)}, bf16[16,64,128]{2,1,0:T(8,128)(2,1)S(1)}, u32[]{:S(2)}, u32[]{:S(2)}) collective-permute-start(bf16[16,64,128]{2,1,0:T(8,128)(2,1)S(1)} %get-tuple-element.29.r2.d1), channel_id=1, source_target_pairs={{0,1},{1,2},{2,3},{3,4},{4,5},{5,6},{6,7},{7,8},{8,9},{9,10},{10,1... | collective-permute-start | bytes 786440 | tf_op jit(solution)/shard_map/ppermute | solution.py:44
  75.8 37.5 %collective-permute-start.9 = (bf16[16,64,128]{2,1,0:T(8,128)(2,1)S(1)}, bf16[16,64,128]{2,1,0:T(8,128)(2,1)S(1)}, u32[]{:S(2)}, u32[]{:S(2)}) collective-permute-start(bf16[16,64,128]{2,1,0:T(8,128)(2,1)S(1)} %get-tuple-element.30.r1.d0), channel_id=1, source_target_pairs={{1,0},{2,1},{3,2},{4,3},{5,4},{6,5},{7,6},{8,7},{9,8},{10,9},{11,1... | collective-permute-start | bytes 786440 | tf_op jit(solution)/shard_map/ppermute | solution.py:48
  80.3 11.1 %collective-permute-start.10 = (bf16[448,128]{1,0:T(8,128)(2,1)S(1)}, bf16[448,128]{1,0:T(8,128)(2,1)S(1)}, u32[]{:S(2)}, u32[]{:S(2)}) collective-permute-start(bf16[448,128]{1,0:T(8,128)(2,1)S(1)} %constant_dynamic-slice_fusion.11), channel_id=1, source_target_pairs={{0,1},{1,0},{2,3},{3,2},{4,5},{5,4},{6,7},{7,6},{8,9},{9,8},{10,11... | collective-permute-start | bytes 344072 | tf_op jit(solution)/shard_map/ppermute | solution.py:270
  80.4 4.7 %collective-permute-start.20 = (bf16[176,128]{1,0:T(8,128)(2,1)S(1)}, bf16[176,128]{1,0:T(8,128)(2,1)S(1)}, u32[]{:S(2)}, u32[]{:S(2)}) collective-permute-start(bf16[176,128]{1,0:T(8,128)(2,1)S(1)} %constant_dynamic-slice_fusion.5), channel_id=1, source_target_pairs={{0,4},{1,5},{2,6},{3,7},{4,0},{5,1},{6,2},{7,3},{8,12},{9,13},{10,... | collective-permute-start | bytes 135176 | tf_op jit(solution)/shard_map/ppermute | solution.py:270
  85.2 3.7 %collective-permute-start.21 = (bf16[88,128]{1,0:T(8,128)(2,1)S(1)}, bf16[88,128]{1,0:T(8,128)(2,1)S(1)}, u32[]{:S(2)}, u32[]{:S(2)}) collective-permute-start(bf16[88,128]{1,0:T(8,128)(2,1)S(1)} %constant_dynamic-slice_fusion.4), channel_id=1, source_target_pairs={{0,8},{1,9},{2,10},{3,11},{4,12},{5,13},{6,14},{7,15},{8,0},{9,1},... | collective-permute-start | bytes 67592 | tf_op jit(solution)/shard_map/ppermute | solution.py:270
  87.7 28.0 %collective-permute-start.27 = (bf16[864,128]{1,0:T(8,128)(2,1)S(1)}, bf16[864,128]{1,0:T(8,128)(2,1)S(1)}, u32[]{:S(2)}, u32[]{:S(2)}) collective-permute-start(bf16[864,128]{1,0:T(8,128)(2,1)S(1)} %constant_dynamic-slice_fusion.2), channel_id=1, source_target_pairs={{0,2},{1,3},{2,0},{3,1},{4,6},{5,7},{6,4},{7,5},{8,10},{9,11},{10,... | collective-permute-start | bytes 663560 | tf_op jit(solution)/shard_map/ppermute | solution.py:270
  88.9 3.6 %collective-permute-start.22 = (bf16[88,128]{1,0:T(8,128)(2,1)S(1)}, bf16[88,128]{1,0:T(8,128)(2,1)S(1)}, u32[]{:S(2)}, u32[]{:S(2)}) collective-permute-start(bf16[88,128]{1,0:T(8,128)(2,1)S(1)} %add_convert_fusion.10), channel_id=1, source_target_pairs={{0,8},{1,9},{2,10},{3,11},{4,12},{5,13},{6,14},{7,15},{8,0},{9,1},... | collective-permute-start | bytes 67592 | tf_op jit(solution)/shard_map/ppermute | solution.py:274
  91.4 4.1 %collective-permute-start.11 = (bf16[224,128]{1,0:T(8,128)(2,1)S(1)}, bf16[224,128]{1,0:T(8,128)(2,1)S(1)}, u32[]{:S(2)}, u32[]{:S(2)}) collective-permute-start(bf16[224,128]{1,0:T(8,128)(2,1)S(1)} %constant_dynamic-slice_fusion.10), channel_id=1, source_target_pairs={{0,2},{1,3},{2,0},{3,1},{4,6},{5,7},{6,4},{7,5},{8,10},{9,11},{10,... | collective-permute-start | bytes 172040 | tf_op jit(solution)/shard_map/ppermute | solution.py:270
  95.5 2.8 %collective-permute-start.12 = (bf16[112,128]{1,0:T(8,128)(2,1)S(1)}, bf16[112,128]{1,0:T(8,128)(2,1)S(1)}, u32[]{:S(2)}, u32[]{:S(2)}) collective-permute-start(bf16[112,128]{1,0:T(8,128)(2,1)S(1)} %constant_dynamic-slice_fusion.9), channel_id=1, source_target_pairs={{0,4},{1,5},{2,6},{3,7},{4,0},{5,1},{6,2},{7,3},{8,12},{9,13},{10,... | collective-permute-start | bytes 86024 | tf_op jit(solution)/shard_map/ppermute | solution.py:270
  96.4 2.9 %collective-permute-start.23 = (bf16[176,128]{1,0:T(8,128)(2,1)S(1)}, bf16[176,128]{1,0:T(8,128)(2,1)S(1)}, u32[]{:S(2)}, u32[]{:S(2)}) collective-permute-start(bf16[176,128]{1,0:T(8,128)(2,1)S(1)} %pad_maximum_fusion.10), channel_id=1, source_target_pairs={{0,4},{1,5},{2,6},{3,7},{4,0},{5,1},{6,2},{7,3},{8,12},{9,13},{10,... | collective-permute-start | bytes 135176 | tf_op jit(solution)/shard_map/ppermute | solution.py:274
  98.4 3.5 %collective-permute-start.13 = (bf16[56,128]{1,0:T(8,128)(2,1)S(1)}, bf16[56,128]{1,0:T(8,128)(2,1)S(1)}, u32[]{:S(2)}, u32[]{:S(2)}) collective-permute-start(bf16[56,128]{1,0:T(8,128)(2,1)S(1)} %constant_dynamic-slice_fusion.8), channel_id=1, source_target_pairs={{0,8},{1,9},{2,10},{3,11},{4,12},{5,13},{6,14},{7,15},{8,0},{9,1},... | collective-permute-start | bytes 43016 | tf_op jit(solution)/shard_map/ppermute | solution.py:270
  101.9 3.5 %collective-permute-start.14 = (bf16[56,128]{1,0:T(8,128)(2,1)S(1)}, bf16[56,128]{1,0:T(8,128)(2,1)S(1)}, u32[]{:S(2)}, u32[]{:S(2)}) collective-permute-start(bf16[56,128]{1,0:T(8,128)(2,1)S(1)} %add_convert_fusion.11), channel_id=1, source_target_pairs={{0,8},{1,9},{2,10},{3,11},{4,12},{5,13},{6,14},{7,15},{8,0},{9,1},... | collective-permute-start | bytes 43016 | tf_op jit(solution)/shard_map/ppermute | solution.py:274
  102.0 4.4 %collective-permute-start.24 = (bf16[352,128]{1,0:T(8,128)(2,1)S(1)}, bf16[352,128]{1,0:T(8,128)(2,1)S(1)}, u32[]{:S(2)}, u32[]{:S(2)}) collective-permute-start(bf16[352,128]{1,0:T(8,128)(2,1)S(1)} %pad_maximum_fusion.7), channel_id=1, source_target_pairs={{0,2},{1,3},{2,0},{3,1},{4,6},{5,7},{6,4},{7,5},{8,10},{9,11},{10,... | collective-permute-start | bytes 270344 | tf_op jit(solution)/shard_map/ppermute | solution.py:274
  105.5 7.5 %collective-permute-start.15 = (bf16[112,128]{1,0:T(8,128)(2,1)S(1)}, bf16[112,128]{1,0:T(8,128)(2,1)S(1)}, u32[]{:S(2)}, u32[]{:S(2)}) collective-permute-start(bf16[112,128]{1,0:T(8,128)(2,1)S(1)} %pad_maximum_fusion.11), channel_id=1, source_target_pairs={{0,4},{1,5},{2,6},{3,7},{4,0},{5,1},{6,2},{7,3},{8,12},{9,13},{10,... | collective-permute-start | bytes 86024 | tf_op jit(solution)/shard_map/ppermute | solution.py:274
  106.5 14.5 %collective-permute-start.25 = (bf16[704,128]{1,0:T(8,128)(2,1)S(1)}, bf16[704,128]{1,0:T(8,128)(2,1)S(1)}, u32[]{:S(2)}, u32[]{:S(2)}) collective-permute-start(bf16[704,128]{1,0:T(8,128)(2,1)S(1)} %pad_maximum_fusion.3), channel_id=1, source_target_pairs={{0,1},{1,0},{2,3},{3,2},{4,5},{5,4},{6,7},{7,6},{8,9},{9,8},{10,11... | collective-permute-start | bytes 540680 | tf_op jit(solution)/shard_map/ppermute | solution.py:274
  113.0 3.6 %collective-permute-start.16 = (bf16[224,128]{1,0:T(8,128)(2,1)S(1)}, bf16[224,128]{1,0:T(8,128)(2,1)S(1)}, u32[]{:S(2)}, u32[]{:S(2)}) collective-permute-start(bf16[224,128]{1,0:T(8,128)(2,1)S(1)} %pad_maximum_fusion.9), channel_id=1, source_target_pairs={{0,2},{1,3},{2,0},{3,1},{4,6},{5,7},{6,4},{7,5},{8,10},{9,11},{10,... | collective-permute-start | bytes 172040 | tf_op jit(solution)/shard_map/ppermute | solution.py:274
  115.9 4.2 %collective-permute-start.28 = (bf16[432,128]{1,0:T(8,128)(2,1)S(1)}, bf16[432,128]{1,0:T(8,128)(2,1)S(1)}, u32[]{:S(2)}, u32[]{:S(2)}) collective-permute-start(bf16[432,128]{1,0:T(8,128)(2,1)S(1)} %constant_dynamic-slice_fusion.1), channel_id=1, source_target_pairs={{0,4},{1,5},{2,6},{3,7},{4,0},{5,1},{6,2},{7,3},{8,12},{9,13},{10,... | collective-permute-start | bytes 331784 | tf_op jit(solution)/shard_map/ppermute | solution.py:270
  116.6 18.4 %collective-permute-start.17 = (bf16[448,128]{1,0:T(8,128)(2,1)S(1)}, bf16[448,128]{1,0:T(8,128)(2,1)S(1)}, u32[]{:S(2)}, u32[]{:S(2)}) collective-permute-start(bf16[448,128]{1,0:T(8,128)(2,1)S(1)} %pad_maximum_fusion.5), channel_id=1, source_target_pairs={{0,1},{1,0},{2,3},{3,2},{4,5},{5,4},{6,7},{7,6},{8,9},{9,8},{10,11... | collective-permute-start | bytes 344072 | tf_op jit(solution)/shard_map/ppermute | solution.py:274
  120.1 4.6 %collective-permute-start.29 = (bf16[216,128]{1,0:T(8,128)(2,1)S(1)}, bf16[216,128]{1,0:T(8,128)(2,1)S(1)}, u32[]{:S(2)}, u32[]{:S(2)}) collective-permute-start(bf16[216,128]{1,0:T(8,128)(2,1)S(1)} %constant_dynamic-slice_fusion), channel_id=1, source_target_pairs={{0,8},{1,9},{2,10},{3,11},{4,12},{5,13},{6,14},{7,15},{8,0},{9,1},... | collective-permute-start | bytes 165896 | tf_op jit(solution)/shard_map/ppermute | solution.py:270
  124.7 5.1 %collective-permute-start.30 = (bf16[216,128]{1,0:T(8,128)(2,1)S(1)}, bf16[216,128]{1,0:T(8,128)(2,1)S(1)}, u32[]{:S(2)}, u32[]{:S(2)}) collective-permute-start(bf16[216,128]{1,0:T(8,128)(2,1)S(1)} %add_convert_fusion.7), channel_id=1, source_target_pairs={{0,8},{1,9},{2,10},{3,11},{4,12},{5,13},{6,14},{7,15},{8,0},{9,1},... | collective-permute-start | bytes 165896 | tf_op jit(solution)/shard_map/ppermute | solution.py:274
  129.9 4.3 %collective-permute-start.31 = (bf16[432,128]{1,0:T(8,128)(2,1)S(1)}, bf16[432,128]{1,0:T(8,128)(2,1)S(1)}, u32[]{:S(2)}, u32[]{:S(2)}) collective-permute-start(bf16[432,128]{1,0:T(8,128)(2,1)S(1)} %pad_maximum_fusion.6), channel_id=1, source_target_pairs={{0,4},{1,5},{2,6},{3,7},{4,0},{5,1},{6,2},{7,3},{8,12},{9,13},{10,... | collective-permute-start | bytes 331784 | tf_op jit(solution)/shard_map/ppermute | solution.py:274
  134.2 4.8 %collective-permute-start.32 = (bf16[864,128]{1,0:T(8,128)(2,1)S(1)}, bf16[864,128]{1,0:T(8,128)(2,1)S(1)}, u32[]{:S(2)}, u32[]{:S(2)}) collective-permute-start(bf16[864,128]{1,0:T(8,128)(2,1)S(1)} %pad_maximum_fusion.2), channel_id=1, source_target_pairs={{0,2},{1,3},{2,0},{3,1},{4,6},{5,7},{6,4},{7,5},{8,10},{9,11},{10,... | collective-permute-start | bytes 663560 | tf_op jit(solution)/shard_map/ppermute | solution.py:274
  139.2 9.1 %collective-permute-start.33 = (bf16[1728,128]{1,0:T(8,128)(2,1)S(1)}, bf16[1728,128]{1,0:T(8,128)(2,1)S(1)}, u32[]{:S(2)}, u32[]{:S(2)}) collective-permute-start(bf16[1728,128]{1,0:T(8,128)(2,1)S(1)} %pad_maximum_fusion.1), channel_id=1, source_target_pairs={{0,1},{1,0},{2,3},{3,2},{4,5},{5,4},{6,7},{7,6},{8,9},{9,8},{10,11... | collective-permute-start | bytes 1327112 | tf_op jit(solution)/shard_map/ppermute | solution.py:274
where the time goes:
time: 151 us; the launch traced here: 150 us
  starting transfers between devices  60.2 us (40%)
  waiting for transfers between devices  39.9 us (26%)
  local copies, waits for them, and re-layouts  22.4 us (15%)
  Pallas kernels  21.6 us (14%)
  other arithmetic  4.08 us (3%)
  between operations  1.88 us (1%)
    ppermute x12, starting transfers between devices, reduced(): got = lax.ppermute(array, AXIS, [(i, i ^ step) for i in range(size)])  23.4 us
    pallas_call x8, Pallas kernels, call(): pl.pallas_call(body, out_shape=[jax.ShapeDtypeStruct(s, d) for s, d in ou...  21.6 us
    ppermute x12, waiting for transfers between devices, reduced(): got = lax.ppermute(array, AXIS, [(i, i ^ step) for i in range(size)])  16.1 us
    ppermute x5, starting transfers between devices, from_before(): return lax.ppermute(array, AXIS, neighbours(array)[0])  15.9 us
    ppermute x12, waiting for transfers between devices, reduced(): got = lax.ppermute(other, AXIS, [(i, i ^ step) for i in range(size)])  11.9 us
    ppermute x5, starting transfers between devices, from_after(): return lax.ppermute(array, AXIS, neighbours(array)[1])  11 us
    ppermute x12, starting transfers between devices, reduced(): got = lax.ppermute(other, AXIS, [(i, i ^ step) for i in range(size)])  9.84 us
    ppermute x5, waiting for transfers between devices, from_after(): return lax.ppermute(array, AXIS, neighbours(array)[1])  9.25 us
  transfers between devices with their start and end apart: 34, of which 15 were waited for; matrix products, arithmetic and copies ran while one was open for 16% of the time, Pallas kernels for 4%

commit v1 on v0

v1 whole, which is shorter than its diff:
```python
import functools

import jax
import jax.numpy as jnp
from jax import lax
from jax.experimental import pallas as pl
from jax.experimental.pallas import tpu as pltpu
from jax.sharding import PartitionSpec as P

BF = jnp.bfloat16
F32 = jnp.float32
NT = (((1,), (1,)), ((), ()))
TN = (((0,), (0,)), ((), ()))
AXIS = "ha"


def dot(a, b, dims=(((1,), (0,)), ((), ()))):
    return lax.dot_general(a, b, dims, preferred_element_type=F32)


def call(body, outs, *args, scratch=(), flops=10**9, smem=0):
    in_specs = [pl.BlockSpec(memory_space=pltpu.SMEM)] * smem
    in_specs += [pl.BlockSpec(memory_space=pltpu.VMEM)] * (len(args) - smem)
    size = sum(a.size * a.dtype.itemsize for a in args)
    return pl.pallas_call(
        body,
        out_shape=[jax.ShapeDtypeStruct(s, d) for s, d in outs],
        in_specs=in_specs,
        out_specs=[pl.BlockSpec(memory_space=pltpu.VMEM)] * len(outs),
        scratch_shapes=list(scratch),
        compiler_params=pltpu.CompilerParams(vmem_limit_bytes=48 * 2**20),
        cost_estimate=pl.CostEstimate(flops=flops, bytes_accessed=size, transcendentals=0),
    )(*args)


def neighbours(array):
    size = lax.axis_size(AXIS)
    up = [(i, i + 1) for i in range(size - 1)]
    down = [(j, i) for i, j in up]
    return up, down


def from_before(array):
    return lax.ppermute(array, AXIS, neighbours(array)[0])


def from_after(array):
    return lax.ppermute(array, AXIS, neighbours(array)[1])


def swapped(array, stride):
    size = lax.axis_size(AXIS)
    return lax.ppermute(array, AXIS, [(i, i ^ stride) for i in range(size)])


def shifted(array, stride, by):
    size = lax.axis_size(AXIS)
    return lax.ppermute(array, AXIS, [(i, (i + by * stride) % size) for i in range(size)])


def sigmoid(value):
    return 0.5 + 0.5 * jnp.tanh(0.5 * value)


def fine_pair(rows, w_ref, col):
    num = rows[0].shape[0]
    chan, deep = rows[0].shape[1], rows[0].shape[2]
    none = jnp.zeros((chan, deep), BF)
    sides = []
    for at in (col, col + 1):
        tiles = []
        for row in rows:
            for k in (-1, 0, 1):
                tiles.append(row[at + k] if 0 <= at + k < num else none)
        sides.append(jnp.concatenate(tiles, 0))
    y = dot(w_ref[...], jnp.concatenate(sides, 1))
    lane = lax.broadcasted_iota(jnp.int32, (chan, deep), 1)
    outs = []
    for side in range(2):
        part = y[:, side * deep : (side + 1) * deep]
        left = jnp.where(lane == 0, 0.0, pltpu.roll(part[:chan], 1, 1))
        right = jnp.where(lane == deep - 1, 0.0, pltpu.roll(part[2 * chan :], deep - 1, 1))
        outs.append(part[chan : 2 * chan] + left + right)
    return outs


def put(halves, block, value):
    num = value.shape[0]
    each = halves.shape[1] // num
    at = block % each * num
    halves[block // each, at : at + num, :] = value


def deal(halves, bit, mine, other):
    mine[...] = halves[bit]
    other[...] = halves[1 - bit]


def fine_grad(sources, deltas, a_scr, b_scr, halves):
    num, chan, deep = deltas[0].shape
    lane = lax.broadcasted_iota(jnp.int32, (chan, deep), 1)
    for r in range(2):
        for at in range(num):
            cols = slice((r * num + at) * deep, (r * num + at + 1) * deep)
            for kh in range(3):
                for kw in range(3):
                    tap = kh * 3 + kw
                    src = at + kw - 1
                    tile = sources[r + kh][src] if 0 <= src < num else jnp.zeros((chan, deep), BF)
                    a_scr[tap * chan : (tap + 1) * chan, cols] = tile
            value = deltas[r][at]
            wide = value.astype(F32)
            b_scr[:chan, cols] = jnp.where(
                lane == deep - 1, 0.0, pltpu.roll(wide, deep - 1, 1)
            ).astype(BF)
            b_scr[chan : 2 * chan, cols] = value
            b_scr[2 * chan :, cols] = jnp.where(lane == 0, 0.0, pltpu.roll(wide, 1, 1)).astype(BF)
    acc = dot(a_scr[...], b_scr[...], NT).astype(BF)
    for tap in range(9):
        put(halves, tap, acc[tap * chan : (tap + 1) * chan, : 2 * chan])
    for tap in range(0, 10, 2):
        first = acc[tap * chan : (tap + 1) * chan, 2 * chan :]
        if tap + 1 < 9:
            other = acc[(tap + 1) * chan : (tap + 2) * chan, 2 * chan :]
        else:
            other = jnp.zeros_like(first)
        put(halves, 9 + tap // 2, jnp.concatenate([first, other], 1))


def fine_grad_scratch(num, chan, deep):
    return (
        pltpu.VMEM((9 * chan, 2 * num * deep), BF),
        pltpu.VMEM((3 * chan, 2 * num * deep), BF),
    )


def coarse_stack(rows, deep):
    size, chan = rows[0].shape
    none = jnp.zeros((deep, chan), BF)
    tiles = []
    for row in rows:
        value = row[...]
        tiles.append(jnp.concatenate([none, value[: size - deep]], 0))
        tiles.append(value)
        tiles.append(jnp.concatenate([value[deep:], none], 0))
    return jnp.concatenate(tiles, 1)


def coarse_conv(rows, w_ref, deep, *dims):
    size, chan = rows[0].shape
    y = dot(coarse_stack(rows, deep), w_ref[...], *dims)
    at = lax.rem(lax.broadcasted_iota(jnp.int32, (size, chan), 0), deep)
    left = jnp.where(at == 0, 0.0, pltpu.roll(y[:, :chan], 1, 0))
    right = jnp.where(at == deep - 1, 0.0, pltpu.roll(y[:, 2 * chan :], size - 1, 0))
    return y[:, chan : 2 * chan] + left + right


def prepare_kernel(
    volume, skip, w_first, w_second, w_down, w_coarse,
    v0, v1, skip_t, first_f, second_f, first_b, second_b, coarse_f, coarse_b, down_f, down_b,
):
    chan = w_first.shape[1]
    wide = w_coarse.shape[1]
    eye = (
        lax.broadcasted_iota(jnp.int32, (chan, chan), 0)
        == lax.broadcasted_iota(jnp.int32, (chan, chan), 1)
    ).astype(BF)
    for w, ahead, back in ((w_first, first_f, first_b), (w_second, second_f, second_b)):
        for kd in range(3):
            stack = jnp.concatenate([w[3 * j + kd] for j in range(9)], 0)
            ahead[kd * chan : (kd + 1) * chan, :] = dot(eye, stack, NT).astype(BF)
            back[kd * chan : (kd + 1) * chan, :] = jnp.concatenate(
                [w[26 - 3 * j - kd] for j in range(9)], 1
            )
    for j in range(9):
        for kd in range(3):
            rows = slice(j * wide, (j + 1) * wide)
            cols = slice(kd * wide, (kd + 1) * wide)
            coarse_f[rows, cols] = w_coarse[3 * j + kd]
            coarse_b[cols, rows] = w_coarse[26 - 3 * j - kd]
    for a in range(2):
        for b in range(2):
            for c in range(2):
                value = w_down[4 * a + 2 * b + c]
                at = 4 * a + 2 * c + b
                down_f[at * chan : (at + 1) * chan, :] = value
                at = 2 * a + b
                down_b[at * chan : (at + 1) * chan, c * wide : (c + 1) * wide] = value
    for r, out in enumerate((v0, v1)):
        out[...] = pltpu.einshape("cwd->wcd", volume[r])
        skip_t[r] = pltpu.einshape("cwd->wcd", skip[r])


def forward_kernel(
    flags, before, own0, own1, after, w_first, w_second, w_down,
    v0, v3, f0, f1, f2, f3, slope1, slope2, act_t, pooled, rows_scr,
):
    num, chan, deep = own0.shape
    half = deep // 2
    firsts = [f0, f1, f2, f3]
    rows_scr[0] = pltpu.einshape("cwd->wcd", before[0])
    v0[...] = pltpu.einshape("cwd->wcd", before[1])
    v3[...] = pltpu.einshape("cwd->wcd", after[0])
    rows_scr[1] = pltpu.einshape("cwd->wcd", after[1])
    sources = [rows_scr.at[0], v0, own0, own1, v3, rows_scr.at[1]]
    for r in range(4):
        for col in range(0, num, 2):
            for side, pre in enumerate(fine_pair(sources[r : r + 3], w_first, col)):
                sigma = sigmoid(pre)
                act = pre * sigma
                slope = sigma + act * (1.0 - sigma)
                if r == 0:
                    act = jnp.where(flags[0] > 0, act, 0.0)
                    slope = jnp.where(flags[0] > 0, slope, 0.0)
                if r == 3:
                    act = jnp.where(flags[1] > 0, act, 0.0)
                    slope = jnp.where(flags[1] > 0, slope, 0.0)
                firsts[r][col + side] = act.astype(BF)
                slope1[r, col + side] = slope
    at = lax.broadcasted_iota(jnp.int32, (deep, deep), 1)
    q = lax.broadcasted_iota(jnp.int32, (deep, deep), 0)
    perm = (at == 2 * lax.rem(q, half) + (q >= half).astype(jnp.int32)).astype(BF)
    for r in range(2):
        rows = firsts[r : r + 3]
        for col in range(0, num, 2):
            acts = []
            for side, pre in enumerate(fine_pair(rows, w_second, col)):
                sigma = sigmoid(pre)
                act = pre * sigma
                acts.append(act.astype(BF))
                slope2[r, col + side] = sigma + act * (1.0 - sigma)
            both = jnp.concatenate(acts, 0)
            wide = both.shape[0]
            turned = dot(perm, both, NT).astype(BF)
            at = slice(col // 2 * half, (col // 2 + 1) * half)
            for c in range(2):
                lanes = slice((2 * r + c) * wide, (2 * r + c + 1) * wide)
                act_t[at, lanes] = turned[c * half : (c + 1) * half]
    pooled[...] = dot(act_t[...], w_down[...]).astype(BF)


def coarse_delta_body(deep, before, own, after, grad, w, delta):
    pre = coarse_conv([before, own, after], w, deep)
    sigma = sigmoid(pre)
    slope = sigma + pre * sigma * (1.0 - sigma)
    delta[...] = (grad[...].astype(F32) * slope).astype(BF)


def coarse_grad_body(deep, flags, before, own, after, delta, mine, other, halves):
    size, chan = own.shape
    wide = delta[...].astype(F32)
    at = lax.rem(lax.broadcasted_iota(jnp.int32, (size, chan), 0), deep)
    up = jnp.where(at == deep - 1, 0.0, pltpu.roll(wide, size - 1, 0)).astype(BF)
    down = jnp.where(at == 0, 0.0, pltpu.roll(wide, 1, 0)).astype(BF)
    moved = jnp.concatenate([up, delta[...], down], 1)
    stack = coarse_stack([before, own, after], deep)
    acc = dot(stack, moved, TN).astype(BF)
    piece = chan // 2
    for k in range(3):
        for j in range(18):
            value = acc[j * piece : (j + 1) * piece, k * chan : (k + 1) * chan]
            put(halves, 18 * k + j, value)
    deal(halves, flags[2], mine, other)


def second_delta_body(deep, before, own, after, w, w_up, skip, slope, pg, delta):
    value = coarse_conv([before, own, after], w, deep, NT).astype(BF)
    pg[...] = value
    turned = value.T
    half = delta.shape[2]
    fine = delta.shape[3]
    row = lax.broadcasted_iota(jnp.int32, (fine, 4 * fine), 0)
    lane = lax.broadcasted_iota(jnp.int32, (fine, 4 * fine), 1)
    odd = (lax.rem(lane, 2 * fine) >= fine).astype(jnp.int32)
    same = (lane >= 2 * fine) == (row >= deep)
    spread = (same & (lax.rem(lane, fine) == 2 * lax.rem(row, deep) + odd)).astype(BF)
    for m in range(turned.shape[1] // (2 * deep)):
        up = dot(turned[:, 2 * m * deep : 2 * (m + 1) * deep], spread).astype(BF)
        parts = [
            jnp.concatenate([up[:, (2 * s + c) * fine : (2 * s + c + 1) * fine] for s in range(2)], 1)
            for c in range(2)
        ]
        back = dot(w_up[...], jnp.concatenate(parts, 0))
        for s in range(2):
            for a in range(2):
                for b in range(2):
                    rows = slice((2 * a + b) * half, (2 * a + b + 1) * half)
                    at = 4 * m + 2 * s + b
                    total = back[rows, s * fine : (s + 1) * fine] + skip[a, at].astype(F32)
                    delta[a, at] = (total * slope[a, at]).astype(BF)


def second_grad_body(flags, s0, s1, s2, s3, delta, act_t, pg, mine, other, a_scr, b_scr, halves):
    fine_grad([s0, s1, s2, s3], [delta.at[0], delta.at[1]], a_scr, b_scr, halves)
    down = dot(act_t[...], pg[...], TN).astype(BF)
    chan = s0.shape[1]
    for j in range(8):
        put(halves, 14 + j, down[j * chan : (j + 1) * chan])
    deal(halves, flags[2], mine, other)


def first_delta_body(
    flags, before, own, after, w, slope, s0, s1, s2, s3, delta, mine, other, a_scr, b_scr, halves
):
    rows = [ref.at[r] for ref in (before, own, after) for r in range(2)]
    for r in range(4):
        for col in range(0, delta.shape[1], 2):
            for side, value in enumerate(fine_pair(rows[r : r + 3], w, col)):
                delta[r, col + side] = (value * slope[r, col + side]).astype(BF)
    fine_grad([s0, s1, s2, s3], [delta.at[1], delta.at[2]], a_scr, b_scr, halves)
    deal(halves, flags[2], mine, other)


def input_grad_body(delta, w, out, scr):
    rows = [delta.at[r] for r in range(4)]
    for r in range(2):
        for col in range(0, delta.shape[1], 2):
            for side, value in enumerate(fine_pair(rows[r : r + 3], w, col)):
                scr[col + side] = value
        out[r] = pltpu.einshape("wcd->cwd", scr[...])


def added(*refs):
    values = [ref[...].astype(F32) for ref in refs]
    while len(values) > 1:
        half = len(values) // 2
        values = [values[t] + values[t + half] for t in range(half)]
    return values[0]


def split_body(flags, mine, got, keep, send):
    half = keep.shape[0]
    bit = flags[3]
    for side in range(2):
        rows = slice(side * half, (side + 1) * half)
        total = (mine[rows, :].astype(F32) + got[rows, :].astype(F32)).astype(BF)

        @pl.when(bit == side)
        def _():
            keep[...] = total

        @pl.when(bit != side)
        def _():
            send[...] = total


def add_body(*refs):
    refs[-1][...] = added(*refs[:-1]).astype(BF)


def order_body(flags, mine, got, out):
    bit = flags[3]
    out[bit] = mine[...]
    out[1 - bit] = got[...]


def block_of(halves, block, num):
    each = halves.shape[1] // num
    at = block % each * num
    return halves[block // each, at : at + num, :].astype(F32)


def fine_blocks(halves, out):
    chan = out.shape[1]
    for tap in range(9):
        value = block_of(halves, tap, chan)
        out[3 * tap] = value[:, :chan]
        out[3 * tap + 1] = value[:, chan:]
        value = block_of(halves, 9 + tap // 2, chan)
        out[3 * tap + 2] = value[:, chan:] if tap % 2 else value[:, :chan]


def gather_halves(flags, mine, got, halves):
    bit = flags[2]
    halves[bit] = mine[...].reshape(halves.shape[1:])
    halves[1 - bit] = got[...].reshape(halves.shape[1:])


def fine_unpack(flags, mine, got, out, halves):
    gather_halves(flags, mine, got, halves)
    fine_blocks(halves, out)


def middle_unpack(flags, mine, got, out, down, halves):
    gather_halves(flags, mine, got, halves)
    fine_blocks(halves, out)
    chan = out.shape[1]
    for a in range(2):
        for b in range(2):
            for c in range(2):
                down[4 * a + 2 * b + c] = block_of(halves, 14 + 4 * a + 2 * c + b, chan)


def coarse_unpack(flags, mine, got, out, halves):
    gather_halves(flags, mine, got, halves)
    piece = out.shape[1] // 2
    for k in range(3):
        for j in range(9):
            for s in range(2):
                out[3 * j + k, s * piece : (s + 1) * piece, :] = block_of(
                    halves, 18 * k + 2 * j + s, piece
                )


def reduced(flags, mine, other, unpack, outs):
    rows, lanes = mine.shape
    quarter = ((rows // 2, lanes), BF)
    got = swapped(other, 1)
    keep, send = call(split_body, [quarter] * 2, flags, mine, got, smem=1)
    (part,) = call(add_body, [quarter], keep, swapped(send, 2))
    parts = [part] + [shifted(part, 4, t) for t in range(1, lax.axis_size(AXIS) // 4)]
    (part,) = call(add_body, [quarter], *parts)
    (pair,) = call(
        order_body, [((2, rows // 2, lanes), BF)], flags, part, swapped(part, 2), smem=1
    )
    return call(
        unpack, outs, flags, pair, swapped(pair, 1), smem=1,
        scratch=(pltpu.VMEM((2, rows, lanes), BF),),
    )


def body(volume, skip_grad, coarse_grad, w_first, w_second, w_down, w_coarse):
    _, chan, num, deep = volume.shape
    wide = w_coarse.shape[-1]
    half = deep // 2
    size = num // 2 * half
    index = lax.axis_index(AXIS)
    flags = jnp.stack(
        [index, lax.axis_size(AXIS) - 1 - index, index % 2, (index // 2) % 2]
    ).astype(jnp.int32)

    fine = ((num, chan, deep), BF)
    coarse = ((size, wide), BF)
    two = ((2, num, chan, deep), BF)
    four = ((4, num, chan, deep), BF)

    before, after = from_before(volume), from_after(volume)
    v1, v2, skip, first_f, second_f, first_b, second_b, coarse_f, coarse_b, down_f, down_b = call(
        prepare_kernel,
        [fine, fine, two]
        + [((3 * chan, 9 * chan), BF)] * 4
        + [((9 * wide, 3 * wide), BF), ((3 * wide, 9 * wide), BF)]
        + [((8 * chan, wide), BF), ((4 * chan, 2 * wide), BF)],
        volume, skip_grad,
        w_first.reshape(27, chan, chan), w_second.reshape(27, chan, chan),
        w_down.reshape(8, chan, wide), w_coarse.reshape(27, wide, wide),
    )
    v0, v3, f0, f1, f2, f3, slope1, slope2, act_t, pooled = call(
        forward_kernel,
        [fine] * 6 + [(four[0], F32), (two[0], F32), ((size, 8 * chan), BF), coarse],
        flags, before, v1, v2, after, first_f, second_f, down_f,
        scratch=(pltpu.VMEM(*two),),
        smem=1,
    )
    rows = [from_before(pooled), pooled, from_after(pooled)]
    (delta,) = call(
        functools.partial(coarse_delta_body, half), [coarse],
        *rows, coarse_grad.reshape(size, wide), coarse_f,
    )
    delta_rows = [from_before(delta), delta, from_after(delta)]

    def dealt(blocks):
        return ((blocks // 2 * chan, 2 * chan), BF)

    def halves(blocks):
        return pltpu.VMEM((2, blocks // 2 * chan, 2 * chan), BF)

    coarse_sum = call(
        functools.partial(coarse_grad_body, half), [dealt(54)] * 2, flags, *rows, delta,
        scratch=(halves(54),), smem=1,
    )
    pg, second = call(
        functools.partial(second_delta_body, half), [coarse, two],
        *delta_rows, coarse_b, down_b, skip, slope2,
    )
    second_before, second_after = from_before(second), from_after(second)
    middle_sum = call(
        second_grad_body, [dealt(22)] * 2, flags, f0, f1, f2, f3, second, act_t, pg,
        scratch=fine_grad_scratch(num, chan, deep) + (halves(22),), smem=1,
    )
    first, *first_sum = call(
        first_delta_body, [four] + [dealt(14)] * 2,
        flags, second_before, second, second_after, second_b, slope1, v0, v1, v2, v3,
        scratch=fine_grad_scratch(num, chan, deep) + (halves(14),), smem=1,
    )
    (input_grad,) = call(
        input_grad_body, [((2, chan, num, deep), F32)], first, first_b,
        scratch=(pltpu.VMEM((num, chan, deep), F32),),
    )
    fine_out = ((27, chan, chan), F32)
    (coarse_out,) = reduced(flags, *coarse_sum, coarse_unpack, [((27, wide, wide), F32)])
    second_out, down_out = reduced(
        flags, *middle_sum, middle_unpack, [fine_out, ((8, chan, wide), F32)]
    )
    (first_out,) = reduced(flags, *first_sum, fine_unpack, [fine_out])
    return (
        input_grad,
        first_out.reshape(3, 3, 3, chan, chan),
        second_out.reshape(3, 3, 3, chan, chan),
        down_out.reshape(2, 2, 2, chan, wide),
        coarse_out.reshape(3, 3, 3, wide, wide),
    )


def solution(mesh):
    rows = P(("group", "ha"), None, None, None)
    kernels = P("group", None, None, None, None)
    return jax.shard_map(
        body,
        mesh=mesh,
        in_specs=(rows, rows, rows, P(), P(), P(), P()),
        out_specs=(rows, kernels, kernels, kernels, kernels),
        check_vma=False,
    )
```

time: 151 us -> 125 us (0.83)
  local copies, waits for them, and re-layouts: 22.4 us -> 5.01 us
  Pallas kernels: 21.6 us -> 36.2 us
  starting transfers between devices: 60.2 us -> 49 us
  waiting for transfers between devices: 39.9 us -> 33.4 us
  other arithmetic: 4.08 us -> 0.08 us
    pallas_call x8 -> x23, Pallas kernels: 21.6 us -> 36.2 us  [call(): pl.pallas_call(body, out_shape=[jax.ShapeDtypeStruct(s, d) for s, d in ou...]
    transpose x11 -> x0, local copies, waits for them, and re-layouts: 12.3 us -> none  [the longest x4 6.03 us: body(): w[::-1, ::-1, ::-1].transpose(2, 3, 0, 1, 4).reshape(3 * chan, 9 * chan)]
    ppermute x24 -> x21, starting transfers between devices: 33.2 us -> 23.6 us  [the longest x12 14.1 us: swapped(): return lax.ppermute(array, AXIS, [(i, i ^ stride) for i in range(size)])]
    ppermute x5 -> x4, waiting for transfers between devices: 9.25 us -> 1.42 us  [from_after(): return lax.ppermute(array, AXIS, neighbours(array)[1])]
    reshape x10 -> x0, local copies, waits for them, and re-layouts: 4.28 us -> none  [the longest x2 2.95 us: body(): w[::-1, ::-1, ::-1].transpose(2, 3, 0, 1, 4).reshape(3 * chan, 9 * chan)]
    ppermute x5 -> x4, waiting for transfers between devices: 2.67 us -> 6.06 us  [from_before(): return lax.ppermute(array, AXIS, neighbours(array)[0])]
    convert_element_type x18 -> x0, other arithmetic: 3.19 us -> none  [the longest x1 1.41 us: body(): coarse_sum.reshape(3, 3, 3, wide, wide).transpose(1, 2, 0, 3, 4).astype(F32)]
    ppermute x5 -> x4, starting transfers between devices: 11 us -> 8.14 us  [from_after(): return lax.ppermute(array, AXIS, neighbours(array)[1])]
  transfers between devices with their start and end apart: 34 -> 29, of which waited for: 15 -> 11; matrix products, arithmetic and copies ran while one was open for 16% -> 0% of each run, Pallas kernels for 4% -> 17%
where the time goes in v1:
time: 125 us
  starting transfers between devices  49 us (39%)
  Pallas kernels  36.2 us (29%)
  waiting for transfers between devices  33.4 us (27%)
  local copies, waits for them, and re-layouts  5.01 us (4%)
    pallas_call x23, Pallas kernels, call(): pl.pallas_call(body, out_shape=[jax.ShapeDtypeStruct(s, d) for s, d in ou...  36.2 us
    ppermute x4, starting transfers between devices, from_before(): return lax.ppermute(array, AXIS, neighbours(array)[0])  17.3 us
    ppermute x9, waiting for transfers between devices, shifted(): lax.ppermute(array, AXIS, [(i, (i + by * stride) % size) for i in range(s...  14.6 us
    ppermute x12, starting transfers between devices, swapped(): return lax.ppermute(array, AXIS, [(i, i ^ stride) for i in range(size)])  14.1 us
    ppermute x12, waiting for transfers between devices, swapped(): return lax.ppermute(array, AXIS, [(i, i ^ stride) for i in range(size)])  11.3 us
    ppermute x9, starting transfers between devices, shifted(): lax.ppermute(array, AXIS, [(i, (i + by * stride) % size) for i in range(s...  9.51 us
    ppermute x4, starting transfers between devices, from_after(): return lax.ppermute(array, AXIS, neighbours(array)[1])  8.14 us
    ppermute x4, waiting for transfers between devices, from_before(): return lax.ppermute(array, AXIS, neighbours(array)[0])  6.06 us
  transfers between devices with their start and end apart: 29, of which 11 were waited for; matrix products, arithmetic and copies ran while one was open for 0% of the time, Pallas kernels for 17%

profile of v1, /device:TPU:1, one launch (start us, length us, event | category | flops | bytes accessed | tf_op | source)
XLA Modules:
  0.0 124.7 jit_solution(2964687338311763717)
XLA Ops:
  0.6 4.5 %collective-permute-start = (bf16[2,64,16,128]{3,2,1,0:T(8,128)(2,1)}, bf16[2,64,16,128]{3,2,1,0:T(8,128)(2,1)S(1)}, u32[]{:S(2)}, u32[]{:S(2)}) collective-permute-start(bf16[2,64,16,128]{3,2,1,0:T(8,128)(2,1)} %volume.1), channel_id=1, source_target_pairs={{0,1},{1,2},{2,3},{3,4},{4,5},{5,6},{6,7},{7,8},{8,9},{9,10},{10,1... | collective-permute-start | bytes 1572872 | tf_op jit(solution)/shard_map/ppermute | solution.py:44
  5.2 1.9 %collective-permute-start.1 = (bf16[2,64,16,128]{3,2,1,0:T(8,128)(2,1)}, bf16[2,64,16,128]{3,2,1,0:T(8,128)(2,1)S(1)}, u32[]{:S(2)}, u32[]{:S(2)}) collective-permute-start(bf16[2,64,16,128]{3,2,1,0:T(8,128)(2,1)} %volume.1), channel_id=1, source_target_pairs={{1,0},{2,1},{3,2},{4,3},{5,4},{6,5},{7,6},{8,7},{9,8},{10,9},{11,1... | collective-permute-start | bytes 1572872 | tf_op jit(solution)/shard_map/ppermute | solution.py:48
  7.2 1.0 copy-done
  8.2 1.0 copy-done.1
  9.2 1.0 copy-done.2
  10.2 1.0 copy-done.3
  11.3 0.9 copy-done.4
  12.2 2.3 %shard_map.110 = (bf16[16,64,128]{2,1,0:T(8,128)(2,1)S(1)}, bf16[16,64,128]{2,1,0:T(8,128)(2,1)S(1)}, bf16[2,16,64,128]{3,2,1,0:T(8,128)(2,1)S(1)}, bf16[192,576...) custom-call(bf16[2,64,16,128]{3,2,1,0:T(8,128)(2,1)S(1)} %copy-done., ...), custom_call_target="tpu_custom_call" | custom-call | flops 1000000000 | bytes 2506752 | tf_op jit(solution)/shard_map/pallas_call | solution.py:25
  14.5 0.1 pad_add_fusion.flags
  14.6 2.6 %collective-permute-done.before = bf16[2,64,16,128]{3,2,1,0:T(8,128)(2,1)S(1)} collective-permute-done((bf16[2,64,16,128]{3,2,1,0:T(8,128)(2,1)}, bf16[2,64,16,128]{3,2,1,0:T(8,128)(2,1)S(1)}, u32[]{:S(2)}, u32[]{:S(2)}) %collective-permute-start) | collective-permute-done | bytes 524320 | tf_op jit(solution)/shard_map/ppermute | solution.py:44
  17.2 10.4 %shard_map.111 = (bf16[16,64,128]{2,1,0:T(8,128)(2,1)S(1)}, bf16[16,64,128]{2,1,0:T(8,128)(2,1)S(1)}, bf16[16,64,128]{2,1,0:T(8,128)(2,1)S(1)}, bf16[16,64,128]{...) custom-call(s32[4]{0:T(128)S(1)} %pad_add_fusion.flags, ...), custom_call_target="tpu_custom_call" | custom-call | flops 1000000000 | bytes 2146320 | tf_op jit(solution)/shard_map/pallas_call | solution.py:25
  27.6 1.9 %collective-permute-start.3 = (bf16[512,128]{1,0:T(8,128)(2,1)S(1)}, bf16[512,128]{1,0:T(8,128)(2,1)S(1)}, u32[]{:S(2)}, u32[]{:S(2)}) collective-permute-start(bf16[512,128]{1,0:T(8,128)(2,1)S(1)} %get-tuple-element.48.own), channel_id=1, source_target_pairs={{1,0},{2,1},{3,2},{4,3},{5,4},{6,5},{7,6},{8,7},{9,8},{10,9},{11,1... | collective-permute-start | bytes 393224 | tf_op jit(solution)/shard_map/ppermute | solution.py:48
  29.5 4.3 %collective-permute-start.2 = (bf16[512,128]{1,0:T(8,128)(2,1)S(1)}, bf16[512,128]{1,0:T(8,128)(2,1)S(1)}, u32[]{:S(2)}, u32[]{:S(2)}) collective-permute-start(bf16[512,128]{1,0:T(8,128)(2,1)S(1)} %get-tuple-element.48.own), channel_id=1, source_target_pairs={{0,1},{1,2},{2,3},{3,4},{4,5},{5,6},{6,7},{7,8},{8,9},{9,10},{10,1... | collective-permute-start | bytes 393224 | tf_op jit(solution)/shard_map/ppermute | solution.py:44
  33.8 0.7 collective-permute-done.3.after
  34.5 1.2 collective-permute-done.2.before
  35.7 0.9 shard_map.112.own.delta
  36.6 1.4 %shard_map.127 = (bf16[1728,128]{1,0:T(8,128)(2,1)S(1)}, bf16[1728,128]{1,0:T(8,128)(2,1)S(1)}) custom-call(s32[4]{0:T(128)S(1)} %pad_add_fusion.flags, bf16[512,128]{1,0:T(8,128)(2,1)S(1)} %collective-permute-done.2.before, bf16[512,128]{1,0:T(8,128)(2,1)S(1)} %get-tuple-element.48.own, bf16[512,128]{1,0:T(8,128)(2,1)S(1)} %collective-permute-done.3.after, ...), custom_call_target="tpu_custom_call" | custom-call | flops 1000000000 | bytes 524304 | tf_op jit(solution)/shard_map/pallas_call | solution.py:25
  38.0 0.1 collective-permute-start.22
  38.1 2.4 %collective-permute-start.5 = (bf16[512,128]{1,0:T(8,128)(2,1)S(1)}, bf16[512,128]{1,0:T(8,128)(2,1)S(1)}, u32[]{:S(2)}, u32[]{:S(2)}) collective-permute-start(bf16[512,128]{1,0:T(8,128)(2,1)S(1)} %shard_map.112.own.delta), channel_id=1, source_target_pairs={{1,0},{2,1},{3,2},{4,3},{5,4},{6,5},{7,6},{8,7},{9,8},{10,9},{11,1... | collective-permute-start | bytes 393224 | tf_op jit(solution)/shard_map/ppermute | solution.py:48
  40.5 3.9 %collective-permute-start.4 = (bf16[512,128]{1,0:T(8,128)(2,1)S(1)}, bf16[512,128]{1,0:T(8,128)(2,1)S(1)}, u32[]{:S(2)}, u32[]{:S(2)}) collective-permute-start(bf16[512,128]{1,0:T(8,128)(2,1)S(1)} %shard_map.112.own.delta), channel_id=1, source_target_pairs={{0,1},{1,2},{2,3},{3,4},{4,5},{5,6},{6,7},{7,8},{8,9},{9,10},{10,1... | collective-permute-start | bytes 393224 | tf_op jit(solution)/shard_map/ppermute | solution.py:44
  44.4 0.7 collective-permute-done.5.after
  45.1 2.2 %collective-permute-done.4.before = bf16[512,128]{1,0:T(8,128)(2,1)S(1)} collective-permute-done((bf16[512,128]{1,0:T(8,128)(2,1)S(1)}, bf16[512,128]{1,0:T(8,128)(2,1)S(1)}, u32[]{:S(2)}, u32[]{:S(2)}) %collective-permute-start.4) | collective-permute-done | bytes 131104 | tf_op jit(solution)/shard_map/ppermute | solution.py:44
  47.3 1.5 %shard_map.113 = (bf16[512,128]{1,0:T(8,128)(2,1)S(1)}, bf16[2,16,64,128]{3,2,1,0:T(8,128)(2,1)S(1)}) custom-call(bf16[512,128]{1,0:T(8,128)(2,1)S(1)} %collective-permute-done.4.before, bf16[512,128]{1,0:T(8,128)(2,1)S(1)} %shard_map.112.own.delta, bf16[512,128]{1,0:T(8,128)(2,1)S(1)} %collective-permute-done.5.after, ...), custom_call_target="tpu_custom_call" | custom-call | flops 1000000000 | bytes 2981888 | tf_op jit(solution)/shard_map/pallas_call | solution.py:25
  48.9 1.9 %collective-permute-start.7 = (bf16[2,16,64,128]{3,2,1,0:T(8,128)(2,1)S(1)}, bf16[2,16,64,128]{3,2,1,0:T(8,128)(2,1)S(1)}, u32[]{:S(2)}, u32[]{:S(2)}) collective-permute-start(bf16[2,16,64,128]{3,2,1,0:T(8,128)(2,1)S(1)} %get-tuple-element.54.own.delta), channel_id=1, source_target_pairs={{1,0},{2,1},{3,2},{4,3},{5,4},{6,5},{7,6},{8,7},{9,8},{10,9},{11,1... | collective-permute-start | bytes 1572872 | tf_op jit(solution)/shard_map/ppermute | solution.py:48
  50.8 4.6 %collective-permute-start.6 = (bf16[2,16,64,128]{3,2,1,0:T(8,128)(2,1)S(1)}, bf16[2,16,64,128]{3,2,1,0:T(8,128)(2,1)S(1)}, u32[]{:S(2)}, u32[]{:S(2)}) collective-permute-start(bf16[2,16,64,128]{3,2,1,0:T(8,128)(2,1)S(1)} %get-tuple-element.54.own.delta), channel_id=1, source_target_pairs={{0,1},{1,2},{2,3},{3,4},{4,5},{5,6},{6,7},{7,8},{8,9},{9,10},{10,1... | collective-permute-start | bytes 1572872 | tf_op jit(solution)/shard_map/ppermute | solution.py:44
  55.4 2.4 %shard_map.121 = (bf16[704,128]{1,0:T(8,128)(2,1)S(1)}, bf16[704,128]{1,0:T(8,128)(2,1)S(1)}) custom-call(s32[4]{0:T(128)S(1)} %pad_add_fusion.flags, bf16[16,64,128]{2,1,0:T(8,128)(2,1)S(1)} %get-tuple-element.65.s0, bf16[16,64,128]{2,1,0:T(8,128)(2,1)S(1)} %get-tuple-element.66.s1, bf16[16,64,128]{2,1,0:T(8,128)(2,1)S(1)} %get-tuple-element.67.s2, ...), custom_call_target="tpu_custom_call" | custom-call | flops 1000000000 | bytes 2228240 | tf_op jit(solution)/shard_map/pallas_call | solution.py:25
  57.8 0.1 collective-permute-start.15
  57.8 0.7 shard_map.128
  58.6 2.6 %collective-permute-start.23 = (bf16[864,128]{1,0:T(8,128)(2,1)S(1)}, bf16[864,128]{1,0:T(8,128)(2,1)S(1)}, u32[]{:S(2)}, u32[]{:S(2)}) collective-permute-start(bf16[864,128]{1,0:T(8,128)(2,1)S(1)} %get-tuple-element.80), channel_id=1, source_target_pairs={{0,2},{1,3},{2,0},{3,1},{4,6},{5,7},{6,4},{7,5},{8,10},{9,11},{10,... | collective-permute-start | bytes 663560 | tf_op jit(solution)/shard_map/ppermute | solution.py:53
  61.2 0.6 shard_map.122
  61.8 0.6 collective-permute-start.16
  62.5 9.6 %collective-permute-done.23.refs_1_ = bf16[864,128]{1,0:T(8,128)(2,1)S(1)} collective-permute-done((bf16[864,128]{1,0:T(8,128)(2,1)S(1)}, bf16[864,128]{1,0:T(8,128)(2,1)S(1)}, u32[]{:S(2)}, u32[]{:S(2)}) %collective-permute-start.23) | collective-permute-done | bytes 221216 | tf_op jit(solution)/shard_map/ppermute | solution.py:53
  72.2 1.5 %collective-permute-start.26 = (bf16[864,128]{1,0:T(8,128)(2,1)S(1)}, bf16[864,128]{1,0:T(8,128)(2,1)S(1)}, u32[]{:S(2)}, u32[]{:S(2)}) collective-permute-start(bf16[864,128]{1,0:T(8,128)(2,1)S(1)} %shard_map.129.refs_0_), channel_id=1, source_target_pairs={{0,12},{1,13},{2,14},{3,15},{4,0},{5,1},{6,2},{7,3},{8,4},{9,5},{1... | collective-permute-start | bytes 663560 | tf_op jit(solution)/shard_map/ppermute | solution.py:58
  73.6 1.9 %collective-permute-start.25 = (bf16[864,128]{1,0:T(8,128)(2,1)S(1)}, bf16[864,128]{1,0:T(8,128)(2,1)S(1)}, u32[]{:S(2)}, u32[]{:S(2)}) collective-permute-start(bf16[864,128]{1,0:T(8,128)(2,1)S(1)} %shard_map.129.refs_0_), channel_id=1, source_target_pairs={{0,8},{1,9},{2,10},{3,11},{4,12},{5,13},{6,14},{7,15},{8,0},{9,1},... | collective-permute-start | bytes 663560 | tf_op jit(solution)/shard_map/ppermute | solution.py:58
  75.5 1.3 %collective-permute-start.24 = (bf16[864,128]{1,0:T(8,128)(2,1)S(1)}, bf16[864,128]{1,0:T(8,128)(2,1)S(1)}, u32[]{:S(2)}, u32[]{:S(2)}) collective-permute-start(bf16[864,128]{1,0:T(8,128)(2,1)S(1)} %shard_map.129.refs_0_), channel_id=1, source_target_pairs={{0,4},{1,5},{2,6},{3,7},{4,8},{5,9},{6,10},{7,11},{8,12},{9,13},{1... | collective-permute-start | bytes 663560 | tf_op jit(solution)/shard_map/ppermute | solution.py:58
  76.8 5.8 %shard_map.114 = (bf16[4,16,64,128]{3,2,1,0:T(8,128)(2,1)S(1)}, bf16[448,128]{1,0:T(8,128)(2,1)S(1)}, bf16[448,128]{1,0:T(8,128)(2,1)S(1)}) custom-call(s32[4]{0:T(128)S(1)} %pad_add_fusion.flags, bf16[2,16,64,128]{3,2,1,0:T(8,128)(2,1)S(1)} %collective-permute-done.6.before, bf16[2,16,64,128]{3,2,1,0:T(8,128)(2,1)S(1)} %get-tuple-element.54.own.delta, ...), custom_call_target="tpu_custom_call" | custom-call | flops 1000000000 | bytes 4939792 | tf_op jit(solution)/shard_map/pallas_call | solution.py:25
  82.6 0.9 collective-permute-start.8
  83.5 2.1 %collective-permute-start.19 = (bf16[352,128]{1,0:T(8,128)(2,1)S(1)}, bf16[352,128]{1,0:T(8,128)(2,1)S(1)}, u32[]{:S(2)}, u32[]{:S(2)}) collective-permute-start(bf16[352,128]{1,0:T(8,128)(2,1)S(1)} %shard_map.123.refs_0_), channel_id=1, source_target_pairs={{0,12},{1,13},{2,14},{3,15},{4,0},{5,1},{6,2},{7,3},{8,4},{9,5},{1... | collective-permute-start | bytes 270344 | tf_op jit(solution)/shard_map/ppermute | solution.py:58
  85.7 0.8 collective-permute-start.18
  86.5 0.6 shard_map.116
  87.1 0.4 collective-permute-start.17
  87.5 11.8 %collective-permute-done.25.refs_2_ = bf16[864,128]{1,0:T(8,128)(2,1)S(1)} collective-permute-done((bf16[864,128]{1,0:T(8,128)(2,1)S(1)}, bf16[864,128]{1,0:T(8,128)(2,1)S(1)}, u32[]{:S(2)}, u32[]{:S(2)}) %collective-permute-start.25) | collective-permute-done | bytes 221216 | tf_op jit(solution)/shard_map/ppermute | solution.py:58
  99.2 1.8 %collective-permute-start.9 = (bf16[224,128]{1,0:T(8,128)(2,1)S(1)}, bf16[224,128]{1,0:T(8,128)(2,1)S(1)}, u32[]{:S(2)}, u32[]{:S(2)}) collective-permute-start(bf16[224,128]{1,0:T(8,128)(2,1)S(1)} %get-tuple-element.64), channel_id=1, source_target_pairs={{0,2},{1,3},{2,0},{3,1},{4,6},{5,7},{6,4},{7,5},{8,10},{9,11},{10,... | collective-permute-start | bytes 172040 | tf_op jit(solution)/shard_map/ppermute | solution.py:53
  101.1 0.1 shard_map.130.mine
  101.2 0.1 collective-permute-start.27
  101.3 1.7 %collective-permute-done.9.refs_1_ = bf16[224,128]{1,0:T(8,128)(2,1)S(1)} collective-permute-done((bf16[224,128]{1,0:T(8,128)(2,1)S(1)}, bf16[224,128]{1,0:T(8,128)(2,1)S(1)}, u32[]{:S(2)}, u32[]{:S(2)}) %collective-permute-start.9) | collective-permute-done | bytes 57376 | tf_op jit(solution)/shard_map/ppermute | solution.py:53
  102.9 0.1 collective-permute-start.12
  103.0 0.1 collective-permute-start.11
  103.1 1.4 %collective-permute-start.10 = (bf16[224,128]{1,0:T(8,128)(2,1)S(1)}, bf16[224,128]{1,0:T(8,128)(2,1)S(1)}, u32[]{:S(2)}, u32[]{:S(2)}) collective-permute-start(bf16[224,128]{1,0:T(8,128)(2,1)S(1)} %shard_map.117.refs_0_), channel_id=1, source_target_pairs={{0,4},{1,5},{2,6},{3,7},{4,8},{5,9},{6,10},{7,11},{8,12},{9,13},{1... | collective-permute-start | bytes 172040 | tf_op jit(solution)/shard_map/ppermute | solution.py:58
  104.6 1.4 %collective-permute-start.20 = (bf16[352,128]{1,0:T(8,128)(2,1)S(1)}, bf16[352,128]{1,0:T(8,128)(2,1)S(1)}, u32[]{:S(2)}, u32[]{:S(2)}) collective-permute-start(bf16[352,128]{1,0:T(8,128)(2,1)S(1)} %shard_map.124.mine), channel_id=1, source_target_pairs={{0,2},{1,3},{2,0},{3,1},{4,6},{5,7},{6,4},{7,5},{8,10},{9,11},{10,... | collective-permute-start | bytes 270344 | tf_op jit(solution)/shard_map/ppermute | solution.py:53
  106.0 0.4 collective-permute-done.12.refs_3_
  106.3 0.7 collective-permute-done.11.refs_2_
  107.0 1.8 %collective-permute-done.10.refs_1_ = bf16[224,128]{1,0:T(8,128)(2,1)S(1)} collective-permute-done((bf16[224,128]{1,0:T(8,128)(2,1)S(1)}, bf16[224,128]{1,0:T(8,128)(2,1)S(1)}, u32[]{:S(2)}, u32[]{:S(2)}) %collective-permute-start.10) | collective-permute-done | bytes 57376 | tf_op jit(solution)/shard_map/ppermute | solution.py:58
  108.9 1.6 %collective-permute-start.13 = (bf16[224,128]{1,0:T(8,128)(2,1)S(1)}, bf16[224,128]{1,0:T(8,128)(2,1)S(1)}, u32[]{:S(2)}, u32[]{:S(2)}) collective-permute-start(bf16[224,128]{1,0:T(8,128)(2,1)S(1)} %shard_map.118.mine), channel_id=1, source_target_pairs={{0,2},{1,3},{2,0},{3,1},{4,6},{5,7},{6,4},{7,5},{8,10},{9,11},{10,... | collective-permute-start | bytes 172040 | tf_op jit(solution)/shard_map/ppermute | solution.py:53
  110.5 0.6 shard_map.131.mine
  111.1 2.2 %collective-permute-start.28 = (bf16[2,864,128]{2,1,0:T(8,128)(2,1)S(1)}, bf16[2,864,128]{2,1,0:T(8,128)(2,1)S(1)}, u32[]{:S(2)}, u32[]{:S(2)}) collective-permute-start(bf16[2,864,128]{2,1,0:T(8,128)(2,1)S(1)} %shard_map.131.mine), channel_id=1, source_target_pairs={{0,1},{1,0},{2,3},{3,2},{4,5},{5,4},{6,7},{7,6},{8,9},{9,8},{10,11... | collective-permute-start | bytes 1327112 | tf_op jit(solution)/shard_map/ppermute | solution.py:53
  113.3 0.6 shard_map.125.mine
  113.8 0.1 collective-permute-start.21
  113.9 0.6 shard_map.119.mine
  114.5 2.6 %collective-permute-start.14 = (bf16[2,224,128]{2,1,0:T(8,128)(2,1)S(1)}, bf16[2,224,128]{2,1,0:T(8,128)(2,1)S(1)}, u32[]{:S(2)}, u32[]{:S(2)}) collective-permute-start(bf16[2,224,128]{2,1,0:T(8,128)(2,1)S(1)} %shard_map.119.mine), channel_id=1, source_target_pairs={{0,1},{1,0},{2,3},{3,2},{4,5},{5,4},{6,7},{7,6},{8,9},{9,8},{10,11... | collective-permute-start | bytes 344072 | tf_op jit(solution)/shard_map/ppermute | solution.py:53
  117.0 2.5 %shard_map.115 = f32[2,64,16,128]{3,2,1,0:T(8,128)} custom-call(bf16[4,16,64,128]{3,2,1,0:T(8,128)(2,1)S(1)} %get-tuple-element.59.delta, bf16[192,576]{1,0:T(8,128)(2,1)S(1)} %get-tuple-element.60.w), custom_call_target="tpu_custom_call" | custom-call | flops 1000000000 | bytes 1269760 | tf_op jit(solution)/shard_map/pallas_call | solution.py:25
  119.5 1.6 %shard_map.126 = (f32[27,64,64]{2,1,0:T(8,128)}, f32[8,64,128]{2,1,0:T(8,128)}) custom-call(s32[4]{0:T(128)S(1)} %pad_add_fusion.flags, bf16[2,352,128]{2,1,0:T(8,128)(2,1)S(1)} %shard_map.125.mine, bf16[2,352,128]{2,1,0:T(8,128)(2,1)S(1)} %collective-permute-done.21.got), custom_call_target="tpu_custom_call" | custom-call | flops 1000000000 | bytes 360464 | tf_op jit(solution)/shard_map/pallas_call | solution.py:25
  121.2 1.6 %shard_map.120 = f32[27,64,64]{2,1,0:T(8,128)} custom-call(s32[4]{0:T(128)S(1)} %pad_add_fusion.flags, bf16[2,224,128]{2,1,0:T(8,128)(2,1)S(1)} %shard_map.119.mine, bf16[2,224,128]{2,1,0:T(8,128)(2,1)S(1)} %collective-permute-done.14.got), custom_call_target="tpu_custom_call" | custom-call | flops 1000000000 | bytes 229392 | tf_op jit(solution)/shard_map/pallas_call | solution.py:25
  122.8 1.9 %shard_map.132 = f32[27,128,128]{2,1,0:T(8,128)} custom-call(s32[4]{0:T(128)S(1)} %pad_add_fusion.flags, bf16[2,864,128]{2,1,0:T(8,128)(2,1)S(1)} %shard_map.131.mine, bf16[2,864,128]{2,1,0:T(8,128)(2,1)S(1)} %collective-permute-done.28.got), custom_call_target="tpu_custom_call" | custom-call | flops 1000000000 | bytes 884752 | tf_op jit(solution)/shard_map/pallas_call | solution.py:25
  (30 shorter events, 0.2 us)
Async XLA Ops:
  0.6 16.6 %collective-permute-start = (bf16[2,64,16,128]{3,2,1,0:T(8,128)(2,1)}, bf16[2,64,16,128]{3,2,1,0:T(8,128)(2,1)S(1)}, u32[]{:S(2)}, u32[]{:S(2)}) collective-permute-start(bf16[2,64,16,128]{3,2,1,0:T(8,128)(2,1)} %volume.1), channel_id=1, source_target_pairs={{0,1},{1,2},{2,3},{3,4},{4,5},{5,6},{6,7},{7,8},{8,9},{9,10},{10,1... | collective-permute-start | bytes 1572872 | tf_op jit(solution)/shard_map/ppermute | solution.py:44
  5.2 12.0 %collective-permute-start.1 = (bf16[2,64,16,128]{3,2,1,0:T(8,128)(2,1)}, bf16[2,64,16,128]{3,2,1,0:T(8,128)(2,1)S(1)}, u32[]{:S(2)}, u32[]{:S(2)}) collective-permute-start(bf16[2,64,16,128]{3,2,1,0:T(8,128)(2,1)} %volume.1), channel_id=1, source_target_pairs={{1,0},{2,1},{3,2},{4,3},{5,4},{6,5},{7,6},{8,7},{9,8},{10,9},{11,1... | collective-permute-start | bytes 1572872 | tf_op jit(solution)/shard_map/ppermute | solution.py:48
  7.1 1.0 copy-start
  8.2 1.0 copy-start.1
  9.2 1.0 copy-start.2
  10.2 1.0 copy-start.3
  11.3 0.9 copy-start.4
  14.5 21.2 %copy-start.5 = (bf16[1,8,64,128]{3,2,1,0:T(8,128)(2,1)S(1)}, bf16[1,8,64,128]{3,2,1,0:T(8,128)(2,1)}, u32[]{:S(2)}) copy-start(bf16[1,8,64,128]{3,2,1,0:T(8,128)(2,1)} %param.9) | copy-start | bytes 393220
  27.6 6.9 %collective-permute-start.3 = (bf16[512,128]{1,0:T(8,128)(2,1)S(1)}, bf16[512,128]{1,0:T(8,128)(2,1)S(1)}, u32[]{:S(2)}, u32[]{:S(2)}) collective-permute-start(bf16[512,128]{1,0:T(8,128)(2,1)S(1)} %get-tuple-element.48.own), channel_id=1, source_target_pairs={{1,0},{2,1},{3,2},{4,3},{5,4},{6,5},{7,6},{8,7},{9,8},{10,9},{11,1... | collective-permute-start | bytes 393224 | tf_op jit(solution)/shard_map/ppermute | solution.py:48
  29.5 6.2 %collective-permute-start.2 = (bf16[512,128]{1,0:T(8,128)(2,1)S(1)}, bf16[512,128]{1,0:T(8,128)(2,1)S(1)}, u32[]{:S(2)}, u32[]{:S(2)}) collective-permute-start(bf16[512,128]{1,0:T(8,128)(2,1)S(1)} %get-tuple-element.48.own), channel_id=1, source_target_pairs={{0,1},{1,2},{2,3},{3,4},{4,5},{5,6},{6,7},{7,8},{8,9},{9,10},{10,1... | collective-permute-start | bytes 393224 | tf_op jit(solution)/shard_map/ppermute | solution.py:44
  38.0 19.8 %collective-permute-start.22 = (bf16[1728,128]{1,0:T(8,128)(2,1)S(1)}, bf16[1728,128]{1,0:T(8,128)(2,1)S(1)}, u32[]{:S(2)}, u32[]{:S(2)}) collective-permute-start(bf16[1728,128]{1,0:T(8,128)(2,1)S(1)} %get-tuple-element.78), channel_id=1, source_target_pairs={{0,1},{1,0},{2,3},{3,2},{4,5},{5,4},{6,7},{7,6},{8,9},{9,8},{10,11... | collective-permute-start | bytes 1327112 | tf_op jit(solution)/shard_map/ppermute | solution.py:53
  38.1 7.0 %collective-permute-start.5 = (bf16[512,128]{1,0:T(8,128)(2,1)S(1)}, bf16[512,128]{1,0:T(8,128)(2,1)S(1)}, u32[]{:S(2)}, u32[]{:S(2)}) collective-permute-start(bf16[512,128]{1,0:T(8,128)(2,1)S(1)} %shard_map.112.own.delta), channel_id=1, source_target_pairs={{1,0},{2,1},{3,2},{4,3},{5,4},{6,5},{7,6},{8,7},{9,8},{10,9},{11,1... | collective-permute-start | bytes 393224 | tf_op jit(solution)/shard_map/ppermute | solution.py:48
  40.5 6.8 %collective-permute-start.4 = (bf16[512,128]{1,0:T(8,128)(2,1)S(1)}, bf16[512,128]{1,0:T(8,128)(2,1)S(1)}, u32[]{:S(2)}, u32[]{:S(2)}) collective-permute-start(bf16[512,128]{1,0:T(8,128)(2,1)S(1)} %shard_map.112.own.delta), channel_id=1, source_target_pairs={{0,1},{1,2},{2,3},{3,4},{4,5},{5,6},{6,7},{7,8},{8,9},{9,10},{10,1... | collective-permute-start | bytes 393224 | tf_op jit(solution)/shard_map/ppermute | solution.py:44
  48.9 26.6 %collective-permute-start.7 = (bf16[2,16,64,128]{3,2,1,0:T(8,128)(2,1)S(1)}, bf16[2,16,64,128]{3,2,1,0:T(8,128)(2,1)S(1)}, u32[]{:S(2)}, u32[]{:S(2)}) collective-permute-start(bf16[2,16,64,128]{3,2,1,0:T(8,128)(2,1)S(1)} %get-tuple-element.54.own.delta), channel_id=1, source_target_pairs={{1,0},{2,1},{3,2},{4,3},{5,4},{6,5},{7,6},{8,7},{9,8},{10,9},{11,1... | collective-permute-start | bytes 1572872 | tf_op jit(solution)/shard_map/ppermute | solution.py:48
  50.8 26.0 %collective-permute-start.6 = (bf16[2,16,64,128]{3,2,1,0:T(8,128)(2,1)S(1)}, bf16[2,16,64,128]{3,2,1,0:T(8,128)(2,1)S(1)}, u32[]{:S(2)}, u32[]{:S(2)}) collective-permute-start(bf16[2,16,64,128]{3,2,1,0:T(8,128)(2,1)S(1)} %get-tuple-element.54.own.delta), channel_id=1, source_target_pairs={{0,1},{1,2},{2,3},{3,4},{4,5},{5,6},{6,7},{7,8},{8,9},{9,10},{10,1... | collective-permute-start | bytes 1572872 | tf_op jit(solution)/shard_map/ppermute | solution.py:44
  57.8 3.5 %collective-permute-start.15 = (bf16[704,128]{1,0:T(8,128)(2,1)S(1)}, bf16[704,128]{1,0:T(8,128)(2,1)S(1)}, u32[]{:S(2)}, u32[]{:S(2)}) collective-permute-start(bf16[704,128]{1,0:T(8,128)(2,1)S(1)} %get-tuple-element.72), channel_id=1, source_target_pairs={{0,1},{1,0},{2,3},{3,2},{4,5},{5,4},{6,7},{7,6},{8,9},{9,8},{10,11... | collective-permute-start | bytes 540680 | tf_op jit(solution)/shard_map/ppermute | solution.py:53
  58.6 13.5 %collective-permute-start.23 = (bf16[864,128]{1,0:T(8,128)(2,1)S(1)}, bf16[864,128]{1,0:T(8,128)(2,1)S(1)}, u32[]{:S(2)}, u32[]{:S(2)}) collective-permute-start(bf16[864,128]{1,0:T(8,128)(2,1)S(1)} %get-tuple-element.80), channel_id=1, source_target_pairs={{0,2},{1,3},{2,0},{3,1},{4,6},{5,7},{6,4},{7,5},{8,10},{9,11},{10,... | collective-permute-start | bytes 663560 | tf_op jit(solution)/shard_map/ppermute | solution.py:53
  61.8 21.7 %collective-permute-start.16 = (bf16[352,128]{1,0:T(8,128)(2,1)S(1)}, bf16[352,128]{1,0:T(8,128)(2,1)S(1)}, u32[]{:S(2)}, u32[]{:S(2)}) collective-permute-start(bf16[352,128]{1,0:T(8,128)(2,1)S(1)} %get-tuple-element.74), channel_id=1, source_target_pairs={{0,2},{1,3},{2,0},{3,1},{4,6},{5,7},{6,4},{7,5},{8,10},{9,11},{10,... | collective-permute-start | bytes 270344 | tf_op jit(solution)/shard_map/ppermute | solution.py:53
  72.2 14.9 %collective-permute-start.26 = (bf16[864,128]{1,0:T(8,128)(2,1)S(1)}, bf16[864,128]{1,0:T(8,128)(2,1)S(1)}, u32[]{:S(2)}, u32[]{:S(2)}) collective-permute-start(bf16[864,128]{1,0:T(8,128)(2,1)S(1)} %shard_map.129.refs_0_), channel_id=1, source_target_pairs={{0,12},{1,13},{2,14},{3,15},{4,0},{5,1},{6,2},{7,3},{8,4},{9,5},{1... | collective-permute-start | bytes 663560 | tf_op jit(solution)/shard_map/ppermute | solution.py:58
  73.6 25.6 %collective-permute-start.25 = (bf16[864,128]{1,0:T(8,128)(2,1)S(1)}, bf16[864,128]{1,0:T(8,128)(2,1)S(1)}, u32[]{:S(2)}, u32[]{:S(2)}) collective-permute-start(bf16[864,128]{1,0:T(8,128)(2,1)S(1)} %shard_map.129.refs_0_), channel_id=1, source_target_pairs={{0,8},{1,9},{2,10},{3,11},{4,12},{5,13},{6,14},{7,15},{8,0},{9,1},... | collective-permute-start | bytes 663560 | tf_op jit(solution)/shard_map/ppermute | solution.py:58
  75.5 25.6 %collective-permute-start.24 = (bf16[864,128]{1,0:T(8,128)(2,1)S(1)}, bf16[864,128]{1,0:T(8,128)(2,1)S(1)}, u32[]{:S(2)}, u32[]{:S(2)}) collective-permute-start(bf16[864,128]{1,0:T(8,128)(2,1)S(1)} %shard_map.129.refs_0_), channel_id=1, source_target_pairs={{0,4},{1,5},{2,6},{3,7},{4,8},{5,9},{6,10},{7,11},{8,12},{9,13},{1... | collective-permute-start | bytes 663560 | tf_op jit(solution)/shard_map/ppermute | solution.py:58
  82.6 3.1 %collective-permute-start.8 = (bf16[448,128]{1,0:T(8,128)(2,1)S(1)}, bf16[448,128]{1,0:T(8,128)(2,1)S(1)}, u32[]{:S(2)}, u32[]{:S(2)}) collective-permute-start(bf16[448,128]{1,0:T(8,128)(2,1)S(1)} %get-tuple-element.62), channel_id=1, source_target_pairs={{0,1},{1,0},{2,3},{3,2},{4,5},{5,4},{6,7},{7,6},{8,9},{9,8},{10,11... | collective-permute-start | bytes 344072 | tf_op jit(solution)/shard_map/ppermute | solution.py:53
  83.5 19.5 %collective-permute-start.19 = (bf16[352,128]{1,0:T(8,128)(2,1)S(1)}, bf16[352,128]{1,0:T(8,128)(2,1)S(1)}, u32[]{:S(2)}, u32[]{:S(2)}) collective-permute-start(bf16[352,128]{1,0:T(8,128)(2,1)S(1)} %shard_map.123.refs_0_), channel_id=1, source_target_pairs={{0,12},{1,13},{2,14},{3,15},{4,0},{5,1},{6,2},{7,3},{8,4},{9,5},{1... | collective-permute-start | bytes 270344 | tf_op jit(solution)/shard_map/ppermute | solution.py:58
  85.7 17.4 %collective-permute-start.18 = (bf16[352,128]{1,0:T(8,128)(2,1)S(1)}, bf16[352,128]{1,0:T(8,128)(2,1)S(1)}, u32[]{:S(2)}, u32[]{:S(2)}) collective-permute-start(bf16[352,128]{1,0:T(8,128)(2,1)S(1)} %shard_map.123.refs_0_), channel_id=1, source_target_pairs={{0,8},{1,9},{2,10},{3,11},{4,12},{5,13},{6,14},{7,15},{8,0},{9,1},... | collective-permute-start | bytes 270344 | tf_op jit(solution)/shard_map/ppermute | solution.py:58
  87.1 17.4 %collective-permute-start.17 = (bf16[352,128]{1,0:T(8,128)(2,1)S(1)}, bf16[352,128]{1,0:T(8,128)(2,1)S(1)}, u32[]{:S(2)}, u32[]{:S(2)}) collective-permute-start(bf16[352,128]{1,0:T(8,128)(2,1)S(1)} %shard_map.123.refs_0_), channel_id=1, source_target_pairs={{0,4},{1,5},{2,6},{3,7},{4,8},{5,9},{6,10},{7,11},{8,12},{9,13},{1... | collective-permute-start | bytes 270344 | tf_op jit(solution)/shard_map/ppermute | solution.py:58
  99.2 3.7 %collective-permute-start.9 = (bf16[224,128]{1,0:T(8,128)(2,1)S(1)}, bf16[224,128]{1,0:T(8,128)(2,1)S(1)}, u32[]{:S(2)}, u32[]{:S(2)}) collective-permute-start(bf16[224,128]{1,0:T(8,128)(2,1)S(1)} %get-tuple-element.64), channel_id=1, source_target_pairs={{0,2},{1,3},{2,0},{3,1},{4,6},{5,7},{6,4},{7,5},{8,10},{9,11},{10,... | collective-permute-start | bytes 172040 | tf_op jit(solution)/shard_map/ppermute | solution.py:53
  101.2 9.3 %collective-permute-start.27 = (bf16[864,128]{1,0:T(8,128)(2,1)S(1)}, bf16[864,128]{1,0:T(8,128)(2,1)S(1)}, u32[]{:S(2)}, u32[]{:S(2)}) collective-permute-start(bf16[864,128]{1,0:T(8,128)(2,1)S(1)} %shard_map.130.mine), channel_id=1, source_target_pairs={{0,2},{1,3},{2,0},{3,1},{4,6},{5,7},{6,4},{7,5},{8,10},{9,11},{10,... | collective-permute-start | bytes 663560 | tf_op jit(solution)/shard_map/ppermute | solution.py:53
  102.9 3.4 %collective-permute-start.12 = (bf16[224,128]{1,0:T(8,128)(2,1)S(1)}, bf16[224,128]{1,0:T(8,128)(2,1)S(1)}, u32[]{:S(2)}, u32[]{:S(2)}) collective-permute-start(bf16[224,128]{1,0:T(8,128)(2,1)S(1)} %shard_map.117.refs_0_), channel_id=1, source_target_pairs={{0,12},{1,13},{2,14},{3,15},{4,0},{5,1},{6,2},{7,3},{8,4},{9,5},{1... | collective-permute-start | bytes 172040 | tf_op jit(solution)/shard_map/ppermute | solution.py:58
  103.0 4.0 %collective-permute-start.11 = (bf16[224,128]{1,0:T(8,128)(2,1)S(1)}, bf16[224,128]{1,0:T(8,128)(2,1)S(1)}, u32[]{:S(2)}, u32[]{:S(2)}) collective-permute-start(bf16[224,128]{1,0:T(8,128)(2,1)S(1)} %shard_map.117.refs_0_), channel_id=1, source_target_pairs={{0,8},{1,9},{2,10},{3,11},{4,12},{5,13},{6,14},{7,15},{8,0},{9,1},... | collective-permute-start | bytes 172040 | tf_op jit(solution)/shard_map/ppermute | solution.py:58
  103.1 5.7 %collective-permute-start.10 = (bf16[224,128]{1,0:T(8,128)(2,1)S(1)}, bf16[224,128]{1,0:T(8,128)(2,1)S(1)}, u32[]{:S(2)}, u32[]{:S(2)}) collective-permute-start(bf16[224,128]{1,0:T(8,128)(2,1)S(1)} %shard_map.117.refs_0_), channel_id=1, source_target_pairs={{0,4},{1,5},{2,6},{3,7},{4,8},{5,9},{6,10},{7,11},{8,12},{9,13},{1... | collective-permute-start | bytes 172040 | tf_op jit(solution)/shard_map/ppermute | solution.py:58
  104.6 8.7 %collective-permute-start.20 = (bf16[352,128]{1,0:T(8,128)(2,1)S(1)}, bf16[352,128]{1,0:T(8,128)(2,1)S(1)}, u32[]{:S(2)}, u32[]{:S(2)}) collective-permute-start(bf16[352,128]{1,0:T(8,128)(2,1)S(1)} %shard_map.124.mine), channel_id=1, source_target_pairs={{0,2},{1,3},{2,0},{3,1},{4,6},{5,7},{6,4},{7,5},{8,10},{9,11},{10,... | collective-permute-start | bytes 270344 | tf_op jit(solution)/shard_map/ppermute | solution.py:53
  108.9 5.0 %collective-permute-start.13 = (bf16[224,128]{1,0:T(8,128)(2,1)S(1)}, bf16[224,128]{1,0:T(8,128)(2,1)S(1)}, u32[]{:S(2)}, u32[]{:S(2)}) collective-permute-start(bf16[224,128]{1,0:T(8,128)(2,1)S(1)} %shard_map.118.mine), channel_id=1, source_target_pairs={{0,2},{1,3},{2,0},{3,1},{4,6},{5,7},{6,4},{7,5},{8,10},{9,11},{10,... | collective-permute-start | bytes 172040 | tf_op jit(solution)/shard_map/ppermute | solution.py:53
  111.1 11.7 %collective-permute-start.28 = (bf16[2,864,128]{2,1,0:T(8,128)(2,1)S(1)}, bf16[2,864,128]{2,1,0:T(8,128)(2,1)S(1)}, u32[]{:S(2)}, u32[]{:S(2)}) collective-permute-start(bf16[2,864,128]{2,1,0:T(8,128)(2,1)S(1)} %shard_map.131.mine), channel_id=1, source_target_pairs={{0,1},{1,0},{2,3},{3,2},{4,5},{5,4},{6,7},{7,6},{8,9},{9,8},{10,11... | collective-permute-start | bytes 1327112 | tf_op jit(solution)/shard_map/ppermute | solution.py:53
  113.8 5.7 %collective-permute-start.21 = (bf16[2,352,128]{2,1,0:T(8,128)(2,1)S(1)}, bf16[2,352,128]{2,1,0:T(8,128)(2,1)S(1)}, u32[]{:S(2)}, u32[]{:S(2)}) collective-permute-start(bf16[2,352,128]{2,1,0:T(8,128)(2,1)S(1)} %shard_map.125.mine), channel_id=1, source_target_pairs={{0,1},{1,0},{2,3},{3,2},{4,5},{5,4},{6,7},{7,6},{8,9},{9,8},{10,11... | collective-permute-start | bytes 540680 | tf_op jit(solution)/shard_map/ppermute | solution.py:53
  114.5 6.7 %collective-permute-start.14 = (bf16[2,224,128]{2,1,0:T(8,128)(2,1)S(1)}, bf16[2,224,128]{2,1,0:T(8,128)(2,1)S(1)}, u32[]{:S(2)}, u32[]{:S(2)}) collective-permute-start(bf16[2,224,128]{2,1,0:T(8,128)(2,1)S(1)} %shard_map.119.mine), channel_id=1, source_target_pairs={{0,1},{1,0},{2,3},{3,2},{4,5},{5,4},{6,7},{7,6},{8,9},{9,8},{10,11... | collective-permute-start | bytes 344072 | tf_op jit(solution)/shard_map/ppermute | solution.py:53

commit v2 on v1

--- a/solution.py
+++ b/solution.py
@@ -12,16 +12,16 @@
 NT = (((1,), (1,)), ((), ()))
 TN = (((0,), (0,)), ((), ()))
 AXIS = "ha"
+COST = 10**9
 
 
 def dot(a, b, dims=(((1,), (0,)), ((), ()))):
     return lax.dot_general(a, b, dims, preferred_element_type=F32)
 
 
-def call(body, outs, *args, scratch=(), flops=10**9, smem=0):
+def call(body, outs, *args, scratch=(), smem=0):
     in_specs = [pl.BlockSpec(memory_space=pltpu.SMEM)] * smem
     in_specs += [pl.BlockSpec(memory_space=pltpu.VMEM)] * (len(args) - smem)
-    size = sum(a.size * a.dtype.itemsize for a in args)
     return pl.pallas_call(
         body,
         out_shape=[jax.ShapeDtypeStruct(s, d) for s, d in outs],
@@ -29,7 +29,7 @@
         out_specs=[pl.BlockSpec(memory_space=pltpu.VMEM)] * len(outs),
         scratch_shapes=list(scratch),
         compiler_params=pltpu.CompilerParams(vmem_limit_bytes=48 * 2**20),
-        cost_estimate=pl.CostEstimate(flops=flops, bytes_accessed=size, transcendentals=0),
+        cost_estimate=pl.CostEstimate(flops=COST, bytes_accessed=2**20, transcendentals=0),
     )(*args)
 
 
@@ -260,6 +260,8 @@
         for j in range(18):
             value = acc[j * piece : (j + 1) * piece, k * chan : (k + 1) * chan]
             put(halves, 18 * k + j, value)
+    for j in range(54, 2 * halves.shape[1] // piece):
+        put(halves, j, jnp.zeros((piece, chan), BF))
     deal(halves, flags[2], mine, other)
 
 
@@ -299,22 +301,28 @@
     deal(halves, flags[2], mine, other)
 
 
+def back_row(rows, w, slope, at, out):
+    for col in range(0, out.shape[0], 2):
+        for side, value in enumerate(fine_pair(rows, w, col)):
+            out[col + side] = (value * slope[at, col + side]).astype(BF)
+
+
 def first_delta_body(
-    flags, before, own, after, w, slope, s0, s1, s2, s3, delta, mine, other, a_scr, b_scr, halves
+    flags, before, own, after, w, slope, s0, s1, s2, s3, e1, e2, mine, other, a_scr, b_scr, halves
 ):
-    rows = [ref.at[r] for ref in (before, own, after) for r in range(2)]
-    for r in range(4):
-        for col in range(0, delta.shape[1], 2):
-            for side, value in enumerate(fine_pair(rows[r : r + 3], w, col)):
-                delta[r, col + side] = (value * slope[r, col + side]).astype(BF)
-    fine_grad([s0, s1, s2, s3], [delta.at[1], delta.at[2]], a_scr, b_scr, halves)
+    rows = [before.at[1], own.at[0], own.at[1], after.at[0]]
+    back_row(rows[:3], w, slope, 1, e1)
+    back_row(rows[1:], w, slope, 2, e2)
+    fine_grad([s0, s1, s2, s3], [e1, e2], a_scr, b_scr, halves)
     deal(halves, flags[2], mine, other)
 
 
-def input_grad_body(delta, w, out, scr):
-    rows = [delta.at[r] for r in range(4)]
+def input_grad_body(before, own, after, w_second, slope, e1, e2, w, out, scr, e0, e3):
+    back_row([before.at[0], before.at[1], own.at[0]], w_second, slope, 0, e0)
+    back_row([own.at[1], after.at[0], after.at[1]], w_second, slope, 3, e3)
+    rows = [e0, e1, e2, e3]
     for r in range(2):
-        for col in range(0, delta.shape[1], 2):
+        for col in range(0, e1.shape[0], 2):
             for side, value in enumerate(fine_pair(rows[r : r + 3], w, col)):
                 scr[col + side] = value
         out[r] = pltpu.einshape("wcd->cwd", scr[...])
@@ -328,20 +336,41 @@
     return values[0]
 
 
-def split_body(flags, mine, got, keep, send):
-    half = keep.shape[0]
-    bit = flags[3]
-    for side in range(2):
-        rows = slice(side * half, (side + 1) * half)
-        total = (mine[rows, :].astype(F32) + got[rows, :].astype(F32)).astype(BF)
-
-        @pl.when(bit == side)
-        def _():
-            keep[...] = total
-
-        @pl.when(bit != side)
-        def _():
-            send[...] = total
+def split_body(count, flags, *refs):
+    keep, send = refs[2 * count :]
+    at = 0
+    for mine, got in zip(refs[:count], refs[count : 2 * count]):
+        half = mine.shape[0] // 2
+        for side in range(2):
+            rows = slice(side * half, (side + 1) * half)
+            total = (mine[rows, :].astype(F32) + got[rows, :].astype(F32)).astype(BF)
+
+            @pl.when(flags[3] == side)
+            def _():
+                keep[at : at + half, :] = total
+
+            @pl.when(flags[3] != side)
+            def _():
+                send[at : at + half, :] = total
+
+        at += half
+
+
+def chunk_body(flags, keep, got, *refs):
+    *outs, scr = refs
+    num, rows, _ = scr.shape
+    for i in range(num):
+        at = slice(i * rows, (i + 1) * rows)
+        scr[i] = (keep[at, :].astype(F32) + got[at, :].astype(F32)).astype(BF)
+    for t, out in enumerate(outs):
+        out[...] = scr[lax.rem(flags[4] + t, num)]
+
+
+def gather_body(flags, *refs):
+    *parts, out = refs
+    num = out.shape[0]
+    for t, part in enumerate(parts):
+        out[lax.rem(flags[4] + num - t, num)] = part[...]
 
 
 def add_body(*refs):
@@ -350,8 +379,8 @@
 
 def order_body(flags, mine, got, out):
     bit = flags[3]
-    out[bit] = mine[...]
-    out[1 - bit] = got[...]
+    out[bit] = mine[...].reshape(out.shape[1:])
+    out[1 - bit] = got[...].reshape(out.shape[1:])
 
 
 def block_of(halves, block, num):
@@ -370,25 +399,26 @@
         out[3 * tap + 2] = value[:, chan:] if tap % 2 else value[:, :chan]
 
 
-def gather_halves(flags, mine, got, halves):
-    bit = flags[2]
-    halves[bit] = mine[...].reshape(halves.shape[1:])
-    halves[1 - bit] = got[...].reshape(halves.shape[1:])
-
-
-def fine_unpack(flags, mine, got, out, halves):
-    gather_halves(flags, mine, got, halves)
-    fine_blocks(halves, out)
-
-
-def middle_unpack(flags, mine, got, out, down, halves):
-    gather_halves(flags, mine, got, halves)
-    fine_blocks(halves, out)
-    chan = out.shape[1]
+def gather_halves(flags, mine, got, *arrays):
+    at = 0
+    for halves in arrays:
+        rows = halves.shape[1] // 2
+        for side in range(2):
+            to = slice(side * rows, (side + 1) * rows)
+            halves[flags[2], to, :] = mine[side, at : at + rows, :]
+            halves[1 - flags[2], to, :] = got[side, at : at + rows, :]
+        at += rows
+
+
+def fine_unpack(flags, mine, got, first, second, down, middle_halves, first_halves):
+    gather_halves(flags, mine, got, middle_halves, first_halves)
+    fine_blocks(first_halves, first)
+    fine_blocks(middle_halves, second)
+    chan = first.shape[1]
     for a in range(2):
         for b in range(2):
             for c in range(2):
-                down[4 * a + 2 * b + c] = block_of(halves, 14 + 4 * a + 2 * c + b, chan)
+                down[4 * a + 2 * b + c] = block_of(middle_halves, 14 + 4 * a + 2 * c + b, chan)
 
 
 def coarse_unpack(flags, mine, got, out, halves):
@@ -402,21 +432,45 @@
                 )
 
 
-def reduced(flags, mine, other, unpack, outs):
-    rows, lanes = mine.shape
-    quarter = ((rows // 2, lanes), BF)
-    got = swapped(other, 1)
-    keep, send = call(split_body, [quarter] * 2, flags, mine, got, smem=1)
-    (part,) = call(add_body, [quarter], keep, swapped(send, 2))
-    parts = [part] + [shifted(part, 4, t) for t in range(1, lax.axis_size(AXIS) // 4)]
-    (part,) = call(add_body, [quarter], *parts)
-    (pair,) = call(
-        order_body, [((2, rows // 2, lanes), BF)], flags, part, swapped(part, 2), smem=1
-    )
+def tied(first, *others):
+    return lax.optimization_barrier((first,) + others)[0]
+
+
+def halved(flags, *pairs):
+    mine, got = zip(*pairs)
+    rows = sum(m.shape[0] for m in mine) // 2
     return call(
-        unpack, outs, flags, pair, swapped(pair, 1), smem=1,
-        scratch=(pltpu.VMEM((2, rows, lanes), BF),),
-    )
+        functools.partial(split_body, len(pairs)), [((rows, mine[0].shape[1]), BF)] * 2,
+        flags, *mine, *got, smem=1,
+    )
+
+
+def summed(*parts):
+    return call(add_body, [(parts[0].shape, BF)], *parts)[0]
+
+
+def chunks(flags, keep, got):
+    num = lax.axis_size(AXIS) // 4
+    shape = (keep.shape[0] // num, keep.shape[1])
+    return call(
+        chunk_body, [(shape, BF)] * num, flags, keep, got, smem=1,
+        scratch=(pltpu.VMEM((num,) + shape, BF),),
+    )
+
+
+def sent(parts):
+    return [shifted(part, 4, t) for t, part in enumerate(parts, 1)]
+
+
+def gathered(flags, parts):
+    return call(gather_body, [((len(parts),) + parts[0].shape, BF)], flags, *parts, smem=1)[0]
+
+
+def paired(flags, part, got):
+    lanes = part.shape[-1]
+    return call(
+        order_body, [((2, part.size // lanes, lanes), BF)], flags, part, got, smem=1
+    )[0]
 
 
 def body(volume, skip_grad, coarse_grad, w_first, w_second, w_down, w_coarse):
@@ -426,13 +480,12 @@
     size = num // 2 * half
     index = lax.axis_index(AXIS)
     flags = jnp.stack(
-        [index, lax.axis_size(AXIS) - 1 - index, index % 2, (index // 2) % 2]
+        [index, lax.axis_size(AXIS) - 1 - index, index % 2, (index // 2) % 2, index // 4]
     ).astype(jnp.int32)
 
     fine = ((num, chan, deep), BF)
     coarse = ((size, wide), BF)
     two = ((2, num, chan, deep), BF)
-    four = ((4, num, chan, deep), BF)
 
     before, after = from_before(volume), from_after(volume)
     v1, v2, skip, first_f, second_f, first_b, second_b, coarse_f, coarse_b, down_f, down_b = call(
@@ -447,7 +500,7 @@
     )
     v0, v3, f0, f1, f2, f3, slope1, slope2, act_t, pooled = call(
         forward_kernel,
-        [fine] * 6 + [(four[0], F32), (two[0], F32), ((size, 8 * chan), BF), coarse],
+        [fine] * 6 + [((4, num, chan, deep), F32), (two[0], F32), ((size, 8 * chan), BF), coarse],
         flags, before, v1, v2, after, first_f, second_f, down_f,
         scratch=(pltpu.VMEM(*two),),
         smem=1,
@@ -465,34 +518,55 @@
     def halves(blocks):
         return pltpu.VMEM((2, blocks // 2 * chan, 2 * chan), BF)
 
-    coarse_sum = call(
-        functools.partial(coarse_grad_body, half), [dealt(54)] * 2, flags, *rows, delta,
-        scratch=(halves(54),), smem=1,
-    )
+    a_mine, a_other = call(
+        functools.partial(coarse_grad_body, half), [dealt(56)] * 2, flags, *rows, delta,
+        scratch=(halves(56),), smem=1,
+    )
+    a_keep, a_send = halved(flags, (a_mine, swapped(a_other, 1)))
+    a_got = swapped(a_send, 2)
     pg, second = call(
         functools.partial(second_delta_body, half), [coarse, two],
         *delta_rows, coarse_b, down_b, skip, slope2,
     )
-    second_before, second_after = from_before(second), from_after(second)
-    middle_sum = call(
+    second_rows = [from_before(second), second, from_after(second)]
+    a_chunks = chunks(flags, a_keep, tied(a_got, second))
+    b_mine, b_other = call(
         second_grad_body, [dealt(22)] * 2, flags, f0, f1, f2, f3, second, act_t, pg,
         scratch=fine_grad_scratch(num, chan, deep) + (halves(22),), smem=1,
     )
-    first, *first_sum = call(
-        first_delta_body, [four] + [dealt(14)] * 2,
-        flags, second_before, second, second_after, second_b, slope1, v0, v1, v2, v3,
+    b_got = swapped(b_other, 1)
+    a_got = sent(a_chunks[1:])
+    e1, e2, c_mine, c_other = call(
+        first_delta_body, [fine, fine] + [dealt(14)] * 2,
+        flags, *second_rows, second_b, slope1, v0, v1, v2, v3,
         scratch=fine_grad_scratch(num, chan, deep) + (halves(14),), smem=1,
     )
+    a_part = summed(tied(a_chunks[0], c_mine), *a_got)
+    a_got = sent([a_part] * len(a_got))
+    keep, send = halved(flags, (b_mine, b_got), (c_mine, swapped(c_other, 1)))
+    got = swapped(send, 2)
     (input_grad,) = call(
-        input_grad_body, [((2, chan, num, deep), F32)], first, first_b,
-        scratch=(pltpu.VMEM((num, chan, deep), F32),),
+        input_grad_body, [((2, chan, num, deep), F32)],
+        tied(second_rows[0], keep), *second_rows[1:], second_b, slope1, e1, e2, first_b,
+        scratch=(pltpu.VMEM((num, chan, deep), F32), pltpu.VMEM(*fine), pltpu.VMEM(*fine)),
+    )
+    part = summed(keep, tied(got, input_grad))
+    got = sent([part] * (lax.axis_size(AXIS) // 4 - 1))
+    a_part = gathered(flags, [tied(a_part, part)] + a_got)
+    a_got = swapped(a_part, 2)
+    a_pair = paired(flags, a_part, a_got)
+    a_got = swapped(a_pair, 1)
+    part = summed(part, *got)
+    pair = paired(flags, tied(part, a_pair), swapped(part, 2))
+    (coarse_out,) = call(
+        coarse_unpack, [((27, wide, wide), F32)], flags, tied(a_pair, pair), a_got,
+        smem=1, scratch=(halves(56),),
     )
     fine_out = ((27, chan, chan), F32)
-    (coarse_out,) = reduced(flags, *coarse_sum, coarse_unpack, [((27, wide, wide), F32)])
-    second_out, down_out = reduced(
-        flags, *middle_sum, middle_unpack, [fine_out, ((8, chan, wide), F32)]
-    )
-    (first_out,) = reduced(flags, *first_sum, fine_unpack, [fine_out])
+    first_out, second_out, down_out = call(
+        fine_unpack, [fine_out, fine_out, ((8, chan, wide), F32)], flags, pair, swapped(pair, 1),
+        smem=1, scratch=(halves(22), halves(14)),
+    )
     return (
         input_grad,
         first_out.reshape(3, 3, 3, chan, chan),

time: 125 us -> 116 us (0.928)
  waiting for transfers between devices: 33.4 us -> 22 us
  starting transfers between devices: 49 us -> 53.2 us
  Pallas kernels: 36.2 us -> 34.2 us
    ppermute x12 -> x9, waiting for transfers between devices: 11.3 us -> 1.23 us  [swapped(): return lax.ppermute(array, AXIS, [(i, i ^ stride) for i in range(size)])]
    ppermute x9, waiting for transfers between devices: 14.6 us -> 7.94 us  [shifted(): lax.ppermute(array, AXIS, [(i, (i + by * stride) % size) for i in range(s...]
    ppermute x4, waiting for transfers between devices: 6.06 us -> 12.2 us  [from_before(): return lax.ppermute(array, AXIS, neighbours(array)[0])]
    ppermute x12 -> x9, starting transfers between devices: 14.1 us -> 16.9 us  [swapped(): return lax.ppermute(array, AXIS, [(i, i ^ stride) for i in range(size)])]
    pallas_call x23 -> x19, Pallas kernels: 36.2 us -> 34.2 us  [call(): pl.pallas_call(body, out_shape=[jax.ShapeDtypeStruct(s, d) for s, d in ou...]
    ppermute x9, starting transfers between devices: 9.51 us -> 11 us  [shifted(): lax.ppermute(array, AXIS, [(i, (i + by * stride) % size) for i in range(s...]
    unnamed x12 -> x14, local copies, waits for them, and re-layouts: 5.01 us -> 5.02 us
  transfers between devices with their start and end apart: 29 -> 26, of which waited for: 11 -> 7; matrix products, arithmetic and copies ran while one was open for 0% -> 0% of each run, Pallas kernels for 17% -> 18%
where the time goes in v2:
time: 116 us
  starting transfers between devices  53.2 us (46%)
  Pallas kernels  34.2 us (29%)
  waiting for transfers between devices  22 us (19%)
  local copies, waits for them, and re-layouts  5.11 us (4%)
    pallas_call x19, Pallas kernels, call(): pl.pallas_call(body, out_shape=[jax.ShapeDtypeStruct(s, d) for s, d in ou...  34.2 us
    ppermute x4, starting transfers between devices, from_before(): return lax.ppermute(array, AXIS, neighbours(array)[0])  17.6 us
    ppermute x9, starting transfers between devices, swapped(): return lax.ppermute(array, AXIS, [(i, i ^ stride) for i in range(size)])  16.9 us
    ppermute x4, waiting for transfers between devices, from_before(): return lax.ppermute(array, AXIS, neighbours(array)[0])  12.2 us
    ppermute x9, starting transfers between devices, shifted(): lax.ppermute(array, AXIS, [(i, (i + by * stride) % size) for i in range(s...  11 us
    ppermute x9, waiting for transfers between devices, shifted(): lax.ppermute(array, AXIS, [(i, (i + by * stride) % size) for i in range(s...  7.94 us
    ppermute x4, starting transfers between devices, from_after(): return lax.ppermute(array, AXIS, neighbours(array)[1])  7.67 us
    unnamed x14, local copies, waits for them, and re-layouts  5.02 us
  transfers between devices with their start and end apart: 26, of which 7 were waited for; matrix products, arithmetic and copies ran while one was open for 0% of the time, Pallas kernels for 18%

profile of v2, /device:TPU:1, one launch (start us, length us, event | category | flops | bytes accessed | tf_op | source)
XLA Modules:
  0.0 115.5 jit_solution(4083321038991431588)
XLA Ops:
  0.6 4.5 %collective-permute-start = (bf16[2,64,16,128]{3,2,1,0:T(8,128)(2,1)}, bf16[2,64,16,128]{3,2,1,0:T(8,128)(2,1)S(1)}, u32[]{:S(2)}, u32[]{:S(2)}) collective-permute-start(bf16[2,64,16,128]{3,2,1,0:T(8,128)(2,1)} %volume.1), channel_id=1, source_target_pairs={{0,1},{1,2},{2,3},{3,4},{4,5},{5,6},{6,7},{7,8},{8,9},{9,10},{10,1... | collective-permute-start | bytes 1572872 | tf_op jit(solution)/shard_map/ppermute | solution.py:44
  5.2 1.9 %collective-permute-start.1 = (bf16[2,64,16,128]{3,2,1,0:T(8,128)(2,1)}, bf16[2,64,16,128]{3,2,1,0:T(8,128)(2,1)S(1)}, u32[]{:S(2)}, u32[]{:S(2)}) collective-permute-start(bf16[2,64,16,128]{3,2,1,0:T(8,128)(2,1)} %volume.1), channel_id=1, source_target_pairs={{1,0},{2,1},{3,2},{4,3},{5,4},{6,5},{7,6},{8,7},{9,8},{10,9},{11,1... | collective-permute-start | bytes 1572872 | tf_op jit(solution)/shard_map/ppermute | solution.py:48
  7.2 0.1 stack.23.flags
  7.2 1.0 copy-done.1
  8.3 1.0 copy-done.2
  9.3 1.0 copy-done.3
  10.3 1.0 copy-done.4
  11.4 0.9 copy-done.5
  12.3 2.3 %shard_map.110 = (bf16[16,64,128]{2,1,0:T(8,128)(2,1)S(1)}, bf16[16,64,128]{2,1,0:T(8,128)(2,1)S(1)}, bf16[2,16,64,128]{3,2,1,0:T(8,128)(2,1)S(1)}, bf16[192,576...) custom-call(bf16[2,64,16,128]{3,2,1,0:T(8,128)(2,1)S(1)} %copy-done., ...), custom_call_target="tpu_custom_call" | custom-call | flops 1000000000 | bytes 1048576 | tf_op jit(solution)/shard_map/pallas_call | solution.py:25
  14.6 0.0 copy-start.6
  14.6 2.6 %collective-permute-done.before = bf16[2,64,16,128]{3,2,1,0:T(8,128)(2,1)S(1)} collective-permute-done((bf16[2,64,16,128]{3,2,1,0:T(8,128)(2,1)}, bf16[2,64,16,128]{3,2,1,0:T(8,128)(2,1)S(1)}, u32[]{:S(2)}, u32[]{:S(2)}) %collective-permute-start) | collective-permute-done | bytes 524320 | tf_op jit(solution)/shard_map/ppermute | solution.py:44
  17.2 0.0 collective-permute-done.1.after
  17.2 10.4 %shard_map.111 = (bf16[16,64,128]{2,1,0:T(8,128)(2,1)S(1)}, bf16[16,64,128]{2,1,0:T(8,128)(2,1)S(1)}, bf16[16,64,128]{2,1,0:T(8,128)(2,1)S(1)}, bf16[16,64,128]{...) custom-call(s32[5]{0:T(128)S(1)} %stack.23.flags, ...), custom_call_target="tpu_custom_call" | custom-call | flops 1000000000 | bytes 1048576 | tf_op jit(solution)/shard_map/pallas_call | solution.py:25
  27.6 1.9 %collective-permute-start.3 = (bf16[512,128]{1,0:T(8,128)(2,1)S(1)}, bf16[512,128]{1,0:T(8,128)(2,1)S(1)}, u32[]{:S(2)}, u32[]{:S(2)}) collective-permute-start(bf16[512,128]{1,0:T(8,128)(2,1)S(1)} %get-tuple-element.59.own), channel_id=1, source_target_pairs={{1,0},{2,1},{3,2},{4,3},{5,4},{6,5},{7,6},{8,7},{9,8},{10,9},{11,1... | collective-permute-start | bytes 393224 | tf_op jit(solution)/shard_map/ppermute | solution.py:48
  29.6 4.3 %collective-permute-start.2 = (bf16[512,128]{1,0:T(8,128)(2,1)S(1)}, bf16[512,128]{1,0:T(8,128)(2,1)S(1)}, u32[]{:S(2)}, u32[]{:S(2)}) collective-permute-start(bf16[512,128]{1,0:T(8,128)(2,1)S(1)} %get-tuple-element.59.own), channel_id=1, source_target_pairs={{0,1},{1,2},{2,3},{3,4},{4,5},{5,6},{6,7},{7,8},{8,9},{9,10},{10,1... | collective-permute-start | bytes 393224 | tf_op jit(solution)/shard_map/ppermute | solution.py:44
  33.8 0.7 collective-permute-done.3.after
  34.6 1.2 %collective-permute-done.2.before = bf16[512,128]{1,0:T(8,128)(2,1)S(1)} collective-permute-done((bf16[512,128]{1,0:T(8,128)(2,1)S(1)}, bf16[512,128]{1,0:T(8,128)(2,1)S(1)}, u32[]{:S(2)}, u32[]{:S(2)}) %collective-permute-start.2) | collective-permute-done | bytes 131104 | tf_op jit(solution)/shard_map/ppermute | solution.py:44
  35.8 0.9 shard_map.112.own.delta
  36.7 1.9 %collective-permute-start.5 = (bf16[512,128]{1,0:T(8,128)(2,1)S(1)}, bf16[512,128]{1,0:T(8,128)(2,1)S(1)}, u32[]{:S(2)}, u32[]{:S(2)}) collective-permute-start(bf16[512,128]{1,0:T(8,128)(2,1)S(1)} %shard_map.112.own.delta), channel_id=1, source_target_pairs={{1,0},{2,1},{3,2},{4,3},{5,4},{6,5},{7,6},{8,7},{9,8},{10,9},{11,1... | collective-permute-start | bytes 393224 | tf_op jit(solution)/shard_map/ppermute | solution.py:48
  38.6 4.4 %collective-permute-start.4 = (bf16[512,128]{1,0:T(8,128)(2,1)S(1)}, bf16[512,128]{1,0:T(8,128)(2,1)S(1)}, u32[]{:S(2)}, u32[]{:S(2)}) collective-permute-start(bf16[512,128]{1,0:T(8,128)(2,1)S(1)} %shard_map.112.own.delta), channel_id=1, source_target_pairs={{0,1},{1,2},{2,3},{3,4},{4,5},{5,6},{6,7},{7,8},{8,9},{9,10},{10,1... | collective-permute-start | bytes 393224 | tf_op jit(solution)/shard_map/ppermute | solution.py:44
  43.0 1.4 %shard_map.120 = (bf16[1792,128]{1,0:T(8,128)(2,1)S(1)}, bf16[1792,128]{1,0:T(8,128)(2,1)S(1)}) custom-call(s32[5]{0:T(128)S(1)} %stack.23.flags, bf16[512,128]{1,0:T(8,128)(2,1)S(1)} %collective-permute-done.2.before, bf16[512,128]{1,0:T(8,128)(2,1)S(1)} %get-tuple-element.59.own, bf16[512,128]{1,0:T(8,128)(2,1)S(1)} %collective-permute-done.3.after, ...), custom_call_target="tpu_custom_call" | custom-call | flops 1000000000 | bytes 1048576 | tf_op jit(solution)/shard_map/pallas_call | solution.py:25
  44.4 0.1 collective-permute-start.14
  44.5 0.0 collective-permute-done.5.after
  44.5 0.8 collective-permute-done.4.before
  45.2 1.5 %shard_map.113 = (bf16[512,128]{1,0:T(8,128)(2,1)S(1)}, bf16[2,16,64,128]{3,2,1,0:T(8,128)(2,1)S(1)}) custom-call(bf16[512,128]{1,0:T(8,128)(2,1)S(1)} %collective-permute-done.4.before, bf16[512,128]{1,0:T(8,128)(2,1)S(1)} %shard_map.112.own.delta, bf16[512,128]{1,0:T(8,128)(2,1)S(1)} %collective-permute-done.5.after, ...), custom_call_target="tpu_custom_call" | custom-call | flops 1000000000 | bytes 1048576 | tf_op jit(solution)/shard_map/pallas_call | solution.py:25
  46.8 1.9 %collective-permute-start.7 = (bf16[2,16,64,128]{3,2,1,0:T(8,128)(2,1)S(1)}, bf16[2,16,64,128]{3,2,1,0:T(8,128)(2,1)S(1)}, u32[]{:S(2)}, u32[]{:S(2)}) collective-permute-start(bf16[2,16,64,128]{3,2,1,0:T(8,128)(2,1)S(1)} %get-tuple-element.65.delta.own), channel_id=1, source_target_pairs={{1,0},{2,1},{3,2},{4,3},{5,4},{6,5},{7,6},{8,7},{9,8},{10,9},{11,1... | collective-permute-start | bytes 1572872 | tf_op jit(solution)/shard_map/ppermute | solution.py:48
  48.7 4.4 %collective-permute-start.6 = (bf16[2,16,64,128]{3,2,1,0:T(8,128)(2,1)S(1)}, bf16[2,16,64,128]{3,2,1,0:T(8,128)(2,1)S(1)}, u32[]{:S(2)}, u32[]{:S(2)}) collective-permute-start(bf16[2,16,64,128]{3,2,1,0:T(8,128)(2,1)S(1)} %get-tuple-element.65.delta.own), channel_id=1, source_target_pairs={{0,1},{1,2},{2,3},{3,4},{4,5},{5,6},{6,7},{7,8},{8,9},{9,10},{10,1... | collective-permute-start | bytes 1572872 | tf_op jit(solution)/shard_map/ppermute | solution.py:44
  53.1 0.9 shard_map.121
  54.1 2.6 %collective-permute-start.15 = (bf16[896,128]{1,0:T(8,128)(2,1)S(1)}, bf16[896,128]{1,0:T(8,128)(2,1)S(1)}, u32[]{:S(2)}, u32[]{:S(2)}) collective-permute-start(bf16[896,128]{1,0:T(8,128)(2,1)S(1)} %get-tuple-element.90), channel_id=1, source_target_pairs={{0,2},{1,3},{2,0},{3,1},{4,6},{5,7},{6,4},{7,5},{8,10},{9,11},{10,... | collective-permute-start | bytes 688136 | tf_op jit(solution)/shard_map/ppermute | solution.py:53
  56.7 2.4 %shard_map.114 = (bf16[704,128]{1,0:T(8,128)(2,1)S(1)}, bf16[704,128]{1,0:T(8,128)(2,1)S(1)}) custom-call(s32[5]{0:T(128)S(1)} %stack.23.flags, bf16[16,64,128]{2,1,0:T(8,128)(2,1)S(1)} %get-tuple-element.66.s0, bf16[16,64,128]{2,1,0:T(8,128)(2,1)S(1)} %get-tuple-element.67.s1, bf16[16,64,128]{2,1,0:T(8,128)(2,1)S(1)} %get-tuple-element.68.s2, ...), custom_call_target="tpu_custom_call" | custom-call | flops 1000000000 | bytes 1048576 | tf_op jit(solution)/shard_map/pallas_call | solution.py:25
  59.1 0.1 collective-permute-start.8
  59.2 0.0 collective-permute-done.7.after
  59.2 7.6 %collective-permute-done.6.before = bf16[2,16,64,128]{3,2,1,0:T(8,128)(2,1)S(1)} collective-permute-done((bf16[2,16,64,128]{3,2,1,0:T(8,128)(2,1)S(1)}, bf16[2,16,64,128]{3,2,1,0:T(8,128)(2,1)S(1)}, u32[]{:S(2)}, u32[]{:S(2)}) %collective-permute-start.6) | collective-permute-done | bytes 524320 | tf_op jit(solution)/shard_map/ppermute | solution.py:44
  66.8 3.5 %shard_map.115 = (bf16[16,64,128]{2,1,0:T(8,128)(2,1)S(1)}, bf16[16,64,128]{2,1,0:T(8,128)(2,1)S(1)}, bf16[448,128]{1,0:T(8,128)(2,1)S(1)}, bf16[448,128]{1,0:T(8,128)(2,1)S(1)}) custom-call(s32[5]{0:T(128)S(1)} %stack.23.flags, bf16[2,16,64,128]{3,2,1,0:T(8,128)(2,1)S(1)} %collective-permute-done.6.before, ...), custom_call_target="tpu_custom_call" | custom-call | flops 1000000000 | bytes 1048576 | tf_op jit(solution)/shard_map/pallas_call | solution.py:25
  70.3 0.1 collective-permute-start.9
  70.4 0.6 shard_map.122
  71.0 1.4 %collective-permute-start.16 = (bf16[224,128]{1,0:T(8,128)(2,1)S(1)}, bf16[224,128]{1,0:T(8,128)(2,1)S(1)}, u32[]{:S(2)}, u32[]{:S(2)}) collective-permute-start(bf16[224,128]{1,0:T(8,128)(2,1)S(1)} %get-tuple-element.94), channel_id=1, source_target_pairs={{0,4},{1,5},{2,6},{3,7},{4,8},{5,9},{6,10},{7,11},{8,12},{9,13},{1... | collective-permute-start | bytes 172040 | tf_op jit(solution)/shard_map/ppermute | solution.py:58
  72.4 1.4 %collective-permute-start.17 = (bf16[224,128]{1,0:T(8,128)(2,1)S(1)}, bf16[224,128]{1,0:T(8,128)(2,1)S(1)}, u32[]{:S(2)}, u32[]{:S(2)}) collective-permute-start(bf16[224,128]{1,0:T(8,128)(2,1)S(1)} %get-tuple-element.95), channel_id=1, source_target_pairs={{0,8},{1,9},{2,10},{3,11},{4,12},{5,13},{6,14},{7,15},{8,0},{9,1},... | collective-permute-start | bytes 172040 | tf_op jit(solution)/shard_map/ppermute | solution.py:58
  73.8 2.0 %collective-permute-start.18 = (bf16[224,128]{1,0:T(8,128)(2,1)S(1)}, bf16[224,128]{1,0:T(8,128)(2,1)S(1)}, u32[]{:S(2)}, u32[]{:S(2)}) collective-permute-start(bf16[224,128]{1,0:T(8,128)(2,1)S(1)} %get-tuple-element.96), channel_id=1, source_target_pairs={{0,12},{1,13},{2,14},{3,15},{4,0},{5,1},{6,2},{7,3},{8,4},{9,5},{1... | collective-permute-start | bytes 172040 | tf_op jit(solution)/shard_map/ppermute | solution.py:58
  75.8 0.0 collective-permute-done.8.refs_2_
  75.8 0.0 collective-permute-done.9.refs_3_
  75.8 0.7 shard_map.116
  76.4 2.6 %collective-permute-start.10 = (bf16[576,128]{1,0:T(8,128)(2,1)S(1)}, bf16[576,128]{1,0:T(8,128)(2,1)S(1)}, u32[]{:S(2)}, u32[]{:S(2)}) collective-permute-start(bf16[576,128]{1,0:T(8,128)(2,1)S(1)} %get-tuple-element.85), channel_id=1, source_target_pairs={{0,2},{1,3},{2,0},{3,1},{4,6},{5,7},{6,4},{7,5},{8,10},{9,11},{10,... | collective-permute-start | bytes 442376 | tf_op jit(solution)/shard_map/ppermute | solution.py:53
  79.1 0.0 collective-permute-done.16.refs_1_
  79.1 0.0 collective-permute-done.17.refs_2_
  79.1 0.0 collective-permute-done.18.refs_3_
  79.1 2.0 %collective-permute-start.21 = (bf16[224,128]{1,0:T(8,128)(2,1)S(1)}, bf16[224,128]{1,0:T(8,128)(2,1)S(1)}, u32[]{:S(2)}, u32[]{:S(2)}) collective-permute-start(bf16[224,128]{1,0:T(8,128)(2,1)S(1)} %shard_map.123.refs_0_), channel_id=1, source_target_pairs={{0,12},{1,13},{2,14},{3,15},{4,0},{5,1},{6,2},{7,3},{8,4},{9,5},{1... | collective-permute-start | bytes 172040 | tf_op jit(solution)/shard_map/ppermute | solution.py:58
  81.1 0.6 collective-permute-start.20
  81.7 0.0 collective-permute-start.19
  81.7 3.7 %shard_map.117 = f32[2,64,16,128]{3,2,1,0:T(8,128)} custom-call(bf16[2,16,64,128]{3,2,1,0:T(8,128)(2,1)S(1)} %collective-permute-done.6.before, bf16[2,16,64,128]{3,2,1,0:T(8,128)(2,1)S(1)} %get-tuple-element.65.delta.own, bf16[2,16,64,128]{3,2,1,0:T(8,128)(2,1)S(1)} %collective-permute-done.7.after, bf16[192,576]{1,0:T(8,128)(2,1)S(1)} %get-tuple-element.73.w.w_second, ...), custom_call_target="tpu_custom_call" | custom-call | flops 1000000000 | bytes 1048576 | tf_op jit(solution)/shard_map/pallas_call | solution.py:25
  85.5 3.3 %collective-permute-start.13 = (bf16[576,128]{1,0:T(8,128)(2,1)S(1)}, bf16[576,128]{1,0:T(8,128)(2,1)S(1)}, u32[]{:S(2)}, u32[]{:S(2)}) collective-permute-start(bf16[576,128]{1,0:T(8,128)(2,1)S(1)} %shard_map.118.refs_0_), channel_id=1, source_target_pairs={{0,12},{1,13},{2,14},{3,15},{4,0},{5,1},{6,2},{7,3},{8,4},{9,5},{1... | collective-permute-start | bytes 442376 | tf_op jit(solution)/shard_map/ppermute | solution.py:58
  88.8 0.4 collective-permute-start.11
  89.2 0.6 shard_map.124.mine
  89.8 2.9 %collective-permute-start.22 = (bf16[4,224,128]{2,1,0:T(8,128)(2,1)S(1)}, bf16[4,224,128]{2,1,0:T(8,128)(2,1)S(1)}, u32[]{:S(2)}, u32[]{:S(2)}) collective-permute-start(bf16[4,224,128]{2,1,0:T(8,128)(2,1)S(1)} %shard_map.124.mine), channel_id=1, source_target_pairs={{0,2},{1,3},{2,0},{3,1},{4,6},{5,7},{6,4},{7,5},{8,10},{9,11},{10,... | collective-permute-start | bytes 688136 | tf_op jit(solution)/shard_map/ppermute | solution.py:53
  92.7 7.9 %collective-permute-done.12.refs_2_ = bf16[576,128]{1,0:T(8,128)(2,1)S(1)} collective-permute-done((bf16[576,128]{1,0:T(8,128)(2,1)S(1)}, bf16[576,128]{1,0:T(8,128)(2,1)S(1)}, u32[]{:S(2)}, u32[]{:S(2)}) %collective-permute-start.12) | collective-permute-done | bytes 147488 | tf_op jit(solution)/shard_map/ppermute | solution.py:58
  100.6 0.1 shard_map.119.mine
  100.7 3.7 %collective-permute-start.23 = (bf16[576,128]{1,0:T(8,128)(2,1)S(1)}, bf16[576,128]{1,0:T(8,128)(2,1)S(1)}, u32[]{:S(2)}, u32[]{:S(2)}) collective-permute-start(bf16[576,128]{1,0:T(8,128)(2,1)S(1)} %shard_map.119.mine), channel_id=1, source_target_pairs={{0,2},{1,3},{2,0},{3,1},{4,6},{5,7},{6,4},{7,5},{8,10},{9,11},{10,... | collective-permute-start | bytes 442376 | tf_op jit(solution)/shard_map/ppermute | solution.py:53
  104.4 0.6 shard_map.125.mine
  105.0 2.3 %collective-permute-start.25 = (bf16[2,896,128]{2,1,0:T(8,128)(2,1)S(1)}, bf16[2,896,128]{2,1,0:T(8,128)(2,1)S(1)}, u32[]{:S(2)}, u32[]{:S(2)}) collective-permute-start(bf16[2,896,128]{2,1,0:T(8,128)(2,1)S(1)} %shard_map.125.mine), channel_id=1, source_target_pairs={{0,1},{1,0},{2,3},{3,2},{4,5},{5,4},{6,7},{7,6},{8,9},{9,8},{10,11... | collective-permute-start | bytes 1376264 | tf_op jit(solution)/shard_map/ppermute | solution.py:53
  107.3 0.6 shard_map.126.mine
  107.8 2.5 %collective-permute-start.24 = (bf16[2,576,128]{2,1,0:T(8,128)(2,1)S(1)}, bf16[2,576,128]{2,1,0:T(8,128)(2,1)S(1)}, u32[]{:S(2)}, u32[]{:S(2)}) collective-permute-start(bf16[2,576,128]{2,1,0:T(8,128)(2,1)S(1)} %shard_map.126.mine), channel_id=1, source_target_pairs={{0,1},{1,0},{2,3},{3,2},{4,5},{5,4},{6,7},{7,6},{8,9},{9,8},{10,11... | collective-permute-start | bytes 884744 | tf_op jit(solution)/shard_map/ppermute | solution.py:53
  110.4 1.2 %collective-permute-done.24.got = bf16[2,576,128]{2,1,0:T(8,128)(2,1)S(1)} collective-permute-done((bf16[2,576,128]{2,1,0:T(8,128)(2,1)S(1)}, bf16[2,576,128]{2,1,0:T(8,128)(2,1)S(1)}, u32[]{:S(2)}, u32[]{:S(2)}) %collective-permute-start.24) | collective-permute-done | bytes 294944 | tf_op jit(solution)/shard_map/ppermute | solution.py:53
  111.6 2.0 %shard_map.127 = (f32[27,64,64]{2,1,0:T(8,128)}, f32[27,64,64]{2,1,0:T(8,128)}, f32[8,64,128]{2,1,0:T(8,128)}) custom-call(s32[5]{0:T(128)S(1)} %stack.23.flags, bf16[2,576,128]{2,1,0:T(8,128)(2,1)S(1)} %shard_map.126.mine, bf16[2,576,128]{2,1,0:T(8,128)(2,1)S(1)} %collective-permute-done.24.got), custom_call_target="tpu_custom_call" | custom-call | flops 1000000000 | bytes 1048576 | tf_op jit(solution)/shard_map/pallas_call | solution.py:25
  113.6 1.9 %shard_map.128 = f32[27,128,128]{2,1,0:T(8,128)} custom-call(s32[5]{0:T(128)S(1)} %stack.23.flags, bf16[2,896,128]{2,1,0:T(8,128)(2,1)S(1)} %shard_map.125.mine, bf16[2,896,128]{2,1,0:T(8,128)(2,1)S(1)} %collective-permute-done.25.got), custom_call_target="tpu_custom_call" | custom-call | flops 1000000000 | bytes 1048576 | tf_op jit(solution)/shard_map/pallas_call | solution.py:25
  (22 shorter events, 0.1 us)
Async XLA Ops:
  0.6 16.6 %collective-permute-start = (bf16[2,64,16,128]{3,2,1,0:T(8,128)(2,1)}, bf16[2,64,16,128]{3,2,1,0:T(8,128)(2,1)S(1)}, u32[]{:S(2)}, u32[]{:S(2)}) collective-permute-start(bf16[2,64,16,128]{3,2,1,0:T(8,128)(2,1)} %volume.1), channel_id=1, source_target_pairs={{0,1},{1,2},{2,3},{3,4},{4,5},{5,6},{6,7},{7,8},{8,9},{9,10},{10,1... | collective-permute-start | bytes 1572872 | tf_op jit(solution)/shard_map/ppermute | solution.py:44
  5.2 12.0 %collective-permute-start.1 = (bf16[2,64,16,128]{3,2,1,0:T(8,128)(2,1)}, bf16[2,64,16,128]{3,2,1,0:T(8,128)(2,1)S(1)}, u32[]{:S(2)}, u32[]{:S(2)}) collective-permute-start(bf16[2,64,16,128]{3,2,1,0:T(8,128)(2,1)} %volume.1), channel_id=1, source_target_pairs={{1,0},{2,1},{3,2},{4,3},{5,4},{6,5},{7,6},{8,7},{9,8},{10,9},{11,1... | collective-permute-start | bytes 1572872 | tf_op jit(solution)/shard_map/ppermute | solution.py:48
  7.2 1.0 copy-start.1
  8.3 1.0 copy-start.2
  9.3 1.0 copy-start.3
  10.3 1.0 copy-start.4
  11.3 0.9 copy-start.5
  14.6 21.2 %copy-start.6 = (bf16[1,8,64,128]{3,2,1,0:T(8,128)(2,1)S(1)}, bf16[1,8,64,128]{3,2,1,0:T(8,128)(2,1)}, u32[]{:S(2)}) copy-start(bf16[1,8,64,128]{3,2,1,0:T(8,128)(2,1)} %param.9) | copy-start | bytes 393220
  27.6 6.9 %collective-permute-start.3 = (bf16[512,128]{1,0:T(8,128)(2,1)S(1)}, bf16[512,128]{1,0:T(8,128)(2,1)S(1)}, u32[]{:S(2)}, u32[]{:S(2)}) collective-permute-start(bf16[512,128]{1,0:T(8,128)(2,1)S(1)} %get-tuple-element.59.own), channel_id=1, source_target_pairs={{1,0},{2,1},{3,2},{4,3},{5,4},{6,5},{7,6},{8,7},{9,8},{10,9},{11,1... | collective-permute-start | bytes 393224 | tf_op jit(solution)/shard_map/ppermute | solution.py:48
  29.6 6.2 %collective-permute-start.2 = (bf16[512,128]{1,0:T(8,128)(2,1)S(1)}, bf16[512,128]{1,0:T(8,128)(2,1)S(1)}, u32[]{:S(2)}, u32[]{:S(2)}) collective-permute-start(bf16[512,128]{1,0:T(8,128)(2,1)S(1)} %get-tuple-element.59.own), channel_id=1, source_target_pairs={{0,1},{1,2},{2,3},{3,4},{4,5},{5,6},{6,7},{7,8},{8,9},{9,10},{10,1... | collective-permute-start | bytes 393224 | tf_op jit(solution)/shard_map/ppermute | solution.py:44
  36.7 7.8 %collective-permute-start.5 = (bf16[512,128]{1,0:T(8,128)(2,1)S(1)}, bf16[512,128]{1,0:T(8,128)(2,1)S(1)}, u32[]{:S(2)}, u32[]{:S(2)}) collective-permute-start(bf16[512,128]{1,0:T(8,128)(2,1)S(1)} %shard_map.112.own.delta), channel_id=1, source_target_pairs={{1,0},{2,1},{3,2},{4,3},{5,4},{6,5},{7,6},{8,7},{9,8},{10,9},{11,1... | collective-permute-start | bytes 393224 | tf_op jit(solution)/shard_map/ppermute | solution.py:48
  38.6 6.6 %collective-permute-start.4 = (bf16[512,128]{1,0:T(8,128)(2,1)S(1)}, bf16[512,128]{1,0:T(8,128)(2,1)S(1)}, u32[]{:S(2)}, u32[]{:S(2)}) collective-permute-start(bf16[512,128]{1,0:T(8,128)(2,1)S(1)} %shard_map.112.own.delta), channel_id=1, source_target_pairs={{0,1},{1,2},{2,3},{3,4},{4,5},{5,6},{6,7},{7,8},{8,9},{9,10},{10,1... | collective-permute-start | bytes 393224 | tf_op jit(solution)/shard_map/ppermute | solution.py:44
  44.4 8.7 %collective-permute-start.14 = (bf16[1792,128]{1,0:T(8,128)(2,1)S(1)}, bf16[1792,128]{1,0:T(8,128)(2,1)S(1)}, u32[]{:S(2)}, u32[]{:S(2)}) collective-permute-start(bf16[1792,128]{1,0:T(8,128)(2,1)S(1)} %get-tuple-element.88), channel_id=1, source_target_pairs={{0,1},{1,0},{2,3},{3,2},{4,5},{5,4},{6,7},{7,6},{8,9},{9,8},{10,11... | collective-permute-start | bytes 1376264 | tf_op jit(solution)/shard_map/ppermute | solution.py:53
  46.8 12.4 %collective-permute-start.7 = (bf16[2,16,64,128]{3,2,1,0:T(8,128)(2,1)S(1)}, bf16[2,16,64,128]{3,2,1,0:T(8,128)(2,1)S(1)}, u32[]{:S(2)}, u32[]{:S(2)}) collective-permute-start(bf16[2,16,64,128]{3,2,1,0:T(8,128)(2,1)S(1)} %get-tuple-element.65.delta.own), channel_id=1, source_target_pairs={{1,0},{2,1},{3,2},{4,3},{5,4},{6,5},{7,6},{8,7},{9,8},{10,9},{11,1... | collective-permute-start | bytes 1572872 | tf_op jit(solution)/shard_map/ppermute | solution.py:48
  48.7 18.1 %collective-permute-start.6 = (bf16[2,16,64,128]{3,2,1,0:T(8,128)(2,1)S(1)}, bf16[2,16,64,128]{3,2,1,0:T(8,128)(2,1)S(1)}, u32[]{:S(2)}, u32[]{:S(2)}) collective-permute-start(bf16[2,16,64,128]{3,2,1,0:T(8,128)(2,1)S(1)} %get-tuple-element.65.delta.own), channel_id=1, source_target_pairs={{0,1},{1,2},{2,3},{3,4},{4,5},{5,6},{6,7},{7,8},{8,9},{9,10},{10,1... | collective-permute-start | bytes 1572872 | tf_op jit(solution)/shard_map/ppermute | solution.py:44
  54.1 12.7 %copy-start = (f32[4,16,64,128]{3,2,1,0:T(8,128)S(1)}, f32[4,16,64,128]{3,2,1,0:T(8,128)}, u32[]{:S(2)}) copy-start(f32[4,16,64,128]{3,2,1,0:T(8,128)} %get-tuple-element.74.slope) | copy-start | bytes 6291460
  54.1 16.3 %collective-permute-start.15 = (bf16[896,128]{1,0:T(8,128)(2,1)S(1)}, bf16[896,128]{1,0:T(8,128)(2,1)S(1)}, u32[]{:S(2)}, u32[]{:S(2)}) collective-permute-start(bf16[896,128]{1,0:T(8,128)(2,1)S(1)} %get-tuple-element.90), channel_id=1, source_target_pairs={{0,2},{1,3},{2,0},{3,1},{4,6},{5,7},{6,4},{7,5},{8,10},{9,11},{10,... | collective-permute-start | bytes 688136 | tf_op jit(solution)/shard_map/ppermute | solution.py:53
  59.1 16.6 %collective-permute-start.8 = (bf16[704,128]{1,0:T(8,128)(2,1)S(1)}, bf16[704,128]{1,0:T(8,128)(2,1)S(1)}, u32[]{:S(2)}, u32[]{:S(2)}) collective-permute-start(bf16[704,128]{1,0:T(8,128)(2,1)S(1)} %get-tuple-element.78), channel_id=1, source_target_pairs={{0,1},{1,0},{2,3},{3,2},{4,5},{5,4},{6,7},{7,6},{8,9},{9,8},{10,11... | collective-permute-start | bytes 540680 | tf_op jit(solution)/shard_map/ppermute | solution.py:53
  70.3 5.4 %collective-permute-start.9 = (bf16[448,128]{1,0:T(8,128)(2,1)S(1)}, bf16[448,128]{1,0:T(8,128)(2,1)S(1)}, u32[]{:S(2)}, u32[]{:S(2)}) collective-permute-start(bf16[448,128]{1,0:T(8,128)(2,1)S(1)} %get-tuple-element.79), channel_id=1, source_target_pairs={{0,1},{1,0},{2,3},{3,2},{4,5},{5,4},{6,7},{7,6},{8,9},{9,8},{10,11... | collective-permute-start | bytes 344072 | tf_op jit(solution)/shard_map/ppermute | solution.py:53
  71.0 8.0 %collective-permute-start.16 = (bf16[224,128]{1,0:T(8,128)(2,1)S(1)}, bf16[224,128]{1,0:T(8,128)(2,1)S(1)}, u32[]{:S(2)}, u32[]{:S(2)}) collective-permute-start(bf16[224,128]{1,0:T(8,128)(2,1)S(1)} %get-tuple-element.94), channel_id=1, source_target_pairs={{0,4},{1,5},{2,6},{3,7},{4,8},{5,9},{6,10},{7,11},{8,12},{9,13},{1... | collective-permute-start | bytes 172040 | tf_op jit(solution)/shard_map/ppermute | solution.py:58
  72.4 6.7 %collective-permute-start.17 = (bf16[224,128]{1,0:T(8,128)(2,1)S(1)}, bf16[224,128]{1,0:T(8,128)(2,1)S(1)}, u32[]{:S(2)}, u32[]{:S(2)}) collective-permute-start(bf16[224,128]{1,0:T(8,128)(2,1)S(1)} %get-tuple-element.95), channel_id=1, source_target_pairs={{0,8},{1,9},{2,10},{3,11},{4,12},{5,13},{6,14},{7,15},{8,0},{9,1},... | collective-permute-start | bytes 172040 | tf_op jit(solution)/shard_map/ppermute | solution.py:58
  73.8 5.3 %collective-permute-start.18 = (bf16[224,128]{1,0:T(8,128)(2,1)S(1)}, bf16[224,128]{1,0:T(8,128)(2,1)S(1)}, u32[]{:S(2)}, u32[]{:S(2)}) collective-permute-start(bf16[224,128]{1,0:T(8,128)(2,1)S(1)} %get-tuple-element.96), channel_id=1, source_target_pairs={{0,12},{1,13},{2,14},{3,15},{4,0},{5,1},{6,2},{7,3},{8,4},{9,5},{1... | collective-permute-start | bytes 172040 | tf_op jit(solution)/shard_map/ppermute | solution.py:58
  76.4 9.0 %collective-permute-start.10 = (bf16[576,128]{1,0:T(8,128)(2,1)S(1)}, bf16[576,128]{1,0:T(8,128)(2,1)S(1)}, u32[]{:S(2)}, u32[]{:S(2)}) collective-permute-start(bf16[576,128]{1,0:T(8,128)(2,1)S(1)} %get-tuple-element.85), channel_id=1, source_target_pairs={{0,2},{1,3},{2,0},{3,1},{4,6},{5,7},{6,4},{7,5},{8,10},{9,11},{10,... | collective-permute-start | bytes 442376 | tf_op jit(solution)/shard_map/ppermute | solution.py:53
  79.1 9.7 %collective-permute-start.21 = (bf16[224,128]{1,0:T(8,128)(2,1)S(1)}, bf16[224,128]{1,0:T(8,128)(2,1)S(1)}, u32[]{:S(2)}, u32[]{:S(2)}) collective-permute-start(bf16[224,128]{1,0:T(8,128)(2,1)S(1)} %shard_map.123.refs_0_), channel_id=1, source_target_pairs={{0,12},{1,13},{2,14},{3,15},{4,0},{5,1},{6,2},{7,3},{8,4},{9,5},{1... | collective-permute-start | bytes 172040 | tf_op jit(solution)/shard_map/ppermute | solution.py:58
  81.1 8.1 %collective-permute-start.20 = (bf16[224,128]{1,0:T(8,128)(2,1)S(1)}, bf16[224,128]{1,0:T(8,128)(2,1)S(1)}, u32[]{:S(2)}, u32[]{:S(2)}) collective-permute-start(bf16[224,128]{1,0:T(8,128)(2,1)S(1)} %shard_map.123.refs_0_), channel_id=1, source_target_pairs={{0,8},{1,9},{2,10},{3,11},{4,12},{5,13},{6,14},{7,15},{8,0},{9,1},... | collective-permute-start | bytes 172040 | tf_op jit(solution)/shard_map/ppermute | solution.py:58
  81.7 7.5 %collective-permute-start.19 = (bf16[224,128]{1,0:T(8,128)(2,1)S(1)}, bf16[224,128]{1,0:T(8,128)(2,1)S(1)}, u32[]{:S(2)}, u32[]{:S(2)}) collective-permute-start(bf16[224,128]{1,0:T(8,128)(2,1)S(1)} %shard_map.123.refs_0_), channel_id=1, source_target_pairs={{0,4},{1,5},{2,6},{3,7},{4,8},{5,9},{6,10},{7,11},{8,12},{9,13},{1... | collective-permute-start | bytes 172040 | tf_op jit(solution)/shard_map/ppermute | solution.py:58
  85.5 7.2 %collective-permute-start.13 = (bf16[576,128]{1,0:T(8,128)(2,1)S(1)}, bf16[576,128]{1,0:T(8,128)(2,1)S(1)}, u32[]{:S(2)}, u32[]{:S(2)}) collective-permute-start(bf16[576,128]{1,0:T(8,128)(2,1)S(1)} %shard_map.118.refs_0_), channel_id=1, source_target_pairs={{0,12},{1,13},{2,14},{3,15},{4,0},{5,1},{6,2},{7,3},{8,4},{9,5},{1... | collective-permute-start | bytes 442376 | tf_op jit(solution)/shard_map/ppermute | solution.py:58
  88.8 11.8 %collective-permute-start.12 = (bf16[576,128]{1,0:T(8,128)(2,1)S(1)}, bf16[576,128]{1,0:T(8,128)(2,1)S(1)}, u32[]{:S(2)}, u32[]{:S(2)}) collective-permute-start(bf16[576,128]{1,0:T(8,128)(2,1)S(1)} %shard_map.118.refs_0_), channel_id=1, source_target_pairs={{0,8},{1,9},{2,10},{3,11},{4,12},{5,13},{6,14},{7,15},{8,0},{9,1},... | collective-permute-start | bytes 442376 | tf_op jit(solution)/shard_map/ppermute | solution.py:58
  88.8 11.8 %collective-permute-start.11 = (bf16[576,128]{1,0:T(8,128)(2,1)S(1)}, bf16[576,128]{1,0:T(8,128)(2,1)S(1)}, u32[]{:S(2)}, u32[]{:S(2)}) collective-permute-start(bf16[576,128]{1,0:T(8,128)(2,1)S(1)} %shard_map.118.refs_0_), channel_id=1, source_target_pairs={{0,4},{1,5},{2,6},{3,7},{4,8},{5,9},{6,10},{7,11},{8,12},{9,13},{1... | collective-permute-start | bytes 442376 | tf_op jit(solution)/shard_map/ppermute | solution.py:58
  89.8 14.6 %collective-permute-start.22 = (bf16[4,224,128]{2,1,0:T(8,128)(2,1)S(1)}, bf16[4,224,128]{2,1,0:T(8,128)(2,1)S(1)}, u32[]{:S(2)}, u32[]{:S(2)}) collective-permute-start(bf16[4,224,128]{2,1,0:T(8,128)(2,1)S(1)} %shard_map.124.mine), channel_id=1, source_target_pairs={{0,2},{1,3},{2,0},{3,1},{4,6},{5,7},{6,4},{7,5},{8,10},{9,11},{10,... | collective-permute-start | bytes 688136 | tf_op jit(solution)/shard_map/ppermute | solution.py:53
  100.7 6.6 %collective-permute-start.23 = (bf16[576,128]{1,0:T(8,128)(2,1)S(1)}, bf16[576,128]{1,0:T(8,128)(2,1)S(1)}, u32[]{:S(2)}, u32[]{:S(2)}) collective-permute-start(bf16[576,128]{1,0:T(8,128)(2,1)S(1)} %shard_map.119.mine), channel_id=1, source_target_pairs={{0,2},{1,3},{2,0},{3,1},{4,6},{5,7},{6,4},{7,5},{8,10},{9,11},{10,... | collective-permute-start | bytes 442376 | tf_op jit(solution)/shard_map/ppermute | solution.py:53
  105.0 8.6 %collective-permute-start.25 = (bf16[2,896,128]{2,1,0:T(8,128)(2,1)S(1)}, bf16[2,896,128]{2,1,0:T(8,128)(2,1)S(1)}, u32[]{:S(2)}, u32[]{:S(2)}) collective-permute-start(bf16[2,896,128]{2,1,0:T(8,128)(2,1)S(1)} %shard_map.125.mine), channel_id=1, source_target_pairs={{0,1},{1,0},{2,3},{3,2},{4,5},{5,4},{6,7},{7,6},{8,9},{9,8},{10,11... | collective-permute-start | bytes 1376264 | tf_op jit(solution)/shard_map/ppermute | solution.py:53
  107.8 3.7 %collective-permute-start.24 = (bf16[2,576,128]{2,1,0:T(8,128)(2,1)S(1)}, bf16[2,576,128]{2,1,0:T(8,128)(2,1)S(1)}, u32[]{:S(2)}, u32[]{:S(2)}) collective-permute-start(bf16[2,576,128]{2,1,0:T(8,128)(2,1)S(1)} %shard_map.126.mine), channel_id=1, source_target_pairs={{0,1},{1,0},{2,3},{3,2},{4,5},{5,4},{6,7},{7,6},{8,9},{9,8},{10,11... | collective-permute-start | bytes 884744 | tf_op jit(solution)/shard_map/ppermute | solution.py:53

commit v3 on v2

--- a/solution.py
+++ b/solution.py
@@ -51,11 +51,6 @@
 def swapped(array, stride):
     size = lax.axis_size(AXIS)
     return lax.ppermute(array, AXIS, [(i, i ^ stride) for i in range(size)])
-
-
-def shifted(array, stride, by):
-    size = lax.axis_size(AXIS)
-    return lax.ppermute(array, AXIS, [(i, (i + by * stride) % size) for i in range(size)])
 
 
 def sigmoid(value):
@@ -208,34 +203,33 @@
             for side, pre in enumerate(fine_pair(sources[r : r + 3], w_first, col)):
                 sigma = sigmoid(pre)
                 act = pre * sigma
-                slope = sigma + act * (1.0 - sigma)
                 if r == 0:
                     act = jnp.where(flags[0] > 0, act, 0.0)
-                    slope = jnp.where(flags[0] > 0, slope, 0.0)
                 if r == 3:
                     act = jnp.where(flags[1] > 0, act, 0.0)
-                    slope = jnp.where(flags[1] > 0, slope, 0.0)
                 firsts[r][col + side] = act.astype(BF)
-                slope1[r, col + side] = slope
+                if 1 <= r <= 2:
+                    slope1[r - 1, col + side] = sigma + act * (1.0 - sigma)
     at = lax.broadcasted_iota(jnp.int32, (deep, deep), 1)
     q = lax.broadcasted_iota(jnp.int32, (deep, deep), 0)
     perm = (at == 2 * lax.rem(q, half) + (q >= half).astype(jnp.int32)).astype(BF)
     for r in range(2):
         rows = firsts[r : r + 3]
         for col in range(0, num, 2):
-            acts = []
             for side, pre in enumerate(fine_pair(rows, w_second, col)):
                 sigma = sigmoid(pre)
                 act = pre * sigma
-                acts.append(act.astype(BF))
+                rows_scr[r, col + side] = act.astype(BF)
                 slope2[r, col + side] = sigma + act * (1.0 - sigma)
-            both = jnp.concatenate(acts, 0)
-            wide = both.shape[0]
-            turned = dot(perm, both, NT).astype(BF)
-            at = slice(col // 2 * half, (col // 2 + 1) * half)
+    wide = 2 * chan
+    for r in range(2):
+        turned = dot(perm, rows_scr[r].reshape(num * chan, deep), NT).astype(BF)
+        for q in range(num // 2):
             for c in range(2):
                 lanes = slice((2 * r + c) * wide, (2 * r + c + 1) * wide)
-                act_t[at, lanes] = turned[c * half : (c + 1) * half]
+                act_t[q * half : (q + 1) * half, lanes] = turned[
+                    c * half : (c + 1) * half, q * wide : (q + 1) * wide
+                ]
     pooled[...] = dot(act_t[...], w_down[...]).astype(BF)
 
 
@@ -260,17 +254,16 @@
         for j in range(18):
             value = acc[j * piece : (j + 1) * piece, k * chan : (k + 1) * chan]
             put(halves, 18 * k + j, value)
-    for j in range(54, 2 * halves.shape[1] // piece):
-        put(halves, j, jnp.zeros((piece, chan), BF))
     deal(halves, flags[2], mine, other)
 
 
-def second_delta_body(deep, before, own, after, w, w_up, skip, slope, pg, delta):
+def second_delta_body(deep, before, own, after, w, w_up, skip, slope, pg, d0, d1):
     value = coarse_conv([before, own, after], w, deep, NT).astype(BF)
     pg[...] = value
     turned = value.T
-    half = delta.shape[2]
-    fine = delta.shape[3]
+    outs = [d0, d1]
+    half = d0.shape[1]
+    fine = d0.shape[2]
     row = lax.broadcasted_iota(jnp.int32, (fine, 4 * fine), 0)
     lane = lax.broadcasted_iota(jnp.int32, (fine, 4 * fine), 1)
     odd = (lax.rem(lane, 2 * fine) >= fine).astype(jnp.int32)
@@ -289,11 +282,11 @@
                     rows = slice((2 * a + b) * half, (2 * a + b + 1) * half)
                     at = 4 * m + 2 * s + b
                     total = back[rows, s * fine : (s + 1) * fine] + skip[a, at].astype(F32)
-                    delta[a, at] = (total * slope[a, at]).astype(BF)
-
-
-def second_grad_body(flags, s0, s1, s2, s3, delta, act_t, pg, mine, other, a_scr, b_scr, halves):
-    fine_grad([s0, s1, s2, s3], [delta.at[0], delta.at[1]], a_scr, b_scr, halves)
+                    outs[a][at] = (total * slope[a, at]).astype(BF)
+
+
+def second_grad_body(flags, s0, s1, s2, s3, d0, d1, act_t, pg, mine, other, a_scr, b_scr, halves):
+    fine_grad([s0, s1, s2, s3], [d0, d1], a_scr, b_scr, halves)
     down = dot(act_t[...], pg[...], TN).astype(BF)
     chan = s0.shape[1]
     for j in range(8):
@@ -308,32 +301,22 @@
 
 
 def first_delta_body(
-    flags, before, own, after, w, slope, s0, s1, s2, s3, e1, e2, mine, other, a_scr, b_scr, halves
+    flags, before, d0, d1, after, w, slope, s0, s1, s2, s3, e1, e2, mine, other, a_scr, b_scr, halves
 ):
-    rows = [before.at[1], own.at[0], own.at[1], after.at[0]]
-    back_row(rows[:3], w, slope, 1, e1)
-    back_row(rows[1:], w, slope, 2, e2)
+    rows = [before, d0, d1, after]
+    back_row(rows[:3], w, slope, 0, e1)
+    back_row(rows[1:], w, slope, 1, e2)
     fine_grad([s0, s1, s2, s3], [e1, e2], a_scr, b_scr, halves)
     deal(halves, flags[2], mine, other)
 
 
-def input_grad_body(before, own, after, w_second, slope, e1, e2, w, out, scr, e0, e3):
-    back_row([before.at[0], before.at[1], own.at[0]], w_second, slope, 0, e0)
-    back_row([own.at[1], after.at[0], after.at[1]], w_second, slope, 3, e3)
-    rows = [e0, e1, e2, e3]
+def input_grad_body(before, e1, e2, after, w, out, scr):
+    rows = [before, e1, e2, after]
     for r in range(2):
         for col in range(0, e1.shape[0], 2):
             for side, value in enumerate(fine_pair(rows[r : r + 3], w, col)):
                 scr[col + side] = value
         out[r] = pltpu.einshape("wcd->cwd", scr[...])
-
-
-def added(*refs):
-    values = [ref[...].astype(F32) for ref in refs]
-    while len(values) > 1:
-        half = len(values) // 2
-        values = [values[t] + values[t + half] for t in range(half)]
-    return values[0]
 
 
 def split_body(count, flags, *refs):
@@ -356,25 +339,8 @@
         at += half
 
 
-def chunk_body(flags, keep, got, *refs):
-    *outs, scr = refs
-    num, rows, _ = scr.shape
-    for i in range(num):
-        at = slice(i * rows, (i + 1) * rows)
-        scr[i] = (keep[at, :].astype(F32) + got[at, :].astype(F32)).astype(BF)
-    for t, out in enumerate(outs):
-        out[...] = scr[lax.rem(flags[4] + t, num)]
-
-
-def gather_body(flags, *refs):
-    *parts, out = refs
-    num = out.shape[0]
-    for t, part in enumerate(parts):
-        out[lax.rem(flags[4] + num - t, num)] = part[...]
-
-
-def add_body(*refs):
-    refs[-1][...] = added(*refs[:-1]).astype(BF)
+def add_body(mine, got, out):
+    out[...] = (mine[...].astype(F32) + got[...].astype(F32)).astype(BF)
 
 
 def order_body(flags, mine, got, out):
@@ -445,25 +411,8 @@
     )
 
 
-def summed(*parts):
-    return call(add_body, [(parts[0].shape, BF)], *parts)[0]
-
-
-def chunks(flags, keep, got):
-    num = lax.axis_size(AXIS) // 4
-    shape = (keep.shape[0] // num, keep.shape[1])
-    return call(
-        chunk_body, [(shape, BF)] * num, flags, keep, got, smem=1,
-        scratch=(pltpu.VMEM((num,) + shape, BF),),
-    )
-
-
-def sent(parts):
-    return [shifted(part, 4, t) for t, part in enumerate(parts, 1)]
-
-
-def gathered(flags, parts):
-    return call(gather_body, [((len(parts),) + parts[0].shape, BF)], flags, *parts, smem=1)[0]
+def summed(mine, got):
+    return call(add_body, [(mine.shape, BF)], mine, got)[0]
 
 
 def paired(flags, part, got):
@@ -480,7 +429,7 @@
     size = num // 2 * half
     index = lax.axis_index(AXIS)
     flags = jnp.stack(
-        [index, lax.axis_size(AXIS) - 1 - index, index % 2, (index // 2) % 2, index // 4]
+        [index, lax.axis_size(AXIS) - 1 - index, index % 2, (index // 2) % 2]
     ).astype(jnp.int32)
 
     fine = ((num, chan, deep), BF)
@@ -500,7 +449,7 @@
     )
     v0, v3, f0, f1, f2, f3, slope1, slope2, act_t, pooled = call(
         forward_kernel,
-        [fine] * 6 + [((4, num, chan, deep), F32), (two[0], F32), ((size, 8 * chan), BF), coarse],
+        [fine] * 6 + [(two[0], F32)] * 2 + [((size, 8 * chan), BF), coarse],
         flags, before, v1, v2, after, first_f, second_f, down_f,
         scratch=(pltpu.VMEM(*two),),
         smem=1,
@@ -519,52 +468,59 @@
         return pltpu.VMEM((2, blocks // 2 * chan, 2 * chan), BF)
 
     a_mine, a_other = call(
-        functools.partial(coarse_grad_body, half), [dealt(56)] * 2, flags, *rows, delta,
-        scratch=(halves(56),), smem=1,
-    )
-    a_keep, a_send = halved(flags, (a_mine, swapped(a_other, 1)))
-    a_got = swapped(a_send, 2)
-    pg, second = call(
-        functools.partial(second_delta_body, half), [coarse, two],
+        functools.partial(coarse_grad_body, half), [dealt(54)] * 2, flags, *rows, delta,
+        scratch=(halves(54),), smem=1,
+    )
+    pg, d0, d1 = call(
+        functools.partial(second_delta_body, half), [coarse, fine, fine],
         *delta_rows, coarse_b, down_b, skip, slope2,
     )
-    second_rows = [from_before(second), second, from_after(second)]
-    a_chunks = chunks(flags, a_keep, tied(a_got, second))
+    second_rows = [from_before(d1), d0, d1, from_after(d0)]
     b_mine, b_other = call(
-        second_grad_body, [dealt(22)] * 2, flags, f0, f1, f2, f3, second, act_t, pg,
+        second_grad_body, [dealt(22)] * 2, flags, f0, f1, f2, f3, d0, d1, act_t, pg,
         scratch=fine_grad_scratch(num, chan, deep) + (halves(22),), smem=1,
     )
+    a_keep, a_send = halved(flags, (a_mine, tied(swapped(a_other, 1), b_mine)))
     b_got = swapped(b_other, 1)
-    a_got = sent(a_chunks[1:])
     e1, e2, c_mine, c_other = call(
         first_delta_body, [fine, fine] + [dealt(14)] * 2,
         flags, *second_rows, second_b, slope1, v0, v1, v2, v3,
         scratch=fine_grad_scratch(num, chan, deep) + (halves(14),), smem=1,
     )
-    a_part = summed(tied(a_chunks[0], c_mine), *a_got)
-    a_got = sent([a_part] * len(a_got))
+    a_got = swapped(tied(a_send, c_mine), 2)
     keep, send = halved(flags, (b_mine, b_got), (c_mine, swapped(c_other, 1)))
     got = swapped(send, 2)
+    first_rows = [from_before(tied(e2, keep)), e1, e2, from_after(tied(e1, keep))]
+    a_part, part = summed(a_keep, tied(a_got, keep)), None
+    strides = []
+    stride = 4
+    while stride < lax.axis_size(AXIS):
+        strides.append(stride)
+        stride *= 2
+    for stride in strides:
+        a_got = swapped(a_part, stride)
+        part = summed(keep, tied(got, a_part)) if part is None else summed(part, tied(got, a_part))
+        got = swapped(part, stride)
+        a_part = summed(a_part, tied(a_got, part))
+    a_got = swapped(a_part, 2)
     (input_grad,) = call(
         input_grad_body, [((2, chan, num, deep), F32)],
-        tied(second_rows[0], keep), *second_rows[1:], second_b, slope1, e1, e2, first_b,
-        scratch=(pltpu.VMEM((num, chan, deep), F32), pltpu.VMEM(*fine), pltpu.VMEM(*fine)),
-    )
-    part = summed(keep, tied(got, input_grad))
-    got = sent([part] * (lax.axis_size(AXIS) // 4 - 1))
-    a_part = gathered(flags, [tied(a_part, part)] + a_got)
-    a_got = swapped(a_part, 2)
-    a_pair = paired(flags, a_part, a_got)
+        tied(first_rows[0], a_part), *first_rows[1:], first_b,
+        scratch=(pltpu.VMEM((num, chan, deep), F32),),
+    )
+    part = summed(part, tied(got, a_part, input_grad))
+    got = swapped(part, 2)
+    a_pair = paired(flags, tied(a_part, part), a_got)
     a_got = swapped(a_pair, 1)
-    part = summed(part, *got)
-    pair = paired(flags, tied(part, a_pair), swapped(part, 2))
+    pair = paired(flags, tied(part, a_pair), got)
     (coarse_out,) = call(
         coarse_unpack, [((27, wide, wide), F32)], flags, tied(a_pair, pair), a_got,
-        smem=1, scratch=(halves(56),),
+        smem=1, scratch=(halves(54),),
     )
     fine_out = ((27, chan, chan), F32)
     first_out, second_out, down_out = call(
-        fine_unpack, [fine_out, fine_out, ((8, chan, wide), F32)], flags, pair, swapped(pair, 1),
+        fine_unpack, [fine_out, fine_out, ((8, chan, wide), F32)],
+        flags, tied(pair, coarse_out), swapped(pair, 1),
         smem=1, scratch=(halves(22), halves(14)),
     )
     return (

time: 116 us -> 109 us (0.940)
  Pallas kernels: 34.2 us -> 27 us
  waiting for transfers between devices: 22 us -> 24 us
  starting transfers between devices: 53.2 us -> 51.7 us
    ppermute x9 -> x13, waiting for transfers between devices: 1.23 us -> 14.8 us  [swapped(): return lax.ppermute(array, AXIS, [(i, i ^ stride) for i in range(size)])]
    ppermute x9 -> x0, starting transfers between devices: 11 us -> none  [shifted(): lax.ppermute(array, AXIS, [(i, (i + by * stride) % size) for i in range(s...]
    ppermute x9 -> x0, waiting for transfers between devices: 7.94 us -> none  [shifted(): lax.ppermute(array, AXIS, [(i, (i + by * stride) % size) for i in range(s...]
    ppermute x4 -> x5, waiting for transfers between devices: 12.2 us -> 4.63 us  [from_before(): return lax.ppermute(array, AXIS, neighbours(array)[0])]
    pallas_call x19 -> x20, Pallas kernels: 34.2 us -> 27 us  [call(): pl.pallas_call(body, out_shape=[jax.ShapeDtypeStruct(s, d) for s, d in ou...]
    ppermute x4 -> x5, starting transfers between devices: 17.6 us -> 21.6 us  [from_before(): return lax.ppermute(array, AXIS, neighbours(array)[0])]
    ppermute x4 -> x5, waiting for transfers between devices: 0.72 us -> 4.6 us  [from_after(): return lax.ppermute(array, AXIS, neighbours(array)[1])]
    ppermute x9 -> x13, starting transfers between devices: 16.9 us -> 20.2 us  [swapped(): return lax.ppermute(array, AXIS, [(i, i ^ stride) for i in range(size)])]
  transfers between devices with their start and end apart: 26 -> 23, of which waited for: 7 -> 13; matrix products, arithmetic and copies ran while one was open for 0% -> 0% of each run, Pallas kernels for 18% -> 16%
where the time goes in v3:
time: 109 us
  starting transfers between devices  51.7 us (47%)
  Pallas kernels  27 us (25%)
  waiting for transfers between devices  24 us (22%)
  local copies, waits for them, and re-layouts  5.01 us (5%)
    pallas_call x20, Pallas kernels, call(): pl.pallas_call(body, out_shape=[jax.ShapeDtypeStruct(s, d) for s, d in ou...  27 us
    ppermute x5, starting transfers between devices, from_before(): return lax.ppermute(array, AXIS, neighbours(array)[0])  21.6 us
    ppermute x13, starting transfers between devices, swapped(): return lax.ppermute(array, AXIS, [(i, i ^ stride) for i in range(size)])  20.2 us
    ppermute x13, waiting for transfers between devices, swapped(): return lax.ppermute(array, AXIS, [(i, i ^ stride) for i in range(size)])  14.8 us
    ppermute x5, starting transfers between devices, from_after(): return lax.ppermute(array, AXIS, neighbours(array)[1])  9.9 us
    unnamed x14, local copies, waits for them, and re-layouts  5.01 us
    ppermute x5, waiting for transfers between devices, from_before(): return lax.ppermute(array, AXIS, neighbours(array)[0])  4.63 us
    ppermute x5, waiting for transfers between devices, from_after(): return lax.ppermute(array, AXIS, neighbours(array)[1])  4.6 us
  transfers between devices with their start and end apart: 23, of which 13 were waited for; matrix products, arithmetic and copies ran while one was open for 0% of the time, Pallas kernels for 16%

profile of v3, /device:TPU:1, one launch (start us, length us, event | category | flops | bytes accessed | tf_op | source)
XLA Modules:
  0.0 108.7 jit_solution(17539827800068133824)
XLA Ops:
  0.6 4.5 %collective-permute-start = (bf16[2,64,16,128]{3,2,1,0:T(8,128)(2,1)}, bf16[2,64,16,128]{3,2,1,0:T(8,128)(2,1)S(1)}, u32[]{:S(2)}, u32[]{:S(2)}) collective-permute-start(bf16[2,64,16,128]{3,2,1,0:T(8,128)(2,1)} %volume.1), channel_id=1, source_target_pairs={{0,1},{1,2},{2,3},{3,4},{4,5},{5,6},{6,7},{7,8},{8,9},{9,10},{10,1... | collective-permute-start | bytes 1572872 | tf_op jit(solution)/shard_map/ppermute | solution.py:44
  5.2 1.9 %collective-permute-start.1 = (bf16[2,64,16,128]{3,2,1,0:T(8,128)(2,1)}, bf16[2,64,16,128]{3,2,1,0:T(8,128)(2,1)S(1)}, u32[]{:S(2)}, u32[]{:S(2)}) collective-permute-start(bf16[2,64,16,128]{3,2,1,0:T(8,128)(2,1)} %volume.1), channel_id=1, source_target_pairs={{1,0},{2,1},{3,2},{4,3},{5,4},{6,5},{7,6},{8,7},{9,8},{10,9},{11,1... | collective-permute-start | bytes 1572872 | tf_op jit(solution)/shard_map/ppermute | solution.py:48
  7.2 1.0 copy-done
  8.2 1.0 copy-done.1
  9.2 1.0 copy-done.2
  10.2 1.0 copy-done.3
  11.3 0.9 copy-done.4
  12.2 2.3 %shard_map.110 = (bf16[16,64,128]{2,1,0:T(8,128)(2,1)S(1)}, bf16[16,64,128]{2,1,0:T(8,128)(2,1)S(1)}, bf16[2,16,64,128]{3,2,1,0:T(8,128)(2,1)S(1)}, bf16[192,576...) custom-call(bf16[2,64,16,128]{3,2,1,0:T(8,128)(2,1)S(1)} %copy-done., ...), custom_call_target="tpu_custom_call" | custom-call | flops 1000000000 | bytes 1048576 | tf_op jit(solution)/shard_map/pallas_call | solution.py:25
  14.5 0.1 pad_add_fusion.flags
  14.6 2.6 %collective-permute-done.before = bf16[2,64,16,128]{3,2,1,0:T(8,128)(2,1)S(1)} collective-permute-done((bf16[2,64,16,128]{3,2,1,0:T(8,128)(2,1)}, bf16[2,64,16,128]{3,2,1,0:T(8,128)(2,1)S(1)}, u32[]{:S(2)}, u32[]{:S(2)}) %collective-permute-start) | collective-permute-done | bytes 524320 | tf_op jit(solution)/shard_map/ppermute | solution.py:44
  17.2 5.6 %shard_map.111 = (bf16[16,64,128]{2,1,0:T(8,128)(2,1)S(1)}, bf16[16,64,128]{2,1,0:T(8,128)(2,1)S(1)}, bf16[16,64,128]{2,1,0:T(8,128)(2,1)S(1)}, bf16[16,64,128]{...) custom-call(s32[4]{0:T(128)S(1)} %pad_add_fusion.flags, ...), custom_call_target="tpu_custom_call" | custom-call | flops 1000000000 | bytes 1048576 | tf_op jit(solution)/shard_map/pallas_call | solution.py:25
  22.8 1.9 %collective-permute-start.3 = (bf16[512,128]{1,0:T(8,128)(2,1)S(1)}, bf16[512,128]{1,0:T(8,128)(2,1)S(1)}, u32[]{:S(2)}, u32[]{:S(2)}) collective-permute-start(bf16[512,128]{1,0:T(8,128)(2,1)S(1)} %get-tuple-element.64.own), channel_id=1, source_target_pairs={{1,0},{2,1},{3,2},{4,3},{5,4},{6,5},{7,6},{8,7},{9,8},{10,9},{11,1... | collective-permute-start | bytes 393224 | tf_op jit(solution)/shard_map/ppermute | solution.py:48
  24.8 4.3 %collective-permute-start.2 = (bf16[512,128]{1,0:T(8,128)(2,1)S(1)}, bf16[512,128]{1,0:T(8,128)(2,1)S(1)}, u32[]{:S(2)}, u32[]{:S(2)}) collective-permute-start(bf16[512,128]{1,0:T(8,128)(2,1)S(1)} %get-tuple-element.64.own), channel_id=1, source_target_pairs={{0,1},{1,2},{2,3},{3,4},{4,5},{5,6},{6,7},{7,8},{8,9},{9,10},{10,1... | collective-permute-start | bytes 393224 | tf_op jit(solution)/shard_map/ppermute | solution.py:44
  29.1 0.7 collective-permute-done.3.after
  29.8 1.2 %collective-permute-done.2.before = bf16[512,128]{1,0:T(8,128)(2,1)S(1)} collective-permute-done((bf16[512,128]{1,0:T(8,128)(2,1)S(1)}, bf16[512,128]{1,0:T(8,128)(2,1)S(1)}, u32[]{:S(2)}, u32[]{:S(2)}) %collective-permute-start.2) | collective-permute-done | bytes 131104 | tf_op jit(solution)/shard_map/ppermute | solution.py:44
  31.0 0.9 shard_map.112.own.delta
  31.9 0.0 copy-start.6
  31.9 2.1 %collective-permute-start.5 = (bf16[512,128]{1,0:T(8,128)(2,1)S(1)}, bf16[512,128]{1,0:T(8,128)(2,1)S(1)}, u32[]{:S(2)}, u32[]{:S(2)}) collective-permute-start(bf16[512,128]{1,0:T(8,128)(2,1)S(1)} %shard_map.112.own.delta), channel_id=1, source_target_pairs={{1,0},{2,1},{3,2},{4,3},{5,4},{6,5},{7,6},{8,7},{9,8},{10,9},{11,1... | collective-permute-start | bytes 393224 | tf_op jit(solution)/shard_map/ppermute | solution.py:48
  33.9 4.4 %collective-permute-start.4 = (bf16[512,128]{1,0:T(8,128)(2,1)S(1)}, bf16[512,128]{1,0:T(8,128)(2,1)S(1)}, u32[]{:S(2)}, u32[]{:S(2)}) collective-permute-start(bf16[512,128]{1,0:T(8,128)(2,1)S(1)} %shard_map.112.own.delta), channel_id=1, source_target_pairs={{0,1},{1,2},{2,3},{3,4},{4,5},{5,6},{6,7},{7,8},{8,9},{9,10},{10,1... | collective-permute-start | bytes 393224 | tf_op jit(solution)/shard_map/ppermute | solution.py:44
  38.3 1.4 %shard_map.117 = (bf16[1728,128]{1,0:T(8,128)(2,1)S(1)}, bf16[1728,128]{1,0:T(8,128)(2,1)S(1)}) custom-call(s32[4]{0:T(128)S(1)} %pad_add_fusion.flags, bf16[512,128]{1,0:T(8,128)(2,1)S(1)} %collective-permute-done.2.before, bf16[512,128]{1,0:T(8,128)(2,1)S(1)} %get-tuple-element.64.own, bf16[512,128]{1,0:T(8,128)(2,1)S(1)} %collective-permute-done.3.after, ...), custom_call_target="tpu_custom_call" | custom-call | flops 1000000000 | bytes 1048576 | tf_op jit(solution)/shard_map/pallas_call | solution.py:25
  39.7 0.1 collective-permute-start.11
  39.8 0.8 collective-permute-done.4.before
  40.6 1.5 %shard_map.113 = (bf16[512,128]{1,0:T(8,128)(2,1)S(1)}, bf16[16,64,128]{2,1,0:T(8,128)(2,1)S(1)}, bf16[16,64,128]{2,1,0:T(8,128)(2,1)S(1)}) custom-call(bf16[512,128]{1,0:T(8,128)(2,1)S(1)} %collective-permute-done.4.before, bf16[512,128]{1,0:T(8,128)(2,1)S(1)} %shard_map.112.own.delta, bf16[512,128]{1,0:T(8,128)(2,1)S(1)} %collective-permute-done.5.after, ...), custom_call_target="tpu_custom_call" | custom-call | flops 1000000000 | bytes 1048576 | tf_op jit(solution)/shard_map/pallas_call | solution.py:25
  42.1 4.4 %collective-permute-start.6 = (bf16[16,64,128]{2,1,0:T(8,128)(2,1)S(1)}, bf16[16,64,128]{2,1,0:T(8,128)(2,1)S(1)}, u32[]{:S(2)}, u32[]{:S(2)}) collective-permute-start(bf16[16,64,128]{2,1,0:T(8,128)(2,1)S(1)} %get-tuple-element.70.d1), channel_id=1, source_target_pairs={{0,1},{1,2},{2,3},{3,4},{4,5},{5,6},{6,7},{7,8},{8,9},{9,10},{10,1... | collective-permute-start | bytes 786440 | tf_op jit(solution)/shard_map/ppermute | solution.py:44
  46.5 2.1 %collective-permute-start.7 = (bf16[16,64,128]{2,1,0:T(8,128)(2,1)S(1)}, bf16[16,64,128]{2,1,0:T(8,128)(2,1)S(1)}, u32[]{:S(2)}, u32[]{:S(2)}) collective-permute-start(bf16[16,64,128]{2,1,0:T(8,128)(2,1)S(1)} %get-tuple-element.71.d0), channel_id=1, source_target_pairs={{1,0},{2,1},{3,2},{4,3},{5,4},{6,5},{7,6},{8,7},{9,8},{10,9},{11,1... | collective-permute-start | bytes 786440 | tf_op jit(solution)/shard_map/ppermute | solution.py:48
  48.6 2.4 %shard_map.115 = (bf16[704,128]{1,0:T(8,128)(2,1)S(1)}, bf16[704,128]{1,0:T(8,128)(2,1)S(1)}) custom-call(s32[4]{0:T(128)S(1)} %pad_add_fusion.flags, bf16[16,64,128]{2,1,0:T(8,128)(2,1)S(1)} %get-tuple-element.77.s0, bf16[16,64,128]{2,1,0:T(8,128)(2,1)S(1)} %get-tuple-element.78.s1, bf16[16,64,128]{2,1,0:T(8,128)(2,1)S(1)} %get-tuple-element.79.s2, ...), custom_call_target="tpu_custom_call" | custom-call | flops 1000000000 | bytes 1048576 | tf_op jit(solution)/shard_map/pallas_call | solution.py:25
  51.0 0.1 collective-permute-start.8
  51.1 0.0 collective-permute-done.6.before
  51.1 3.1 %collective-permute-done.7.after = bf16[16,64,128]{2,1,0:T(8,128)(2,1)S(1)} collective-permute-done((bf16[16,64,128]{2,1,0:T(8,128)(2,1)S(1)}, bf16[16,64,128]{2,1,0:T(8,128)(2,1)S(1)}, u32[]{:S(2)}, u32[]{:S(2)}) %collective-permute-start.7) | collective-permute-done | bytes 262176 | tf_op jit(solution)/shard_map/ppermute | solution.py:48
  54.2 3.6 %shard_map.114 = (bf16[16,64,128]{2,1,0:T(8,128)(2,1)S(1)}, bf16[16,64,128]{2,1,0:T(8,128)(2,1)S(1)}, bf16[448,128]{1,0:T(8,128)(2,1)S(1)}, bf16[448,128]{1,0:T(8,128)(2,1)S(1)}) custom-call(s32[4]{0:T(128)S(1)} %pad_add_fusion.flags, bf16[16,64,128]{2,1,0:T(8,128)(2,1)S(1)} %collective-permute-done.6.before, bf16[16,64,128]{2,1,0:T(8,128)(2,1)S(1)} %get-tuple-element.71.d0, ...), custom_call_target="tpu_custom_call" | custom-call | flops 1000000000 | bytes 1048576 | tf_op jit(solution)/shard_map/pallas_call | solution.py:25
  57.8 0.0 collective-permute-done.11.refs_1_
  57.8 0.7 shard_map.118
  58.5 3.5 %collective-permute-start.12 = (bf16[864,128]{1,0:T(8,128)(2,1)S(1)}, bf16[864,128]{1,0:T(8,128)(2,1)S(1)}, u32[]{:S(2)}, u32[]{:S(2)}) collective-permute-start(bf16[864,128]{1,0:T(8,128)(2,1)S(1)} %get-tuple-element.94), channel_id=1, source_target_pairs={{0,2},{1,3},{2,0},{3,1},{4,6},{5,7},{6,4},{7,5},{8,10},{9,11},{10,... | collective-permute-start | bytes 663560 | tf_op jit(solution)/shard_map/ppermute | solution.py:53
  62.1 0.0 collective-permute-start.9
  62.1 0.0 collective-permute-done.8.refs_2_
  62.1 1.3 %collective-permute-done.9.refs_3_ = bf16[448,128]{1,0:T(8,128)(2,1)S(1)} collective-permute-done((bf16[448,128]{1,0:T(8,128)(2,1)S(1)}, bf16[448,128]{1,0:T(8,128)(2,1)S(1)}, u32[]{:S(2)}, u32[]{:S(2)}) %collective-permute-start.9) | collective-permute-done | bytes 114720 | tf_op jit(solution)/shard_map/ppermute | solution.py:53
  63.4 0.7 shard_map.116
  64.1 0.1 collective-permute-start.14
  64.2 1.2 %collective-permute-done.12.got = bf16[864,128]{1,0:T(8,128)(2,1)S(1)} collective-permute-done((bf16[864,128]{1,0:T(8,128)(2,1)S(1)}, bf16[864,128]{1,0:T(8,128)(2,1)S(1)}, u32[]{:S(2)}, u32[]{:S(2)}) %collective-permute-start.12) | collective-permute-done | bytes 221216 | tf_op jit(solution)/shard_map/ppermute | solution.py:53
  65.4 0.1 shard_map.119.mine
  65.5 3.1 %collective-permute-start.13 = (bf16[864,128]{1,0:T(8,128)(2,1)S(1)}, bf16[864,128]{1,0:T(8,128)(2,1)S(1)}, u32[]{:S(2)}, u32[]{:S(2)}) collective-permute-start(bf16[864,128]{1,0:T(8,128)(2,1)S(1)} %shard_map.119.mine), channel_id=1, source_target_pairs={{0,4},{1,5},{2,6},{3,7},{4,0},{5,1},{6,2},{7,3},{8,12},{9,13},{10,... | collective-permute-start | bytes 663560 | tf_op jit(solution)/shard_map/ppermute | solution.py:53
  68.6 0.8 collective-permute-done.14.got
  69.5 2.5 %collective-permute-start.16 = (bf16[576,128]{1,0:T(8,128)(2,1)S(1)}, bf16[576,128]{1,0:T(8,128)(2,1)S(1)}, u32[]{:S(2)}, u32[]{:S(2)}) collective-permute-start(bf16[576,128]{1,0:T(8,128)(2,1)S(1)} %shard_map.120.mine), channel_id=1, source_target_pairs={{0,4},{1,5},{2,6},{3,7},{4,0},{5,1},{6,2},{7,3},{8,12},{9,13},{10,... | collective-permute-start | bytes 442376 | tf_op jit(solution)/shard_map/ppermute | solution.py:53
  72.0 2.3 %collective-permute-done.13.got = bf16[864,128]{1,0:T(8,128)(2,1)S(1)} collective-permute-done((bf16[864,128]{1,0:T(8,128)(2,1)S(1)}, bf16[864,128]{1,0:T(8,128)(2,1)S(1)}, u32[]{:S(2)}, u32[]{:S(2)}) %collective-permute-start.13) | collective-permute-done | bytes 221216 | tf_op jit(solution)/shard_map/ppermute | solution.py:53
  74.3 0.1 shard_map.121.mine
  74.3 2.2 %collective-permute-start.15 = (bf16[864,128]{1,0:T(8,128)(2,1)S(1)}, bf16[864,128]{1,0:T(8,128)(2,1)S(1)}, u32[]{:S(2)}, u32[]{:S(2)}) collective-permute-start(bf16[864,128]{1,0:T(8,128)(2,1)S(1)} %shard_map.121.mine), channel_id=1, source_target_pairs={{0,8},{1,9},{2,10},{3,11},{4,12},{5,13},{6,14},{7,15},{8,0},{9,1},... | collective-permute-start | bytes 663560 | tf_op jit(solution)/shard_map/ppermute | solution.py:53
  76.5 4.1 %collective-permute-start.10 = (bf16[16,64,128]{2,1,0:T(8,128)(2,1)S(1)}, bf16[16,64,128]{2,1,0:T(8,128)(2,1)S(1)}, u32[]{:S(2)}, u32[]{:S(2)}) collective-permute-start(bf16[16,64,128]{2,1,0:T(8,128)(2,1)S(1)} %get-tuple-element.88.e2), channel_id=1, source_target_pairs={{0,1},{1,2},{2,3},{3,4},{4,5},{5,6},{6,7},{7,8},{8,9},{9,10},{10,1... | collective-permute-start | bytes 786440 | tf_op jit(solution)/shard_map/ppermute | solution.py:44
  80.6 1.9 %collective-permute-start.17 = (bf16[16,64,128]{2,1,0:T(8,128)(2,1)S(1)}, bf16[16,64,128]{2,1,0:T(8,128)(2,1)S(1)}, u32[]{:S(2)}, u32[]{:S(2)}) collective-permute-start(bf16[16,64,128]{2,1,0:T(8,128)(2,1)S(1)} %get-tuple-element.103.e1), channel_id=1, source_target_pairs={{1,0},{2,1},{3,2},{4,3},{5,4},{6,5},{7,6},{8,7},{9,8},{10,9},{11,1... | collective-permute-start | bytes 786440 | tf_op jit(solution)/shard_map/ppermute | solution.py:48
  82.5 0.0 collective-permute-done.16.got
  82.6 0.1 collective-permute-start.18
  82.6 3.3 %collective-permute-done.15.got = bf16[864,128]{1,0:T(8,128)(2,1)S(1)} collective-permute-done((bf16[864,128]{1,0:T(8,128)(2,1)S(1)}, bf16[864,128]{1,0:T(8,128)(2,1)S(1)}, u32[]{:S(2)}, u32[]{:S(2)}) %collective-permute-start.15) | collective-permute-done | bytes 221216 | tf_op jit(solution)/shard_map/ppermute | solution.py:53
  85.9 0.1 shard_map.123.mine
  86.0 1.8 %collective-permute-start.19 = (bf16[864,128]{1,0:T(8,128)(2,1)S(1)}, bf16[864,128]{1,0:T(8,128)(2,1)S(1)}, u32[]{:S(2)}, u32[]{:S(2)}) collective-permute-start(bf16[864,128]{1,0:T(8,128)(2,1)S(1)} %shard_map.123.mine), channel_id=1, source_target_pairs={{0,2},{1,3},{2,0},{3,1},{4,6},{5,7},{6,4},{7,5},{8,10},{9,11},{10,... | collective-permute-start | bytes 663560 | tf_op jit(solution)/shard_map/ppermute | solution.py:53
  87.8 0.8 collective-permute-done.17.after
  88.6 2.5 %shard_map.124 = f32[2,64,16,128]{3,2,1,0:T(8,128)} custom-call(bf16[16,64,128]{2,1,0:T(8,128)(2,1)S(1)} %collective-permute-done.10.before, bf16[16,64,128]{2,1,0:T(8,128)(2,1)S(1)} %get-tuple-element.103.e1, bf16[16,64,128]{2,1,0:T(8,128)(2,1)S(1)} %get-tuple-element.88.e2, bf16[16,64,128]{2,1,0:T(8,128)(2,1)S(1)} %collective-permute-done.17.after, ...), custom_call_target="tpu_custom_call" | custom-call | flops 1000000000 | bytes 1048576 | tf_op jit(solution)/shard_map/pallas_call | solution.py:25
  91.1 1.8 %collective-permute-done.19.got = bf16[864,128]{1,0:T(8,128)(2,1)S(1)} collective-permute-done((bf16[864,128]{1,0:T(8,128)(2,1)S(1)}, bf16[864,128]{1,0:T(8,128)(2,1)S(1)}, u32[]{:S(2)}, u32[]{:S(2)}) %collective-permute-start.19) | collective-permute-done | bytes 221216 | tf_op jit(solution)/shard_map/ppermute | solution.py:53
  92.9 0.6 shard_map.126.mine
  93.5 4.3 %collective-permute-start.21 = (bf16[2,864,128]{2,1,0:T(8,128)(2,1)S(1)}, bf16[2,864,128]{2,1,0:T(8,128)(2,1)S(1)}, u32[]{:S(2)}, u32[]{:S(2)}) collective-permute-start(bf16[2,864,128]{2,1,0:T(8,128)(2,1)S(1)} %shard_map.126.mine), channel_id=1, source_target_pairs={{0,1},{1,0},{2,3},{3,2},{4,5},{5,4},{6,7},{7,6},{8,9},{9,8},{10,11... | collective-permute-start | bytes 1327112 | tf_op jit(solution)/shard_map/ppermute | solution.py:53
  97.7 1.6 %collective-permute-start.20 = (bf16[576,128]{1,0:T(8,128)(2,1)S(1)}, bf16[576,128]{1,0:T(8,128)(2,1)S(1)}, u32[]{:S(2)}, u32[]{:S(2)}) collective-permute-start(bf16[576,128]{1,0:T(8,128)(2,1)S(1)} %shard_map.125.mine), channel_id=1, source_target_pairs={{0,2},{1,3},{2,0},{3,1},{4,6},{5,7},{6,4},{7,5},{8,10},{9,11},{10,... | collective-permute-start | bytes 442376 | tf_op jit(solution)/shard_map/ppermute | solution.py:53
  99.3 4.0 %collective-permute-done.20.got = bf16[576,128]{1,0:T(8,128)(2,1)S(1)} collective-permute-done((bf16[576,128]{1,0:T(8,128)(2,1)S(1)}, bf16[576,128]{1,0:T(8,128)(2,1)S(1)}, u32[]{:S(2)}, u32[]{:S(2)}) %collective-permute-start.20) | collective-permute-done | bytes 147488 | tf_op jit(solution)/shard_map/ppermute | solution.py:53
  103.3 0.6 shard_map.127.mine
  103.9 0.8 collective-permute-start.22
  104.7 1.9 %shard_map.128 = f32[27,128,128]{2,1,0:T(8,128)} custom-call(s32[4]{0:T(128)S(1)} %pad_add_fusion.flags, bf16[2,864,128]{2,1,0:T(8,128)(2,1)S(1)} %shard_map.126.mine, bf16[2,864,128]{2,1,0:T(8,128)(2,1)S(1)} %collective-permute-done.21.got), custom_call_target="tpu_custom_call" | custom-call | flops 1000000000 | bytes 1048576 | tf_op jit(solution)/shard_map/pallas_call | solution.py:25
  106.7 2.0 %shard_map.129 = (f32[27,64,64]{2,1,0:T(8,128)}, f32[27,64,64]{2,1,0:T(8,128)}, f32[8,64,128]{2,1,0:T(8,128)}) custom-call(s32[4]{0:T(128)S(1)} %pad_add_fusion.flags, bf16[2,576,128]{2,1,0:T(8,128)(2,1)S(1)} %shard_map.127.mine, bf16[2,576,128]{2,1,0:T(8,128)(2,1)S(1)} %collective-permute-done.22.got), custom_call_target="tpu_custom_call" | custom-call | flops 1000000000 | bytes 1048576 | tf_op jit(solution)/shard_map/pallas_call | solution.py:25
  (17 shorter events, 0.1 us)
Async XLA Ops:
  0.6 16.6 %collective-permute-start = (bf16[2,64,16,128]{3,2,1,0:T(8,128)(2,1)}, bf16[2,64,16,128]{3,2,1,0:T(8,128)(2,1)S(1)}, u32[]{:S(2)}, u32[]{:S(2)}) collective-permute-start(bf16[2,64,16,128]{3,2,1,0:T(8,128)(2,1)} %volume.1), channel_id=1, source_target_pairs={{0,1},{1,2},{2,3},{3,4},{4,5},{5,6},{6,7},{7,8},{8,9},{9,10},{10,1... | collective-permute-start | bytes 1572872 | tf_op jit(solution)/shard_map/ppermute | solution.py:44
  5.2 12.0 %collective-permute-start.1 = (bf16[2,64,16,128]{3,2,1,0:T(8,128)(2,1)}, bf16[2,64,16,128]{3,2,1,0:T(8,128)(2,1)S(1)}, u32[]{:S(2)}, u32[]{:S(2)}) collective-permute-start(bf16[2,64,16,128]{3,2,1,0:T(8,128)(2,1)} %volume.1), channel_id=1, source_target_pairs={{1,0},{2,1},{3,2},{4,3},{5,4},{6,5},{7,6},{8,7},{9,8},{10,9},{11,1... | collective-permute-start | bytes 1572872 | tf_op jit(solution)/shard_map/ppermute | solution.py:48
  7.1 1.0 copy-start
  8.2 1.0 copy-start.1
  9.2 1.0 copy-start.2
  10.2 1.0 copy-start.3
  11.3 0.9 copy-start.4
  17.2 13.8 %copy-start.5 = (bf16[1,8,64,128]{3,2,1,0:T(8,128)(2,1)S(1)}, bf16[1,8,64,128]{3,2,1,0:T(8,128)(2,1)}, u32[]{:S(2)}) copy-start(bf16[1,8,64,128]{3,2,1,0:T(8,128)(2,1)} %param.9) | copy-start | bytes 393220
  22.8 6.9 %collective-permute-start.3 = (bf16[512,128]{1,0:T(8,128)(2,1)S(1)}, bf16[512,128]{1,0:T(8,128)(2,1)S(1)}, u32[]{:S(2)}, u32[]{:S(2)}) collective-permute-start(bf16[512,128]{1,0:T(8,128)(2,1)S(1)} %get-tuple-element.64.own), channel_id=1, source_target_pairs={{1,0},{2,1},{3,2},{4,3},{5,4},{6,5},{7,6},{8,7},{9,8},{10,9},{11,1... | collective-permute-start | bytes 393224 | tf_op jit(solution)/shard_map/ppermute | solution.py:48
  24.8 6.2 %collective-permute-start.2 = (bf16[512,128]{1,0:T(8,128)(2,1)S(1)}, bf16[512,128]{1,0:T(8,128)(2,1)S(1)}, u32[]{:S(2)}, u32[]{:S(2)}) collective-permute-start(bf16[512,128]{1,0:T(8,128)(2,1)S(1)} %get-tuple-element.64.own), channel_id=1, source_target_pairs={{0,1},{1,2},{2,3},{3,4},{4,5},{5,6},{6,7},{7,8},{8,9},{9,10},{10,1... | collective-permute-start | bytes 393224 | tf_op jit(solution)/shard_map/ppermute | solution.py:44
  31.9 8.7 %copy-start.6 = (f32[2,16,64,128]{3,2,1,0:T(8,128)S(1)}, f32[2,16,64,128]{3,2,1,0:T(8,128)}, u32[]{:S(2)}) copy-start(f32[2,16,64,128]{3,2,1,0:T(8,128)} %get-tuple-element.69.slope) | copy-start | bytes 3145732
  31.9 7.9 %collective-permute-start.5 = (bf16[512,128]{1,0:T(8,128)(2,1)S(1)}, bf16[512,128]{1,0:T(8,128)(2,1)S(1)}, u32[]{:S(2)}, u32[]{:S(2)}) collective-permute-start(bf16[512,128]{1,0:T(8,128)(2,1)S(1)} %shard_map.112.own.delta), channel_id=1, source_target_pairs={{1,0},{2,1},{3,2},{4,3},{5,4},{6,5},{7,6},{8,7},{9,8},{10,9},{11,1... | collective-permute-start | bytes 393224 | tf_op jit(solution)/shard_map/ppermute | solution.py:48
  33.9 6.6 %collective-permute-start.4 = (bf16[512,128]{1,0:T(8,128)(2,1)S(1)}, bf16[512,128]{1,0:T(8,128)(2,1)S(1)}, u32[]{:S(2)}, u32[]{:S(2)}) collective-permute-start(bf16[512,128]{1,0:T(8,128)(2,1)S(1)} %shard_map.112.own.delta), channel_id=1, source_target_pairs={{0,1},{1,2},{2,3},{3,4},{4,5},{5,6},{6,7},{7,8},{8,9},{9,10},{10,1... | collective-permute-start | bytes 393224 | tf_op jit(solution)/shard_map/ppermute | solution.py:44
  39.7 18.1 %collective-permute-start.11 = (bf16[1728,128]{1,0:T(8,128)(2,1)S(1)}, bf16[1728,128]{1,0:T(8,128)(2,1)S(1)}, u32[]{:S(2)}, u32[]{:S(2)}) collective-permute-start(bf16[1728,128]{1,0:T(8,128)(2,1)S(1)} %get-tuple-element.90), channel_id=1, source_target_pairs={{0,1},{1,0},{2,3},{3,2},{4,5},{5,4},{6,7},{7,6},{8,9},{9,8},{10,11... | collective-permute-start | bytes 1327112 | tf_op jit(solution)/shard_map/ppermute | solution.py:53
  42.1 9.0 %collective-permute-start.6 = (bf16[16,64,128]{2,1,0:T(8,128)(2,1)S(1)}, bf16[16,64,128]{2,1,0:T(8,128)(2,1)S(1)}, u32[]{:S(2)}, u32[]{:S(2)}) collective-permute-start(bf16[16,64,128]{2,1,0:T(8,128)(2,1)S(1)} %get-tuple-element.70.d1), channel_id=1, source_target_pairs={{0,1},{1,2},{2,3},{3,4},{4,5},{5,6},{6,7},{7,8},{8,9},{9,10},{10,1... | collective-permute-start | bytes 786440 | tf_op jit(solution)/shard_map/ppermute | solution.py:44
  46.5 7.7 %collective-permute-start.7 = (bf16[16,64,128]{2,1,0:T(8,128)(2,1)S(1)}, bf16[16,64,128]{2,1,0:T(8,128)(2,1)S(1)}, u32[]{:S(2)}, u32[]{:S(2)}) collective-permute-start(bf16[16,64,128]{2,1,0:T(8,128)(2,1)S(1)} %get-tuple-element.71.d0), channel_id=1, source_target_pairs={{1,0},{2,1},{3,2},{4,3},{5,4},{6,5},{7,6},{8,7},{9,8},{10,9},{11,1... | collective-permute-start | bytes 786440 | tf_op jit(solution)/shard_map/ppermute | solution.py:48
  51.0 11.1 %collective-permute-start.8 = (bf16[704,128]{1,0:T(8,128)(2,1)S(1)}, bf16[704,128]{1,0:T(8,128)(2,1)S(1)}, u32[]{:S(2)}, u32[]{:S(2)}) collective-permute-start(bf16[704,128]{1,0:T(8,128)(2,1)S(1)} %get-tuple-element.85), channel_id=1, source_target_pairs={{0,1},{1,0},{2,3},{3,2},{4,5},{5,4},{6,7},{7,6},{8,9},{9,8},{10,11... | collective-permute-start | bytes 540680 | tf_op jit(solution)/shard_map/ppermute | solution.py:53
  58.5 6.9 %collective-permute-start.12 = (bf16[864,128]{1,0:T(8,128)(2,1)S(1)}, bf16[864,128]{1,0:T(8,128)(2,1)S(1)}, u32[]{:S(2)}, u32[]{:S(2)}) collective-permute-start(bf16[864,128]{1,0:T(8,128)(2,1)S(1)} %get-tuple-element.94), channel_id=1, source_target_pairs={{0,2},{1,3},{2,0},{3,1},{4,6},{5,7},{6,4},{7,5},{8,10},{9,11},{10,... | collective-permute-start | bytes 663560 | tf_op jit(solution)/shard_map/ppermute | solution.py:53
  62.1 1.3 %collective-permute-start.9 = (bf16[448,128]{1,0:T(8,128)(2,1)S(1)}, bf16[448,128]{1,0:T(8,128)(2,1)S(1)}, u32[]{:S(2)}, u32[]{:S(2)}) collective-permute-start(bf16[448,128]{1,0:T(8,128)(2,1)S(1)} %get-tuple-element.86), channel_id=1, source_target_pairs={{0,1},{1,0},{2,3},{3,2},{4,5},{5,4},{6,7},{7,6},{8,9},{9,8},{10,11... | collective-permute-start | bytes 344072 | tf_op jit(solution)/shard_map/ppermute | solution.py:53
  64.1 5.4 %collective-permute-start.14 = (bf16[576,128]{1,0:T(8,128)(2,1)S(1)}, bf16[576,128]{1,0:T(8,128)(2,1)S(1)}, u32[]{:S(2)}, u32[]{:S(2)}) collective-permute-start(bf16[576,128]{1,0:T(8,128)(2,1)S(1)} %get-tuple-element.96), channel_id=1, source_target_pairs={{0,2},{1,3},{2,0},{3,1},{4,6},{5,7},{6,4},{7,5},{8,10},{9,11},{10,... | collective-permute-start | bytes 442376 | tf_op jit(solution)/shard_map/ppermute | solution.py:53
  65.5 8.8 %collective-permute-start.13 = (bf16[864,128]{1,0:T(8,128)(2,1)S(1)}, bf16[864,128]{1,0:T(8,128)(2,1)S(1)}, u32[]{:S(2)}, u32[]{:S(2)}) collective-permute-start(bf16[864,128]{1,0:T(8,128)(2,1)S(1)} %shard_map.119.mine), channel_id=1, source_target_pairs={{0,4},{1,5},{2,6},{3,7},{4,0},{5,1},{6,2},{7,3},{8,12},{9,13},{10,... | collective-permute-start | bytes 663560 | tf_op jit(solution)/shard_map/ppermute | solution.py:53
  69.5 13.0 %collective-permute-start.16 = (bf16[576,128]{1,0:T(8,128)(2,1)S(1)}, bf16[576,128]{1,0:T(8,128)(2,1)S(1)}, u32[]{:S(2)}, u32[]{:S(2)}) collective-permute-start(bf16[576,128]{1,0:T(8,128)(2,1)S(1)} %shard_map.120.mine), channel_id=1, source_target_pairs={{0,4},{1,5},{2,6},{3,7},{4,0},{5,1},{6,2},{7,3},{8,12},{9,13},{10,... | collective-permute-start | bytes 442376 | tf_op jit(solution)/shard_map/ppermute | solution.py:53
  74.3 11.6 %collective-permute-start.15 = (bf16[864,128]{1,0:T(8,128)(2,1)S(1)}, bf16[864,128]{1,0:T(8,128)(2,1)S(1)}, u32[]{:S(2)}, u32[]{:S(2)}) collective-permute-start(bf16[864,128]{1,0:T(8,128)(2,1)S(1)} %shard_map.121.mine), channel_id=1, source_target_pairs={{0,8},{1,9},{2,10},{3,11},{4,12},{5,13},{6,14},{7,15},{8,0},{9,1},... | collective-permute-start | bytes 663560 | tf_op jit(solution)/shard_map/ppermute | solution.py:53
  76.5 11.3 %collective-permute-start.10 = (bf16[16,64,128]{2,1,0:T(8,128)(2,1)S(1)}, bf16[16,64,128]{2,1,0:T(8,128)(2,1)S(1)}, u32[]{:S(2)}, u32[]{:S(2)}) collective-permute-start(bf16[16,64,128]{2,1,0:T(8,128)(2,1)S(1)} %get-tuple-element.88.e2), channel_id=1, source_target_pairs={{0,1},{1,2},{2,3},{3,4},{4,5},{5,6},{6,7},{7,8},{8,9},{9,10},{10,1... | collective-permute-start | bytes 786440 | tf_op jit(solution)/shard_map/ppermute | solution.py:44
  80.6 8.0 %collective-permute-start.17 = (bf16[16,64,128]{2,1,0:T(8,128)(2,1)S(1)}, bf16[16,64,128]{2,1,0:T(8,128)(2,1)S(1)}, u32[]{:S(2)}, u32[]{:S(2)}) collective-permute-start(bf16[16,64,128]{2,1,0:T(8,128)(2,1)S(1)} %get-tuple-element.103.e1), channel_id=1, source_target_pairs={{1,0},{2,1},{3,2},{4,3},{5,4},{6,5},{7,6},{8,7},{9,8},{10,9},{11,1... | collective-permute-start | bytes 786440 | tf_op jit(solution)/shard_map/ppermute | solution.py:48
  82.6 8.5 %collective-permute-start.18 = (bf16[576,128]{1,0:T(8,128)(2,1)S(1)}, bf16[576,128]{1,0:T(8,128)(2,1)S(1)}, u32[]{:S(2)}, u32[]{:S(2)}) collective-permute-start(bf16[576,128]{1,0:T(8,128)(2,1)S(1)} %shard_map.122.mine), channel_id=1, source_target_pairs={{0,8},{1,9},{2,10},{3,11},{4,12},{5,13},{6,14},{7,15},{8,0},{9,1},... | collective-permute-start | bytes 442376 | tf_op jit(solution)/shard_map/ppermute | solution.py:53
  86.0 6.9 %collective-permute-start.19 = (bf16[864,128]{1,0:T(8,128)(2,1)S(1)}, bf16[864,128]{1,0:T(8,128)(2,1)S(1)}, u32[]{:S(2)}, u32[]{:S(2)}) collective-permute-start(bf16[864,128]{1,0:T(8,128)(2,1)S(1)} %shard_map.123.mine), channel_id=1, source_target_pairs={{0,2},{1,3},{2,0},{3,1},{4,6},{5,7},{6,4},{7,5},{8,10},{9,11},{10,... | collective-permute-start | bytes 663560 | tf_op jit(solution)/shard_map/ppermute | solution.py:53
  93.5 11.2 %collective-permute-start.21 = (bf16[2,864,128]{2,1,0:T(8,128)(2,1)S(1)}, bf16[2,864,128]{2,1,0:T(8,128)(2,1)S(1)}, u32[]{:S(2)}, u32[]{:S(2)}) collective-permute-start(bf16[2,864,128]{2,1,0:T(8,128)(2,1)S(1)} %shard_map.126.mine), channel_id=1, source_target_pairs={{0,1},{1,0},{2,3},{3,2},{4,5},{5,4},{6,7},{7,6},{8,9},{9,8},{10,11... | collective-permute-start | bytes 1327112 | tf_op jit(solution)/shard_map/ppermute | solution.py:53
  97.7 5.6 %collective-permute-start.20 = (bf16[576,128]{1,0:T(8,128)(2,1)S(1)}, bf16[576,128]{1,0:T(8,128)(2,1)S(1)}, u32[]{:S(2)}, u32[]{:S(2)}) collective-permute-start(bf16[576,128]{1,0:T(8,128)(2,1)S(1)} %shard_map.125.mine), channel_id=1, source_target_pairs={{0,2},{1,3},{2,0},{3,1},{4,6},{5,7},{6,4},{7,5},{8,10},{9,11},{10,... | collective-permute-start | bytes 442376 | tf_op jit(solution)/shard_map/ppermute | solution.py:53
  103.9 2.8 %collective-permute-start.22 = (bf16[2,576,128]{2,1,0:T(8,128)(2,1)S(1)}, bf16[2,576,128]{2,1,0:T(8,128)(2,1)S(1)}, u32[]{:S(2)}, u32[]{:S(2)}) collective-permute-start(bf16[2,576,128]{2,1,0:T(8,128)(2,1)S(1)} %shard_map.127.mine), channel_id=1, source_target_pairs={{0,1},{1,0},{2,3},{3,2},{4,5},{5,4},{6,7},{7,6},{8,9},{9,8},{10,11... | collective-permute-start | bytes 884744 | tf_op jit(solution)/shard_map/ppermute | solution.py:53

commit v4 on v3

--- a/solution.py
+++ b/solution.py
@@ -12,7 +12,7 @@
 NT = (((1,), (1,)), ((), ()))
 TN = (((0,), (0,)), ((), ()))
 AXIS = "ha"
-COST = 10**9
+COST = 4 * 10**9
 
 
 def dot(a, b, dims=(((1,), (0,)), ((), ()))):
@@ -343,10 +343,15 @@
     out[...] = (mine[...].astype(F32) + got[...].astype(F32)).astype(BF)
 
 
-def order_body(flags, mine, got, out):
+def order_body(count, flags, *refs):
     bit = flags[3]
-    out[bit] = mine[...].reshape(out.shape[1:])
-    out[1 - bit] = got[...].reshape(out.shape[1:])
+    out = refs[-1]
+    at = 0
+    for mine, got in zip(refs[:count], refs[count : 2 * count]):
+        rows = slice(at, at + mine.shape[0])
+        out[bit, rows, :] = mine[...]
+        out[1 - bit, rows, :] = got[...]
+        at += mine.shape[0]
 
 
 def block_of(halves, block, num):
@@ -376,8 +381,10 @@
         at += rows
 
 
-def fine_unpack(flags, mine, got, first, second, down, middle_halves, first_halves):
-    gather_halves(flags, mine, got, middle_halves, first_halves)
+def unpack_body(
+    flags, mine, got, first, second, down, coarse, coarse_halves, middle_halves, first_halves
+):
+    gather_halves(flags, mine, got, coarse_halves, middle_halves, first_halves)
     fine_blocks(first_halves, first)
     fine_blocks(middle_halves, second)
     chan = first.shape[1]
@@ -385,16 +392,12 @@
         for b in range(2):
             for c in range(2):
                 down[4 * a + 2 * b + c] = block_of(middle_halves, 14 + 4 * a + 2 * c + b, chan)
-
-
-def coarse_unpack(flags, mine, got, out, halves):
-    gather_halves(flags, mine, got, halves)
-    piece = out.shape[1] // 2
+    piece = coarse.shape[1] // 2
     for k in range(3):
         for j in range(9):
             for s in range(2):
-                out[3 * j + k, s * piece : (s + 1) * piece, :] = block_of(
-                    halves, 18 * k + 2 * j + s, piece
+                coarse[3 * j + k, s * piece : (s + 1) * piece, :] = block_of(
+                    coarse_halves, 18 * k + 2 * j + s, piece
                 )
 
 
@@ -415,10 +418,12 @@
     return call(add_body, [(mine.shape, BF)], mine, got)[0]
 
 
-def paired(flags, part, got):
-    lanes = part.shape[-1]
+def paired(flags, *pairs):
+    mine, got = zip(*pairs)
+    rows = sum(m.shape[0] for m in mine)
     return call(
-        order_body, [((2, part.size // lanes, lanes), BF)], flags, part, got, smem=1
+        functools.partial(order_body, len(pairs)), [((2, rows, mine[0].shape[1]), BF)],
+        flags, *mine, *got, smem=1,
     )[0]
 
 
@@ -481,47 +486,51 @@
         scratch=fine_grad_scratch(num, chan, deep) + (halves(22),), smem=1,
     )
     a_keep, a_send = halved(flags, (a_mine, tied(swapped(a_other, 1), b_mine)))
+    a_got = swapped(a_send, 2)
     b_got = swapped(b_other, 1)
     e1, e2, c_mine, c_other = call(
         first_delta_body, [fine, fine] + [dealt(14)] * 2,
-        flags, *second_rows, second_b, slope1, v0, v1, v2, v3,
+        flags, tied(second_rows[0], a_keep), *second_rows[1:], second_b, slope1, v0, v1, v2, v3,
         scratch=fine_grad_scratch(num, chan, deep) + (halves(14),), smem=1,
     )
-    a_got = swapped(tied(a_send, c_mine), 2)
-    keep, send = halved(flags, (b_mine, b_got), (c_mine, swapped(c_other, 1)))
+    a_part = summed(a_keep, tied(a_got, c_mine))
+    c_got = swapped(c_other, 1)
+    keep, send = halved(flags, (b_mine, tied(b_got, a_part)), (c_mine, c_got))
     got = swapped(send, 2)
-    first_rows = [from_before(tied(e2, keep)), e1, e2, from_after(tied(e1, keep))]
-    a_part, part = summed(a_keep, tied(a_got, keep)), None
     strides = []
     stride = 4
     while stride < lax.axis_size(AXIS):
         strides.append(stride)
         stride *= 2
-    for stride in strides:
+    a_got = swapped(a_part, strides[0])
+    a_part = summed(a_part, tied(a_got, keep))
+    a_got = swapped(a_part, strides[1])
+    part = summed(keep, tied(got, a_part))
+    got = swapped(part, strides[0])
+    face = part
+    part = summed(part, tied(got, face))
+    got = swapped(part, strides[1])
+    first_rows = [from_before(tied(e2, face)), e1, e2, from_after(tied(e1, face))]
+    for stride in strides[2:]:
+        a_part = summed(a_part, tied(a_got, part))
         a_got = swapped(a_part, stride)
-        part = summed(keep, tied(got, a_part)) if part is None else summed(part, tied(got, a_part))
+        part = summed(part, tied(got, a_part))
         got = swapped(part, stride)
-        a_part = summed(a_part, tied(a_got, part))
+    a_part = summed(a_part, tied(a_got, part))
     a_got = swapped(a_part, 2)
     (input_grad,) = call(
         input_grad_body, [((2, chan, num, deep), F32)],
         tied(first_rows[0], a_part), *first_rows[1:], first_b,
         scratch=(pltpu.VMEM((num, chan, deep), F32),),
     )
-    part = summed(part, tied(got, a_part, input_grad))
-    got = swapped(part, 2)
-    a_pair = paired(flags, tied(a_part, part), a_got)
-    a_got = swapped(a_pair, 1)
-    pair = paired(flags, tied(part, a_pair), got)
-    (coarse_out,) = call(
-        coarse_unpack, [((27, wide, wide), F32)], flags, tied(a_pair, pair), a_got,
-        smem=1, scratch=(halves(54),),
-    )
+    part = summed(part, tied(got, input_grad))
+    pair = paired(flags, (a_part, tied(a_got, part)), (part, swapped(part, 2)))
     fine_out = ((27, chan, chan), F32)
-    first_out, second_out, down_out = call(
-        fine_unpack, [fine_out, fine_out, ((8, chan, wide), F32)],
-        flags, tied(pair, coarse_out), swapped(pair, 1),
-        smem=1, scratch=(halves(22), halves(14)),
+    first_out, second_out, down_out, coarse_out = call(
+        unpack_body,
+        [fine_out, fine_out, ((8, chan, wide), F32), ((27, wide, wide), F32)],
+        flags, pair, swapped(pair, 1),
+        smem=1, scratch=(halves(54), halves(22), halves(14)),
     )
     return (
         input_grad,

time: 109 us -> 103 us (0.945)
  waiting for transfers between devices: 24 us -> 17.4 us
  starting transfers between devices: 51.7 us -> 53.8 us
  Pallas kernels: 27 us -> 25.3 us
    ppermute x13 -> x12, waiting for transfers between devices: 14.8 us -> 9.37 us  [swapped(): return lax.ppermute(array, AXIS, [(i, i ^ stride) for i in range(size)])]
    ppermute x13 -> x12, starting transfers between devices: 20.2 us -> 22.3 us  [swapped(): return lax.ppermute(array, AXIS, [(i, i ^ stride) for i in range(size)])]
    pallas_call x20 -> x18, Pallas kernels: 27 us -> 25.3 us  [call(): pl.pallas_call(body, out_shape=[jax.ShapeDtypeStruct(s, d) for s, d in ou...]
    ppermute x5, waiting for transfers between devices: 4.6 us -> 3.44 us  [from_after(): return lax.ppermute(array, AXIS, neighbours(array)[1])]
  transfers between devices with their start and end apart: 23 -> 22, of which waited for: 13 -> 9; matrix products, arithmetic and copies ran while one was open for 0% -> 0% of each run, Pallas kernels for 16% -> 15%
where the time goes in v4:
time: 103 us
  starting transfers between devices  53.8 us (52%)
  Pallas kernels  25.3 us (25%)
  waiting for transfers between devices  17.4 us (17%)
  local copies, waits for them, and re-layouts  5.02 us (5%)
    pallas_call x18, Pallas kernels, call(): pl.pallas_call(body, out_shape=[jax.ShapeDtypeStruct(s, d) for s, d in ou...  25.3 us
    ppermute x12, starting transfers between devices, swapped(): return lax.ppermute(array, AXIS, [(i, i ^ stride) for i in range(size)])  22.3 us
    ppermute x5, starting transfers between devices, from_before(): return lax.ppermute(array, AXIS, neighbours(array)[0])  21.8 us
    ppermute x5, starting transfers between devices, from_after(): return lax.ppermute(array, AXIS, neighbours(array)[1])  9.72 us
    ppermute x12, waiting for transfers between devices, swapped(): return lax.ppermute(array, AXIS, [(i, i ^ stride) for i in range(size)])  9.37 us
    unnamed x14, local copies, waits for them, and re-layouts  5.02 us
    ppermute x5, waiting for transfers between devices, from_before(): return lax.ppermute(array, AXIS, neighbours(array)[0])  4.64 us
    ppermute x5, waiting for transfers between devices, from_after(): return lax.ppermute(array, AXIS, neighbours(array)[1])  3.44 us
  transfers between devices with their start and end apart: 22, of which 9 were waited for; matrix products, arithmetic and copies ran while one was open for 0% of the time, Pallas kernels for 15%

profile of v4, /device:TPU:1, one launch (start us, length us, event | category | flops | bytes accessed | tf_op | source)
XLA Modules:
  0.0 102.5 jit_solution(9769446857463846603)
XLA Ops:
  0.6 4.5 %collective-permute-start = (bf16[2,64,16,128]{3,2,1,0:T(8,128)(2,1)}, bf16[2,64,16,128]{3,2,1,0:T(8,128)(2,1)S(1)}, u32[]{:S(2)}, u32[]{:S(2)}) collective-permute-start(bf16[2,64,16,128]{3,2,1,0:T(8,128)(2,1)} %volume.1), channel_id=1, source_target_pairs={{0,1},{1,2},{2,3},{3,4},{4,5},{5,6},{6,7},{7,8},{8,9},{9,10},{10,1... | collective-permute-start | bytes 1572872 | tf_op jit(solution)/shard_map/ppermute | solution.py:44
  5.2 1.9 %collective-permute-start.1 = (bf16[2,64,16,128]{3,2,1,0:T(8,128)(2,1)}, bf16[2,64,16,128]{3,2,1,0:T(8,128)(2,1)S(1)}, u32[]{:S(2)}, u32[]{:S(2)}) collective-permute-start(bf16[2,64,16,128]{3,2,1,0:T(8,128)(2,1)} %volume.1), channel_id=1, source_target_pairs={{1,0},{2,1},{3,2},{4,3},{5,4},{6,5},{7,6},{8,7},{9,8},{10,9},{11,1... | collective-permute-start | bytes 1572872 | tf_op jit(solution)/shard_map/ppermute | solution.py:48
  7.1 0.1 pad_add_fusion.flags
  7.2 1.0 %copy-done = bf16[2,64,16,128]{3,2,1,0:T(8,128)(2,1)S(1)} copy-done((bf16[2,64,16,128]{3,2,1,0:T(8,128)(2,1)S(1)}, bf16[2,64,16,128]{3,2,1,0:T(8,128)(2,1)}, u32[]{:S(2)}) %copy-start) | copy-done | bytes 524312
  8.3 1.0 %copy-done.1 = bf16[2,64,16,128]{3,2,1,0:T(8,128)(2,1)S(1)} copy-done((bf16[2,64,16,128]{3,2,1,0:T(8,128)(2,1)S(1)}, bf16[2,64,16,128]{3,2,1,0:T(8,128)(2,1)}, u32[]{:S(2)}) %copy-start.1) | copy-done | bytes 524312
  9.3 1.0 copy-done.2
  10.3 1.0 copy-done.3
  11.3 0.9 copy-done.4
  12.2 2.3 %shard_map.110 = (bf16[16,64,128]{2,1,0:T(8,128)(2,1)S(1)}, bf16[16,64,128]{2,1,0:T(8,128)(2,1)S(1)}, bf16[2,16,64,128]{3,2,1,0:T(8,128)(2,1)S(1)}, bf16[192,576...) custom-call(bf16[2,64,16,128]{3,2,1,0:T(8,128)(2,1)S(1)} %copy-done., ...), custom_call_target="tpu_custom_call" | custom-call | flops 4000000000 | bytes 1048576 | tf_op jit(solution)/shard_map/pallas_call | solution.py:25
  14.6 2.6 %collective-permute-done.before = bf16[2,64,16,128]{3,2,1,0:T(8,128)(2,1)S(1)} collective-permute-done((bf16[2,64,16,128]{3,2,1,0:T(8,128)(2,1)}, bf16[2,64,16,128]{3,2,1,0:T(8,128)(2,1)S(1)}, u32[]{:S(2)}, u32[]{:S(2)}) %collective-permute-start) | collective-permute-done | bytes 524320 | tf_op jit(solution)/shard_map/ppermute | solution.py:44
  17.2 0.0 collective-permute-done.1.after
  17.2 5.6 %shard_map.111 = (bf16[16,64,128]{2,1,0:T(8,128)(2,1)S(1)}, bf16[16,64,128]{2,1,0:T(8,128)(2,1)S(1)}, bf16[16,64,128]{2,1,0:T(8,128)(2,1)S(1)}, bf16[16,64,128]{...) custom-call(s32[4]{0:T(128)S(1)} %pad_add_fusion.flags, ...), custom_call_target="tpu_custom_call" | custom-call | flops 4000000000 | bytes 1048576 | tf_op jit(solution)/shard_map/pallas_call | solution.py:25
  22.8 1.9 %collective-permute-start.3 = (bf16[512,128]{1,0:T(8,128)(2,1)S(1)}, bf16[512,128]{1,0:T(8,128)(2,1)S(1)}, u32[]{:S(2)}, u32[]{:S(2)}) collective-permute-start(bf16[512,128]{1,0:T(8,128)(2,1)S(1)} %get-tuple-element.63.own), channel_id=1, source_target_pairs={{1,0},{2,1},{3,2},{4,3},{5,4},{6,5},{7,6},{8,7},{9,8},{10,9},{11,1... | collective-permute-start | bytes 393224 | tf_op jit(solution)/shard_map/ppermute | solution.py:48
  24.8 4.3 %collective-permute-start.2 = (bf16[512,128]{1,0:T(8,128)(2,1)S(1)}, bf16[512,128]{1,0:T(8,128)(2,1)S(1)}, u32[]{:S(2)}, u32[]{:S(2)}) collective-permute-start(bf16[512,128]{1,0:T(8,128)(2,1)S(1)} %get-tuple-element.63.own), channel_id=1, source_target_pairs={{0,1},{1,2},{2,3},{3,4},{4,5},{5,6},{6,7},{7,8},{8,9},{9,10},{10,1... | collective-permute-start | bytes 393224 | tf_op jit(solution)/shard_map/ppermute | solution.py:44
  29.0 0.7 collective-permute-done.3.after
  29.8 1.2 %collective-permute-done.2.before = bf16[512,128]{1,0:T(8,128)(2,1)S(1)} collective-permute-done((bf16[512,128]{1,0:T(8,128)(2,1)S(1)}, bf16[512,128]{1,0:T(8,128)(2,1)S(1)}, u32[]{:S(2)}, u32[]{:S(2)}) %collective-permute-start.2) | collective-permute-done | bytes 131104 | tf_op jit(solution)/shard_map/ppermute | solution.py:44
  31.0 0.9 shard_map.112.own.delta
  31.9 0.0 copy-start.6
  31.9 2.1 %collective-permute-start.5 = (bf16[512,128]{1,0:T(8,128)(2,1)S(1)}, bf16[512,128]{1,0:T(8,128)(2,1)S(1)}, u32[]{:S(2)}, u32[]{:S(2)}) collective-permute-start(bf16[512,128]{1,0:T(8,128)(2,1)S(1)} %shard_map.112.own.delta), channel_id=1, source_target_pairs={{1,0},{2,1},{3,2},{4,3},{5,4},{6,5},{7,6},{8,7},{9,8},{10,9},{11,1... | collective-permute-start | bytes 393224 | tf_op jit(solution)/shard_map/ppermute | solution.py:48
  33.9 4.4 %collective-permute-start.4 = (bf16[512,128]{1,0:T(8,128)(2,1)S(1)}, bf16[512,128]{1,0:T(8,128)(2,1)S(1)}, u32[]{:S(2)}, u32[]{:S(2)}) collective-permute-start(bf16[512,128]{1,0:T(8,128)(2,1)S(1)} %shard_map.112.own.delta), channel_id=1, source_target_pairs={{0,1},{1,2},{2,3},{3,4},{4,5},{5,6},{6,7},{7,8},{8,9},{9,10},{10,1... | collective-permute-start | bytes 393224 | tf_op jit(solution)/shard_map/ppermute | solution.py:44
  38.3 1.4 %shard_map.114 = (bf16[1728,128]{1,0:T(8,128)(2,1)S(1)}, bf16[1728,128]{1,0:T(8,128)(2,1)S(1)}) custom-call(s32[4]{0:T(128)S(1)} %pad_add_fusion.flags, bf16[512,128]{1,0:T(8,128)(2,1)S(1)} %collective-permute-done.2.before, bf16[512,128]{1,0:T(8,128)(2,1)S(1)} %get-tuple-element.63.own, bf16[512,128]{1,0:T(8,128)(2,1)S(1)} %collective-permute-done.3.after, ...), custom_call_target="tpu_custom_call" | custom-call | flops 4000000000 | bytes 1048576 | tf_op jit(solution)/shard_map/pallas_call | solution.py:25
  39.7 0.1 collective-permute-start.7
  39.8 0.0 collective-permute-done.5.after
  39.8 0.8 collective-permute-done.4.before
  40.6 1.5 %shard_map.113 = (bf16[512,128]{1,0:T(8,128)(2,1)S(1)}, bf16[16,64,128]{2,1,0:T(8,128)(2,1)S(1)}, bf16[16,64,128]{2,1,0:T(8,128)(2,1)S(1)}) custom-call(bf16[512,128]{1,0:T(8,128)(2,1)S(1)} %collective-permute-done.4.before, bf16[512,128]{1,0:T(8,128)(2,1)S(1)} %shard_map.112.own.delta, bf16[512,128]{1,0:T(8,128)(2,1)S(1)} %collective-permute-done.5.after, ...), custom_call_target="tpu_custom_call" | custom-call | flops 4000000000 | bytes 1048576 | tf_op jit(solution)/shard_map/pallas_call | solution.py:25
  42.1 4.4 %collective-permute-start.6 = (bf16[16,64,128]{2,1,0:T(8,128)(2,1)S(1)}, bf16[16,64,128]{2,1,0:T(8,128)(2,1)S(1)}, u32[]{:S(2)}, u32[]{:S(2)}) collective-permute-start(bf16[16,64,128]{2,1,0:T(8,128)(2,1)S(1)} %get-tuple-element.69.d1), channel_id=1, source_target_pairs={{0,1},{1,2},{2,3},{3,4},{4,5},{5,6},{6,7},{7,8},{8,9},{9,10},{10,1... | collective-permute-start | bytes 786440 | tf_op jit(solution)/shard_map/ppermute | solution.py:44
  46.5 1.9 %collective-permute-start.8 = (bf16[16,64,128]{2,1,0:T(8,128)(2,1)S(1)}, bf16[16,64,128]{2,1,0:T(8,128)(2,1)S(1)}, u32[]{:S(2)}, u32[]{:S(2)}) collective-permute-start(bf16[16,64,128]{2,1,0:T(8,128)(2,1)S(1)} %get-tuple-element.76.d0), channel_id=1, source_target_pairs={{1,0},{2,1},{3,2},{4,3},{5,4},{6,5},{7,6},{8,7},{9,8},{10,9},{11,1... | collective-permute-start | bytes 786440 | tf_op jit(solution)/shard_map/ppermute | solution.py:48
  48.5 2.4 %shard_map.115 = (bf16[704,128]{1,0:T(8,128)(2,1)S(1)}, bf16[704,128]{1,0:T(8,128)(2,1)S(1)}) custom-call(s32[4]{0:T(128)S(1)} %pad_add_fusion.flags, bf16[16,64,128]{2,1,0:T(8,128)(2,1)S(1)} %get-tuple-element.72.s0, bf16[16,64,128]{2,1,0:T(8,128)(2,1)S(1)} %get-tuple-element.73.s1, bf16[16,64,128]{2,1,0:T(8,128)(2,1)S(1)} %get-tuple-element.74.s2, ...), custom_call_target="tpu_custom_call" | custom-call | flops 4000000000 | bytes 1048576 | tf_op jit(solution)/shard_map/pallas_call | solution.py:25
  50.9 0.1 collective-permute-start.9
  50.9 0.0 collective-permute-done.7.refs_1_
  50.9 0.9 shard_map.116
  51.9 0.0 collective-permute-done.6.before
  51.9 2.6 %collective-permute-start.10 = (bf16[864,128]{1,0:T(8,128)(2,1)S(1)}, bf16[864,128]{1,0:T(8,128)(2,1)S(1)}, u32[]{:S(2)}, u32[]{:S(2)}) collective-permute-start(bf16[864,128]{1,0:T(8,128)(2,1)S(1)} %get-tuple-element.90), channel_id=1, source_target_pairs={{0,2},{1,3},{2,0},{3,1},{4,6},{5,7},{6,4},{7,5},{8,10},{9,11},{10,... | collective-permute-start | bytes 663560 | tf_op jit(solution)/shard_map/ppermute | solution.py:53
  54.5 0.0 collective-permute-done.8.after
  54.5 3.5 %shard_map.117 = (bf16[16,64,128]{2,1,0:T(8,128)(2,1)S(1)}, bf16[16,64,128]{2,1,0:T(8,128)(2,1)S(1)}, bf16[448,128]{1,0:T(8,128)(2,1)S(1)}, bf16[448,128]{1,0:T(8,128)(2,1)S(1)}) custom-call(s32[4]{0:T(128)S(1)} %pad_add_fusion.flags, bf16[16,64,128]{2,1,0:T(8,128)(2,1)S(1)} %collective-permute-done.6.before, bf16[16,64,128]{2,1,0:T(8,128)(2,1)S(1)} %get-tuple-element.76.d0, ...), custom_call_target="tpu_custom_call" | custom-call | flops 4000000000 | bytes 1048576 | tf_op jit(solution)/shard_map/pallas_call | solution.py:25
  58.1 0.8 collective-permute-start.11
  58.9 1.4 %collective-permute-done.10.got = bf16[864,128]{1,0:T(8,128)(2,1)S(1)} collective-permute-done((bf16[864,128]{1,0:T(8,128)(2,1)S(1)}, bf16[864,128]{1,0:T(8,128)(2,1)S(1)}, u32[]{:S(2)}, u32[]{:S(2)}) %collective-permute-start.10) | collective-permute-done | bytes 221216 | tf_op jit(solution)/shard_map/ppermute | solution.py:53
  60.4 0.1 shard_map.118.mine
  60.4 2.8 %collective-permute-start.13 = (bf16[864,128]{1,0:T(8,128)(2,1)S(1)}, bf16[864,128]{1,0:T(8,128)(2,1)S(1)}, u32[]{:S(2)}, u32[]{:S(2)}) collective-permute-start(bf16[864,128]{1,0:T(8,128)(2,1)S(1)} %shard_map.118.mine), channel_id=1, source_target_pairs={{0,4},{1,5},{2,6},{3,7},{4,0},{5,1},{6,2},{7,3},{8,12},{9,13},{10,... | collective-permute-start | bytes 663560 | tf_op jit(solution)/shard_map/ppermute | solution.py:53
  63.2 0.0 collective-permute-done.9.refs_2_
  63.2 0.0 collective-permute-done.11.refs_3_
  63.2 0.7 shard_map.119
  63.9 0.8 collective-permute-start.12
  64.7 3.5 %collective-permute-done.13.got = bf16[864,128]{1,0:T(8,128)(2,1)S(1)} collective-permute-done((bf16[864,128]{1,0:T(8,128)(2,1)S(1)}, bf16[864,128]{1,0:T(8,128)(2,1)S(1)}, u32[]{:S(2)}, u32[]{:S(2)}) %collective-permute-start.13) | collective-permute-done | bytes 221216 | tf_op jit(solution)/shard_map/ppermute | solution.py:53
  68.2 0.1 shard_map.120.mine
  68.3 0.0 collective-permute-done.12.got
  68.4 1.2 %collective-permute-start.16 = (bf16[576,128]{1,0:T(8,128)(2,1)S(1)}, bf16[576,128]{1,0:T(8,128)(2,1)S(1)}, u32[]{:S(2)}, u32[]{:S(2)}) collective-permute-start(bf16[576,128]{1,0:T(8,128)(2,1)S(1)} %shard_map.121.mine), channel_id=1, source_target_pairs={{0,4},{1,5},{2,6},{3,7},{4,0},{5,1},{6,2},{7,3},{8,12},{9,13},{10,... | collective-permute-start | bytes 442376 | tf_op jit(solution)/shard_map/ppermute | solution.py:53
  69.6 2.3 %collective-permute-start.15 = (bf16[864,128]{1,0:T(8,128)(2,1)S(1)}, bf16[864,128]{1,0:T(8,128)(2,1)S(1)}, u32[]{:S(2)}, u32[]{:S(2)}) collective-permute-start(bf16[864,128]{1,0:T(8,128)(2,1)S(1)} %shard_map.120.mine), channel_id=1, source_target_pairs={{0,8},{1,9},{2,10},{3,11},{4,12},{5,13},{6,14},{7,15},{8,0},{9,1},... | collective-permute-start | bytes 663560 | tf_op jit(solution)/shard_map/ppermute | solution.py:53
  71.9 4.2 %collective-permute-start.14 = (bf16[16,64,128]{2,1,0:T(8,128)(2,1)S(1)}, bf16[16,64,128]{2,1,0:T(8,128)(2,1)S(1)}, u32[]{:S(2)}, u32[]{:S(2)}) collective-permute-start(bf16[16,64,128]{2,1,0:T(8,128)(2,1)S(1)} %get-tuple-element.98.e2), channel_id=1, source_target_pairs={{0,1},{1,2},{2,3},{3,4},{4,5},{5,6},{6,7},{7,8},{8,9},{9,10},{10,1... | collective-permute-start | bytes 786440 | tf_op jit(solution)/shard_map/ppermute | solution.py:44
  76.1 1.9 %collective-permute-start.17 = (bf16[16,64,128]{2,1,0:T(8,128)(2,1)S(1)}, bf16[16,64,128]{2,1,0:T(8,128)(2,1)S(1)}, u32[]{:S(2)}, u32[]{:S(2)}) collective-permute-start(bf16[16,64,128]{2,1,0:T(8,128)(2,1)S(1)} %get-tuple-element.103.e1), channel_id=1, source_target_pairs={{1,0},{2,1},{3,2},{4,3},{5,4},{6,5},{7,6},{8,7},{9,8},{10,9},{11,1... | collective-permute-start | bytes 786440 | tf_op jit(solution)/shard_map/ppermute | solution.py:48
  78.0 0.0 collective-permute-done.16.got
  78.1 0.7 collective-permute-start.18
  78.8 0.0 collective-permute-done.15.got
  78.8 0.1 shard_map.123.refs_0_
  78.8 3.3 %collective-permute-start.19 = (bf16[864,128]{1,0:T(8,128)(2,1)S(1)}, bf16[864,128]{1,0:T(8,128)(2,1)S(1)}, u32[]{:S(2)}, u32[]{:S(2)}) collective-permute-start(bf16[864,128]{1,0:T(8,128)(2,1)S(1)} %shard_map.123.refs_0_), channel_id=1, source_target_pairs={{0,2},{1,3},{2,0},{3,1},{4,6},{5,7},{6,4},{7,5},{8,10},{9,11},{10,... | collective-permute-start | bytes 663560 | tf_op jit(solution)/shard_map/ppermute | solution.py:53
  82.1 0.0 collective-permute-done.14.before
  82.1 2.7 %collective-permute-done.17.after = bf16[16,64,128]{2,1,0:T(8,128)(2,1)S(1)} collective-permute-done((bf16[16,64,128]{2,1,0:T(8,128)(2,1)S(1)}, bf16[16,64,128]{2,1,0:T(8,128)(2,1)S(1)}, u32[]{:S(2)}, u32[]{:S(2)}) %collective-permute-start.17) | collective-permute-done | bytes 262176 | tf_op jit(solution)/shard_map/ppermute | solution.py:48
  84.8 2.5 %shard_map.124 = f32[2,64,16,128]{3,2,1,0:T(8,128)} custom-call(bf16[16,64,128]{2,1,0:T(8,128)(2,1)S(1)} %collective-permute-done.14.before, bf16[16,64,128]{2,1,0:T(8,128)(2,1)S(1)} %get-tuple-element.103.e1, bf16[16,64,128]{2,1,0:T(8,128)(2,1)S(1)} %get-tuple-element.98.e2, bf16[16,64,128]{2,1,0:T(8,128)(2,1)S(1)} %collective-permute-done.17.after, ...), custom_call_target="tpu_custom_call" | custom-call | flops 4000000000 | bytes 1048576 | tf_op jit(solution)/shard_map/pallas_call | solution.py:25
  87.4 3.7 %collective-permute-start.20 = (bf16[576,128]{1,0:T(8,128)(2,1)S(1)}, bf16[576,128]{1,0:T(8,128)(2,1)S(1)}, u32[]{:S(2)}, u32[]{:S(2)}) collective-permute-start(bf16[576,128]{1,0:T(8,128)(2,1)S(1)} %shard_map.125.refs_1_), channel_id=1, source_target_pairs={{0,2},{1,3},{2,0},{3,1},{4,6},{5,7},{6,4},{7,5},{8,10},{9,11},{10,... | collective-permute-start | bytes 442376 | tf_op jit(solution)/shard_map/ppermute | solution.py:53
  91.1 2.5 %collective-permute-done.20.refs_3_ = bf16[576,128]{1,0:T(8,128)(2,1)S(1)} collective-permute-done((bf16[576,128]{1,0:T(8,128)(2,1)S(1)}, bf16[576,128]{1,0:T(8,128)(2,1)S(1)}, u32[]{:S(2)}, u32[]{:S(2)}) %collective-permute-start.20) | collective-permute-done | bytes 147488 | tf_op jit(solution)/shard_map/ppermute | solution.py:53
  93.6 0.6 shard_map.126.mine
  94.2 3.9 %collective-permute-start.21 = (bf16[2,1440,128]{2,1,0:T(8,128)(2,1)S(1)}, bf16[2,1440,128]{2,1,0:T(8,128)(2,1)S(1)}, u32[]{:S(2)}, u32[]{:S(2)}) collective-permute-start(bf16[2,1440,128]{2,1,0:T(8,128)(2,1)S(1)} %shard_map.126.mine), channel_id=1, source_target_pairs={{0,1},{1,0},{2,3},{3,2},{4,5},{5,4},{6,7},{7,6},{8,9},{9,8},{10,11... | collective-permute-start | bytes 2211848 | tf_op jit(solution)/shard_map/ppermute | solution.py:53
  98.1 1.8 %collective-permute-done.21.got = bf16[2,1440,128]{2,1,0:T(8,128)(2,1)S(1)} collective-permute-done((bf16[2,1440,128]{2,1,0:T(8,128)(2,1)S(1)}, bf16[2,1440,128]{2,1,0:T(8,128)(2,1)S(1)}, u32[]{:S(2)}, u32[]{:S(2)}) %collective-permute-start.21) | collective-permute-done | bytes 737312 | tf_op jit(solution)/shard_map/ppermute | solution.py:53
  99.9 2.6 %shard_map.127 = (f32[27,64,64]{2,1,0:T(8,128)}, f32[27,64,64]{2,1,0:T(8,128)}, f32[8,64,128]{2,1,0:T(8,128)}, f32[27,128,128]{2,1,0:T(8,128)}) custom-call(s32[4]{0:T(128)S(1)} %pad_add_fusion.flags, bf16[2,1440,128]{2,1,0:T(8,128)(2,1)S(1)} %shard_map.126.mine, bf16[2,1440,128]{2,1,0:T(8,128)(2,1)S(1)} %collective-permute-done.21.got), custom_call_target="tpu_custom_call" | custom-call | flops 4000000000 | bytes 1048576 | tf_op jit(solution)/shard_map/pallas_call | solution.py:25
  (13 shorter events, 0.1 us)
Async XLA Ops:
  0.6 16.6 %collective-permute-start = (bf16[2,64,16,128]{3,2,1,0:T(8,128)(2,1)}, bf16[2,64,16,128]{3,2,1,0:T(8,128)(2,1)S(1)}, u32[]{:S(2)}, u32[]{:S(2)}) collective-permute-start(bf16[2,64,16,128]{3,2,1,0:T(8,128)(2,1)} %volume.1), channel_id=1, source_target_pairs={{0,1},{1,2},{2,3},{3,4},{4,5},{5,6},{6,7},{7,8},{8,9},{9,10},{10,1... | collective-permute-start | bytes 1572872 | tf_op jit(solution)/shard_map/ppermute | solution.py:44
  5.2 12.0 %collective-permute-start.1 = (bf16[2,64,16,128]{3,2,1,0:T(8,128)(2,1)}, bf16[2,64,16,128]{3,2,1,0:T(8,128)(2,1)S(1)}, u32[]{:S(2)}, u32[]{:S(2)}) collective-permute-start(bf16[2,64,16,128]{3,2,1,0:T(8,128)(2,1)} %volume.1), channel_id=1, source_target_pairs={{1,0},{2,1},{3,2},{4,3},{5,4},{6,5},{7,6},{8,7},{9,8},{10,9},{11,1... | collective-permute-start | bytes 1572872 | tf_op jit(solution)/shard_map/ppermute | solution.py:48
  7.2 1.0 %copy-start = (bf16[2,64,16,128]{3,2,1,0:T(8,128)(2,1)S(1)}, bf16[2,64,16,128]{3,2,1,0:T(8,128)(2,1)}, u32[]{:S(2)}) copy-start(bf16[2,64,16,128]{3,2,1,0:T(8,128)(2,1)} %skip.1) | copy-start | bytes 1572868
  8.3 1.0 %copy-start.1 = (bf16[2,64,16,128]{3,2,1,0:T(8,128)(2,1)S(1)}, bf16[2,64,16,128]{3,2,1,0:T(8,128)(2,1)}, u32[]{:S(2)}) copy-start(bf16[2,64,16,128]{3,2,1,0:T(8,128)(2,1)} %volume.1) | copy-start | bytes 1572868
  9.3 1.0 copy-start.2
  10.3 1.0 copy-start.3
  11.3 0.9 copy-start.4
  17.2 13.8 %copy-start.5 = (bf16[1,8,64,128]{3,2,1,0:T(8,128)(2,1)S(1)}, bf16[1,8,64,128]{3,2,1,0:T(8,128)(2,1)}, u32[]{:S(2)}) copy-start(bf16[1,8,64,128]{3,2,1,0:T(8,128)(2,1)} %param.9) | copy-start | bytes 393220
  22.8 6.9 %collective-permute-start.3 = (bf16[512,128]{1,0:T(8,128)(2,1)S(1)}, bf16[512,128]{1,0:T(8,128)(2,1)S(1)}, u32[]{:S(2)}, u32[]{:S(2)}) collective-permute-start(bf16[512,128]{1,0:T(8,128)(2,1)S(1)} %get-tuple-element.63.own), channel_id=1, source_target_pairs={{1,0},{2,1},{3,2},{4,3},{5,4},{6,5},{7,6},{8,7},{9,8},{10,9},{11,1... | collective-permute-start | bytes 393224 | tf_op jit(solution)/shard_map/ppermute | solution.py:48
  24.8 6.2 %collective-permute-start.2 = (bf16[512,128]{1,0:T(8,128)(2,1)S(1)}, bf16[512,128]{1,0:T(8,128)(2,1)S(1)}, u32[]{:S(2)}, u32[]{:S(2)}) collective-permute-start(bf16[512,128]{1,0:T(8,128)(2,1)S(1)} %get-tuple-element.63.own), channel_id=1, source_target_pairs={{0,1},{1,2},{2,3},{3,4},{4,5},{5,6},{6,7},{7,8},{8,9},{9,10},{10,1... | collective-permute-start | bytes 393224 | tf_op jit(solution)/shard_map/ppermute | solution.py:44
  31.9 8.7 %copy-start.6 = (f32[2,16,64,128]{3,2,1,0:T(8,128)S(1)}, f32[2,16,64,128]{3,2,1,0:T(8,128)}, u32[]{:S(2)}) copy-start(f32[2,16,64,128]{3,2,1,0:T(8,128)} %get-tuple-element.68.slope) | copy-start | bytes 3145732
  31.9 7.9 %collective-permute-start.5 = (bf16[512,128]{1,0:T(8,128)(2,1)S(1)}, bf16[512,128]{1,0:T(8,128)(2,1)S(1)}, u32[]{:S(2)}, u32[]{:S(2)}) collective-permute-start(bf16[512,128]{1,0:T(8,128)(2,1)S(1)} %shard_map.112.own.delta), channel_id=1, source_target_pairs={{1,0},{2,1},{3,2},{4,3},{5,4},{6,5},{7,6},{8,7},{9,8},{10,9},{11,1... | collective-permute-start | bytes 393224 | tf_op jit(solution)/shard_map/ppermute | solution.py:48
  33.9 6.7 %collective-permute-start.4 = (bf16[512,128]{1,0:T(8,128)(2,1)S(1)}, bf16[512,128]{1,0:T(8,128)(2,1)S(1)}, u32[]{:S(2)}, u32[]{:S(2)}) collective-permute-start(bf16[512,128]{1,0:T(8,128)(2,1)S(1)} %shard_map.112.own.delta), channel_id=1, source_target_pairs={{0,1},{1,2},{2,3},{3,4},{4,5},{5,6},{6,7},{7,8},{8,9},{9,10},{10,1... | collective-permute-start | bytes 393224 | tf_op jit(solution)/shard_map/ppermute | solution.py:44
  39.7 11.2 %collective-permute-start.7 = (bf16[1728,128]{1,0:T(8,128)(2,1)S(1)}, bf16[1728,128]{1,0:T(8,128)(2,1)S(1)}, u32[]{:S(2)}, u32[]{:S(2)}) collective-permute-start(bf16[1728,128]{1,0:T(8,128)(2,1)S(1)} %get-tuple-element.71), channel_id=1, source_target_pairs={{0,1},{1,0},{2,3},{3,2},{4,5},{5,4},{6,7},{7,6},{8,9},{9,8},{10,11... | collective-permute-start | bytes 1327112 | tf_op jit(solution)/shard_map/ppermute | solution.py:53
  42.1 9.7 %collective-permute-start.6 = (bf16[16,64,128]{2,1,0:T(8,128)(2,1)S(1)}, bf16[16,64,128]{2,1,0:T(8,128)(2,1)S(1)}, u32[]{:S(2)}, u32[]{:S(2)}) collective-permute-start(bf16[16,64,128]{2,1,0:T(8,128)(2,1)S(1)} %get-tuple-element.69.d1), channel_id=1, source_target_pairs={{0,1},{1,2},{2,3},{3,4},{4,5},{5,6},{6,7},{7,8},{8,9},{9,10},{10,1... | collective-permute-start | bytes 786440 | tf_op jit(solution)/shard_map/ppermute | solution.py:44
  46.5 8.0 %collective-permute-start.8 = (bf16[16,64,128]{2,1,0:T(8,128)(2,1)S(1)}, bf16[16,64,128]{2,1,0:T(8,128)(2,1)S(1)}, u32[]{:S(2)}, u32[]{:S(2)}) collective-permute-start(bf16[16,64,128]{2,1,0:T(8,128)(2,1)S(1)} %get-tuple-element.76.d0), channel_id=1, source_target_pairs={{1,0},{2,1},{3,2},{4,3},{5,4},{6,5},{7,6},{8,7},{9,8},{10,9},{11,1... | collective-permute-start | bytes 786440 | tf_op jit(solution)/shard_map/ppermute | solution.py:48
  50.9 12.4 %collective-permute-start.9 = (bf16[704,128]{1,0:T(8,128)(2,1)S(1)}, bf16[704,128]{1,0:T(8,128)(2,1)S(1)}, u32[]{:S(2)}, u32[]{:S(2)}) collective-permute-start(bf16[704,128]{1,0:T(8,128)(2,1)S(1)} %get-tuple-element.89), channel_id=1, source_target_pairs={{0,1},{1,0},{2,3},{3,2},{4,5},{5,4},{6,7},{7,6},{8,9},{9,8},{10,11... | collective-permute-start | bytes 540680 | tf_op jit(solution)/shard_map/ppermute | solution.py:53
  51.9 8.5 %collective-permute-start.10 = (bf16[864,128]{1,0:T(8,128)(2,1)S(1)}, bf16[864,128]{1,0:T(8,128)(2,1)S(1)}, u32[]{:S(2)}, u32[]{:S(2)}) collective-permute-start(bf16[864,128]{1,0:T(8,128)(2,1)S(1)} %get-tuple-element.90), channel_id=1, source_target_pairs={{0,2},{1,3},{2,0},{3,1},{4,6},{5,7},{6,4},{7,5},{8,10},{9,11},{10,... | collective-permute-start | bytes 663560 | tf_op jit(solution)/shard_map/ppermute | solution.py:53
  58.1 5.2 %collective-permute-start.11 = (bf16[448,128]{1,0:T(8,128)(2,1)S(1)}, bf16[448,128]{1,0:T(8,128)(2,1)S(1)}, u32[]{:S(2)}, u32[]{:S(2)}) collective-permute-start(bf16[448,128]{1,0:T(8,128)(2,1)S(1)} %get-tuple-element.93), channel_id=1, source_target_pairs={{0,1},{1,0},{2,3},{3,2},{4,5},{5,4},{6,7},{7,6},{8,9},{9,8},{10,11... | collective-permute-start | bytes 344072 | tf_op jit(solution)/shard_map/ppermute | solution.py:53
  60.4 7.8 %collective-permute-start.13 = (bf16[864,128]{1,0:T(8,128)(2,1)S(1)}, bf16[864,128]{1,0:T(8,128)(2,1)S(1)}, u32[]{:S(2)}, u32[]{:S(2)}) collective-permute-start(bf16[864,128]{1,0:T(8,128)(2,1)S(1)} %shard_map.118.mine), channel_id=1, source_target_pairs={{0,4},{1,5},{2,6},{3,7},{4,0},{5,1},{6,2},{7,3},{8,12},{9,13},{10,... | collective-permute-start | bytes 663560 | tf_op jit(solution)/shard_map/ppermute | solution.py:53
  63.9 4.4 %collective-permute-start.12 = (bf16[576,128]{1,0:T(8,128)(2,1)S(1)}, bf16[576,128]{1,0:T(8,128)(2,1)S(1)}, u32[]{:S(2)}, u32[]{:S(2)}) collective-permute-start(bf16[576,128]{1,0:T(8,128)(2,1)S(1)} %get-tuple-element.95), channel_id=1, source_target_pairs={{0,2},{1,3},{2,0},{3,1},{4,6},{5,7},{6,4},{7,5},{8,10},{9,11},{10,... | collective-permute-start | bytes 442376 | tf_op jit(solution)/shard_map/ppermute | solution.py:53
  68.4 9.7 %collective-permute-start.16 = (bf16[576,128]{1,0:T(8,128)(2,1)S(1)}, bf16[576,128]{1,0:T(8,128)(2,1)S(1)}, u32[]{:S(2)}, u32[]{:S(2)}) collective-permute-start(bf16[576,128]{1,0:T(8,128)(2,1)S(1)} %shard_map.121.mine), channel_id=1, source_target_pairs={{0,4},{1,5},{2,6},{3,7},{4,0},{5,1},{6,2},{7,3},{8,12},{9,13},{10,... | collective-permute-start | bytes 442376 | tf_op jit(solution)/shard_map/ppermute | solution.py:53
  69.6 9.2 %collective-permute-start.15 = (bf16[864,128]{1,0:T(8,128)(2,1)S(1)}, bf16[864,128]{1,0:T(8,128)(2,1)S(1)}, u32[]{:S(2)}, u32[]{:S(2)}) collective-permute-start(bf16[864,128]{1,0:T(8,128)(2,1)S(1)} %shard_map.120.mine), channel_id=1, source_target_pairs={{0,8},{1,9},{2,10},{3,11},{4,12},{5,13},{6,14},{7,15},{8,0},{9,1},... | collective-permute-start | bytes 663560 | tf_op jit(solution)/shard_map/ppermute | solution.py:53
  71.9 10.2 %collective-permute-start.14 = (bf16[16,64,128]{2,1,0:T(8,128)(2,1)S(1)}, bf16[16,64,128]{2,1,0:T(8,128)(2,1)S(1)}, u32[]{:S(2)}, u32[]{:S(2)}) collective-permute-start(bf16[16,64,128]{2,1,0:T(8,128)(2,1)S(1)} %get-tuple-element.98.e2), channel_id=1, source_target_pairs={{0,1},{1,2},{2,3},{3,4},{4,5},{5,6},{6,7},{7,8},{8,9},{9,10},{10,1... | collective-permute-start | bytes 786440 | tf_op jit(solution)/shard_map/ppermute | solution.py:44
  76.1 8.7 %collective-permute-start.17 = (bf16[16,64,128]{2,1,0:T(8,128)(2,1)S(1)}, bf16[16,64,128]{2,1,0:T(8,128)(2,1)S(1)}, u32[]{:S(2)}, u32[]{:S(2)}) collective-permute-start(bf16[16,64,128]{2,1,0:T(8,128)(2,1)S(1)} %get-tuple-element.103.e1), channel_id=1, source_target_pairs={{1,0},{2,1},{3,2},{4,3},{5,4},{6,5},{7,6},{8,7},{9,8},{10,9},{11,1... | collective-permute-start | bytes 786440 | tf_op jit(solution)/shard_map/ppermute | solution.py:48
  78.1 9.2 %collective-permute-start.18 = (bf16[576,128]{1,0:T(8,128)(2,1)S(1)}, bf16[576,128]{1,0:T(8,128)(2,1)S(1)}, u32[]{:S(2)}, u32[]{:S(2)}) collective-permute-start(bf16[576,128]{1,0:T(8,128)(2,1)S(1)} %shard_map.122.mine), channel_id=1, source_target_pairs={{0,8},{1,9},{2,10},{3,11},{4,12},{5,13},{6,14},{7,15},{8,0},{9,1},... | collective-permute-start | bytes 442376 | tf_op jit(solution)/shard_map/ppermute | solution.py:53
  78.8 12.3 %collective-permute-start.19 = (bf16[864,128]{1,0:T(8,128)(2,1)S(1)}, bf16[864,128]{1,0:T(8,128)(2,1)S(1)}, u32[]{:S(2)}, u32[]{:S(2)}) collective-permute-start(bf16[864,128]{1,0:T(8,128)(2,1)S(1)} %shard_map.123.refs_0_), channel_id=1, source_target_pairs={{0,2},{1,3},{2,0},{3,1},{4,6},{5,7},{6,4},{7,5},{8,10},{9,11},{10,... | collective-permute-start | bytes 663560 | tf_op jit(solution)/shard_map/ppermute | solution.py:53
  87.4 6.2 %collective-permute-start.20 = (bf16[576,128]{1,0:T(8,128)(2,1)S(1)}, bf16[576,128]{1,0:T(8,128)(2,1)S(1)}, u32[]{:S(2)}, u32[]{:S(2)}) collective-permute-start(bf16[576,128]{1,0:T(8,128)(2,1)S(1)} %shard_map.125.refs_1_), channel_id=1, source_target_pairs={{0,2},{1,3},{2,0},{3,1},{4,6},{5,7},{6,4},{7,5},{8,10},{9,11},{10,... | collective-permute-start | bytes 442376 | tf_op jit(solution)/shard_map/ppermute | solution.py:53
  94.2 5.7 %collective-permute-start.21 = (bf16[2,1440,128]{2,1,0:T(8,128)(2,1)S(1)}, bf16[2,1440,128]{2,1,0:T(8,128)(2,1)S(1)}, u32[]{:S(2)}, u32[]{:S(2)}) collective-permute-start(bf16[2,1440,128]{2,1,0:T(8,128)(2,1)S(1)} %shard_map.126.mine), channel_id=1, source_target_pairs={{0,1},{1,0},{2,3},{3,2},{4,5},{5,4},{6,7},{7,6},{8,9},{9,8},{10,11... | collective-permute-start | bytes 2211848 | tf_op jit(solution)/shard_map/ppermute | solution.py:53
